TPU v7x, 32 devices: a whole 2x2x4 slice. The times are simulated.
32 devices in a mesh: dp: 4 (over y, x), heads: 4 (over z), tensor: 2 (over core).
Axes of the slice: x: 2, y: 2, z: 4, core: 2. Of those that a mesh axis runs over, the one named last changes fastest.
Arguments:
- tokens: bfloat16 [6144, 2048], P('dp', ('heads', 'tensor')), may hold values from -6 to 6
- cotangent: bfloat16 [6144, 2048], P('dp', ('heads', 'tensor')), may hold values from -6 to 6
- lengths: int32 [12], replicated, may hold values from 1 to 1024, as said below
- dealing: int32 [12], replicated, may hold values from 0 to 11, as said below
- w_query: float32 [2048, 2048], P('dp', ('heads', 'tensor')), may hold values from -0.125 to 0.125
- w_key: float32 [2048, 2048], P('dp', ('heads', 'tensor')), may hold values from -0.125 to 0.125
- w_value: float32 [2048, 4096], P('dp', ('heads', 'tensor')), may hold values from -0.125 to 0.125
- w_swish: float32 [2048, 4096], P('dp', ('heads', 'tensor')), may hold values from -0.125 to 0.125
- w_out: float32 [4096, 2048], P(('heads', 'tensor'), 'dp'), may hold values from -0.1875 to 0.1875
- w_gate: float32 [2048, 4096], P('dp', ('heads', 'tensor')), may hold values from -0.125 to 0.125
- w_up: float32 [2048, 4096], P('dp', ('heads', 'tensor')), may hold values from -0.125 to 0.125
- w_down: float32 [4096, 2048], P(('heads', 'tensor'), 'dp'), may hold values from -0.1875 to 0.1875
- gain_attn: float32 [2048], P('dp'), may hold values from 0.25 to 1.75
- gain_mlp: float32 [2048], P('dp'), may hold values from 0.25 to 1.75
Outputs:
- mixed: bfloat16 [6144, 2048], P('dp', ('heads', 'tensor'))
- grad_tokens: bfloat16 [6144, 2048], P('dp', ('heads', 'tensor'))
- grad_query: float32 [2048, 2048], P('dp', ('heads', 'tensor'))
- grad_key: float32 [2048, 2048], P('dp', ('heads', 'tensor'))
- grad_value: float32 [2048, 4096], P('dp', ('heads', 'tensor'))
- grad_swish: float32 [2048, 4096], P('dp', ('heads', 'tensor'))
- grad_out: float32 [4096, 2048], P(('heads', 'tensor'), 'dp')
- grad_gate: float32 [2048, 4096], P('dp', ('heads', 'tensor'))
- grad_up: float32 [2048, 4096], P('dp', ('heads', 'tensor'))
- grad_down: float32 [4096, 2048], P(('heads', 'tensor'), 'dp')
- grad_gain_attn: float32 [2048], P('dp')
- grad_gain_mlp: float32 [2048], P('dp')
Inputs may be any that keep to these rules, and one draw needn't show every extreme that they name: For each g, the 3 sequences named by dealing[g * 3] to dealing[(g + 1) * 3 - 1] have lengths that sum to 1536, and exactly one of them has length 1024. `dealing`: A permutation of the sequences.
All inputs are finite; a program needn't handle non-finite values.
Results may differ from a plain program's by a relative error of at most 0.02.
The roundings to bfloat16 on the way count: a program that leaves them out, or rounds other values in their place, can miss the bound.
Values may be sent and summed in bfloat16 or wider, within the bound.
A program may use at most 256 MiB of HBM per device.

v0:
```python
import jax
import jax.numpy as jnp
from jax import lax
from jax.sharding import PartitionSpec as P

QK_DIM = 256
SEQ_DEV = 3
QBLOCK = 512


EPSILON = 1e-05
GROUP_EPS = 1.0


def layer_norm(values, epsilon):
    center = values - jnp.mean(values, -1, keepdims=True)
    scale = lax.rsqrt(jnp.mean(center * center, -1, keepdims=True) + epsilon)
    return (center * scale, scale)


def norm_back(grad, normed, scale):
    return scale * (
        grad
        - jnp.mean(grad, -1, keepdims=True)
        - normed * jnp.mean(grad * normed, -1, keepdims=True)
    )


def product(left, right):
    return jnp.dot(left, right, preferred_element_type=jnp.float32)


def inner_rows(left, right):
    return lax.dot_general(
        left, right, (((1,), (1,)), ((), ())), preferred_element_type=jnp.float32
    )


def inner_cols(left, right):
    return lax.dot_general(
        left, right, (((0,), (0,)), ((), ())), preferred_element_type=jnp.float32
    )


def lowered(value):
    return value.astype(jnp.bfloat16)


def pick_rows(targets, carry, pieces):
    count = pieces[0].shape[0]
    inside = ((targets >= 0) & (targets < count))[:, None]
    position = jnp.clip(targets, 0, count - 1)
    return tuple(
        (
            jnp.where(inside, jnp.take(piece, position, axis=0), held)
            for piece, held in zip(pieces, carry)
        )
    )


def decay_block(start, seq_ids, log_decay, block, factor):
    every = jnp.arange(seq_ids.shape[0], dtype=jnp.int32)
    near = start + jnp.arange(block, dtype=jnp.int32)
    distance = near[:, None] - every[None, :]
    own = lax.dynamic_slice_in_dim(seq_ids, start, block)
    valid = (distance >= 0) & (own[:, None] == seq_ids[None, :])
    return (
        jnp.where(valid, jnp.exp(jnp.maximum(distance, 0).astype(jnp.float32) * log_decay), 0.0)
        * factor
    )


def shards(
    tokens,
    cotangent,
    lengths,
    dealing,
    w_query,
    w_key,
    w_value,
    w_swish,
    w_out,
    w_gate,
    w_up,
    w_down,
    gain_attn,
    gain_mlp,
):
    group = lax.axis_index("dp")
    place = lax.axis_index(("heads", "tensor"))
    rows_dev = tokens.shape[0]
    slice_width = tokens.shape[1]
    seq_count = lengths.shape[0]
    ident = jnp.arange(seq_count, dtype=jnp.int32)
    starts = jnp.cumsum(lengths) - lengths
    picked = lax.dynamic_slice_in_dim(dealing, group * SEQ_DEV, SEQ_DEV)
    match = picked[:, None] == ident[None, :]
    dealt_len = jnp.sum(jnp.where(match, lengths[None, :], 0), 1)
    home_start = jnp.sum(jnp.where(match, starts[None, :], 0), 1)
    dealt_start = jnp.cumsum(dealt_len) - dealt_len
    rows = jnp.arange(rows_dev, dtype=jnp.int32)
    seq_ids = jnp.sum((rows[:, None] >= dealt_start[None, :]).astype(jnp.int32), 1) - 1
    member = seq_ids[:, None] == jnp.arange(SEQ_DEV, dtype=jnp.int32)[None, :]
    source = jnp.sum(jnp.where(member, (home_start - dealt_start)[None, :], 0), 1) + rows
    empty = jnp.zeros(tokens.shape, jnp.bfloat16)
    x_part, dy_part = pick_rows(
        source,
        (empty, empty),
        (
            lax.all_gather(tokens, "dp", axis=0, tiled=True),
            lax.all_gather(cotangent, "dp", axis=0, tiled=True),
        ),
    )
    x_full, dy_full = (
        lax.all_gather(x_part, ("heads", "tensor"), axis=1, tiled=True),
        lax.all_gather(dy_part, ("heads", "tensor"), axis=1, tiled=True),
    )
    query_w, key_w, value_w, swish_w, out_w, gate_w, up_w, down_w, gain_one, gain_two = (
        lax.all_gather(lowered(w_query), "dp", axis=0, tiled=True),
        lax.all_gather(lowered(w_key), "dp", axis=0, tiled=True),
        lax.all_gather(lowered(w_value), "dp", axis=0, tiled=True),
        lax.all_gather(lowered(w_swish), "dp", axis=0, tiled=True),
        lax.all_gather(lowered(w_out), "dp", axis=1, tiled=True),
        lax.all_gather(lowered(w_gate), "dp", axis=0, tiled=True),
        lax.all_gather(lowered(w_up), "dp", axis=0, tiled=True),
        lax.all_gather(lowered(w_down), "dp", axis=1, tiled=True),
        lax.all_gather(lowered(gain_attn), "dp", axis=0, tiled=True),
        lax.all_gather(lowered(gain_mlp), "dp", axis=0, tiled=True),
    )
    inputs = x_full.astype(jnp.float32)
    unit_one, scale_one = layer_norm(inputs, EPSILON)
    normed_in = (unit_one * gain_one.astype(jnp.float32)).astype(jnp.bfloat16)
    query = product(normed_in, query_w).astype(jnp.bfloat16)
    keys = product(normed_in, key_w).astype(jnp.bfloat16)
    values = product(normed_in, value_w).astype(jnp.bfloat16)
    swish_in = product(normed_in, swish_w)
    log_decay = jnp.log1p(-jnp.exp2(-5.0 - place.astype(jnp.float32)))
    score_factor = QK_DIM ** (-0.5)
    blocks = rows_dev // QBLOCK

    def forward_block(number):
        start = number * QBLOCK
        decay = decay_block(start, seq_ids, log_decay, QBLOCK, score_factor)
        weight = (inner_rows(lax.dynamic_slice_in_dim(query, start, QBLOCK), keys) * decay).astype(
            jnp.bfloat16
        )
        return product(weight, values)

    retained = lax.map(forward_block, jnp.arange(blocks, dtype=jnp.int32)).reshape(
        rows_dev, values.shape[1]
    )
    normed, scale_head = layer_norm(retained, GROUP_EPS)
    gate_sig = jax.nn.sigmoid(swish_in)
    swished = swish_in * gate_sig
    mixed_in = (swished * normed).astype(jnp.bfloat16)
    branch_part = product(mixed_in, out_w)
    col_start = place * slice_width
    resid = inputs + lax.psum(branch_part, ("heads", "tensor"))
    unit_two, scale_two = layer_norm(resid, EPSILON)
    normed_mid = (unit_two * gain_two.astype(jnp.float32)).astype(jnp.bfloat16)
    gate = product(normed_mid, gate_w)
    up_proj = product(normed_mid, up_w)
    activated, gelu_back = jax.vjp(jax.nn.gelu, gate)
    hidden = (activated * up_proj).astype(jnp.bfloat16)
    mlp_part = lax.psum_scatter(
        product(hidden, down_w).astype(jnp.bfloat16),
        ("heads", "tensor"),
        scatter_dimension=1,
        tiled=True,
    ).astype(jnp.float32)
    resid_share = lax.dynamic_slice_in_dim(resid, col_start, slice_width, 1)
    mixed_share = (resid_share + mlp_part).astype(jnp.bfloat16)
    query_w, key_w, value_w, swish_w, out_w, gate_w, up_w, down_w, gain_one, gain_two = (
        lax.all_gather(lowered(w_query), "dp", axis=0, tiled=True),
        lax.all_gather(lowered(w_key), "dp", axis=0, tiled=True),
        lax.all_gather(lowered(w_value), "dp", axis=0, tiled=True),
        lax.all_gather(lowered(w_swish), "dp", axis=0, tiled=True),
        lax.all_gather(lowered(w_out), "dp", axis=1, tiled=True),
        lax.all_gather(lowered(w_gate), "dp", axis=0, tiled=True),
        lax.all_gather(lowered(w_up), "dp", axis=0, tiled=True),
        lax.all_gather(lowered(w_down), "dp", axis=1, tiled=True),
        lax.all_gather(lowered(gain_attn), "dp", axis=0, tiled=True),
        lax.all_gather(lowered(gain_mlp), "dp", axis=0, tiled=True),
    )
    upstream = dy_full.astype(jnp.float32)
    delta_hidden = inner_rows(dy_full, down_w)
    grad_down = inner_cols(hidden, dy_full)
    delta_gate = gelu_back(delta_hidden * up_proj)[0].astype(jnp.bfloat16)
    delta_up = (delta_hidden * activated).astype(jnp.bfloat16)
    grad_gate = inner_cols(normed_mid, delta_gate)
    grad_up = inner_cols(normed_mid, delta_up)
    delta_mid = lax.psum(
        inner_rows(delta_gate, gate_w) + inner_rows(delta_up, up_w), ("heads", "tensor")
    )
    grad_gain_two = jnp.sum(delta_mid * unit_two, 0)
    delta_resid = upstream + norm_back(
        delta_mid * gain_two.astype(jnp.float32), unit_two, scale_two
    )
    delta_branch = delta_resid.astype(jnp.bfloat16)
    grad_out = inner_cols(mixed_in, delta_branch)
    delta_mixed = inner_rows(delta_branch, out_w)
    delta_swish = (delta_mixed * normed * gate_sig * (1.0 + swish_in * (1.0 - gate_sig))).astype(
        jnp.bfloat16
    )
    delta_normed = delta_mixed * swished
    delta_retained = norm_back(delta_normed, normed, scale_head).astype(jnp.bfloat16)

    def backward_block(carry, number):
        delta_keys, delta_values = carry
        start = number * QBLOCK
        decay = decay_block(start, seq_ids, log_decay, QBLOCK, score_factor)
        query_block = lax.dynamic_slice_in_dim(query, start, QBLOCK)
        grad_block = lax.dynamic_slice_in_dim(delta_retained, start, QBLOCK)
        weight = (inner_rows(query_block, keys) * decay).astype(jnp.bfloat16)
        delta_score = (inner_rows(grad_block, values) * decay).astype(jnp.bfloat16)
        delta_keys = delta_keys + inner_cols(delta_score, query_block)
        delta_values = delta_values + inner_cols(weight, grad_block)
        return ((delta_keys, delta_values), product(delta_score, keys))

    start_carry = (jnp.zeros(keys.shape, jnp.float32), jnp.zeros(values.shape, jnp.float32))
    (delta_keys, delta_values), delta_query = lax.scan(
        backward_block, start_carry, jnp.arange(blocks, dtype=jnp.int32)
    )
    delta_query = delta_query.reshape(rows_dev, query.shape[1]).astype(jnp.bfloat16)
    delta_keys = delta_keys.astype(jnp.bfloat16)
    delta_values = delta_values.astype(jnp.bfloat16)
    grad_query = inner_cols(normed_in, delta_query)
    grad_key = inner_cols(normed_in, delta_keys)
    grad_value = inner_cols(normed_in, delta_values)
    grad_swish = inner_cols(normed_in, delta_swish)
    delta_part = (
        inner_rows(delta_query, query_w)
        + inner_rows(delta_keys, key_w)
        + inner_rows(delta_values, value_w)
        + inner_rows(delta_swish, swish_w)
    )
    delta_in = lax.psum(delta_part.astype(jnp.bfloat16), ("heads", "tensor")).astype(jnp.float32)
    grad_gain_one = jnp.sum(delta_in * unit_one, 0)
    delta_tokens = delta_resid + norm_back(
        delta_in * gain_one.astype(jnp.float32), unit_one, scale_one
    )
    grad_share = lax.dynamic_slice_in_dim(delta_tokens, col_start, slice_width, 1).astype(
        jnp.bfloat16
    )
    grads = (
        lax.psum_scatter(
            grad_query.astype(jnp.bfloat16), "dp", scatter_dimension=0, tiled=True
        ).astype(jnp.float32),
        lax.psum_scatter(
            grad_key.astype(jnp.bfloat16), "dp", scatter_dimension=0, tiled=True
        ).astype(jnp.float32),
        lax.psum_scatter(
            grad_value.astype(jnp.bfloat16), "dp", scatter_dimension=0, tiled=True
        ).astype(jnp.float32),
        lax.psum_scatter(
            grad_swish.astype(jnp.bfloat16), "dp", scatter_dimension=0, tiled=True
        ).astype(jnp.float32),
        lax.psum_scatter(
            grad_out.astype(jnp.bfloat16), "dp", scatter_dimension=1, tiled=True
        ).astype(jnp.float32),
        lax.psum_scatter(
            grad_gate.astype(jnp.bfloat16), "dp", scatter_dimension=0, tiled=True
        ).astype(jnp.float32),
        lax.psum_scatter(
            grad_up.astype(jnp.bfloat16), "dp", scatter_dimension=0, tiled=True
        ).astype(jnp.float32),
        lax.psum_scatter(
            grad_down.astype(jnp.bfloat16), "dp", scatter_dimension=1, tiled=True
        ).astype(jnp.float32),
        lax.psum_scatter(
            grad_gain_one.astype(jnp.bfloat16), "dp", scatter_dimension=0, tiled=True
        ).astype(jnp.float32),
        lax.psum_scatter(
            grad_gain_two.astype(jnp.bfloat16), "dp", scatter_dimension=0, tiled=True
        ).astype(jnp.float32),
    )
    slot_match = dealing[:, None] == ident[None, :]
    slot_len = jnp.sum(jnp.where(slot_match, lengths[None, :], 0), 1)
    slot_home = jnp.sum(jnp.where(slot_match, starts[None, :], 0), 1)
    per_group = slot_len.reshape(-1, SEQ_DEV)
    slot_start = (jnp.cumsum(per_group, 1) - per_group).reshape(-1)
    slot_base = ident // SEQ_DEV * rows_dev + slot_start - slot_home
    owner_base = jnp.sum(jnp.where(dealing[None, :] == ident[:, None], slot_base[None, :], 0), 1)
    global_rows = group * rows_dev + rows
    seq_of = jnp.sum((global_rows[:, None] >= starts[None, :]).astype(jnp.int32), 1) - 1
    targets = (
        jnp.sum(jnp.where(seq_of[:, None] == ident[None, :], owner_base[None, :], 0), 1)
        + global_rows
    )
    mixed_rows, grad_rows = pick_rows(
        targets,
        (empty, empty),
        (
            lax.all_gather(mixed_share, "dp", axis=0, tiled=True),
            lax.all_gather(grad_share, "dp", axis=0, tiled=True),
        ),
    )
    return (
        mixed_rows,
        grad_rows,
        grads[0],
        grads[1],
        grads[2],
        grads[3],
        grads[4],
        grads[5],
        grads[6],
        grads[7],
        grads[8],
        grads[9],
    )


def solution(mesh):
    in_specs = (
        P("dp", ("heads", "tensor")),
        P("dp", ("heads", "tensor")),
        P(),
        P(),
        P("dp", ("heads", "tensor")),
        P("dp", ("heads", "tensor")),
        P("dp", ("heads", "tensor")),
        P("dp", ("heads", "tensor")),
        P(("heads", "tensor"), "dp"),
        P("dp", ("heads", "tensor")),
        P("dp", ("heads", "tensor")),
        P(("heads", "tensor"), "dp"),
        P("dp"),
        P("dp"),
    )
    out_specs = (
        P("dp", ("heads", "tensor")),
        P("dp", ("heads", "tensor")),
        P("dp", ("heads", "tensor")),
        P("dp", ("heads", "tensor")),
        P("dp", ("heads", "tensor")),
        P("dp", ("heads", "tensor")),
        P(("heads", "tensor"), "dp"),
        P("dp", ("heads", "tensor")),
        P("dp", ("heads", "tensor")),
        P(("heads", "tensor"), "dp"),
        P("dp"),
        P("dp"),
    )
    return jax.shard_map(shards, mesh=mesh, in_specs=in_specs, out_specs=out_specs, check_vma=False)
```

profile of v0, /device:TPU:0, one launch (start us, length us, event | category | flops | bytes accessed | tf_op | source)
XLA Modules:
  0.0 1795.8 jit_solution(6043142709427130776)
XLA Ops:
  12.8 43.8 %all-gather.39.cloned.1.call-done = bf16[6144,256]{1,0:T(8,128)(2,1)} async-done(((bf16[1536,256]{1,0:T(8,128)(2,1)}), bf16[6144,256]{1,0:T(8,128)(2,1)}) %all-gather.39.cloned.1.call-update) | async-done | bytes 3145744 | tf_op jit(solution)/shard_map/all_gather | solution.py:111
  62.5 39.9 %all-gather.17.cloned.1.call-done = bf16[6144,256]{1,0:T(8,128)(2,1)} async-done(((bf16[1536,256]{1,0:T(8,128)(2,1)}), bf16[6144,256]{1,0:T(8,128)(2,1)}) %all-gather.17.cloned.1.call-update) | async-done | bytes 3145744 | tf_op jit(solution)/shard_map/all_gather | solution.py:110
  117.3 8.0 all-gather
  125.4 50.4 %all-gather.19.cloned.1.call-done = bf16[1536,2048]{1,0:T(8,128)(2,1)} async-done(((bf16[1536,256]{1,0:T(8,128)(2,1)}), bf16[1536,2048]{1,0:T(8,128)(2,1)}) %all-gather.19.cloned.1.call-update) | async-done | bytes 6291472 | tf_op jit(solution)/shard_map/all_gather | solution.py:115
  186.7 16.2 all-gather.25.cloned.1.call-done
  208.6 23.2 %all-gather.23.cloned.1.call-done = bf16[2048,256]{1,0:T(8,128)(2,1)} async-done(((bf16[512,256]{1,0:T(8,128)(2,1)}), bf16[2048,256]{1,0:T(8,128)(2,1)}) %all-gather.23.cloned.1.call-update) | async-done | bytes 1048592 | tf_op jit(solution)/shard_map/all_gather | solution.py:119
  237.5 31.9 %all-gather.27.cloned.1.call-done = bf16[2048,512]{1,0:T(8,128)(2,1)} async-done(((bf16[512,512]{1,0:T(8,128)(2,1)}), bf16[2048,512]{1,0:T(8,128)(2,1)}) %all-gather.27.cloned.1.call-update) | async-done | bytes 2097168 | tf_op jit(solution)/shard_map/all_gather | solution.py:121
  269.4 8.0 convolution_convert_fusion.6
  277.4 16.1 while.25
  297.2 10.0 all-gather.21.cloned.1.call-done
  307.2 10.0 multiply_convert_fusion.6
  317.2 27.6 %all-gather.29.cloned.1.call-done = bf16[512,2048]{1,0:T(8,128)(2,1)} async-done(((bf16[512,512]{1,0:T(8,128)(2,1)}), bf16[512,2048]{1,0:T(8,128)(2,1)}) %all-gather.29.cloned.1.call-update) | async-done | bytes 2097168 | tf_op jit(solution)/shard_map/all_gather | solution.py:123
  344.8 7.9 fusion.62
  357.5 8.0 all-gather.1
  365.5 241.9 %all-reduce.7.cloned.1.call-done = f32[1536,2048]{1,0:T(8,128)} async-done(((f32[1536,2048]{1,0:T(8,128)}), f32[1536,2048]{1,0:T(8,128)}) %all-reduce.7.cloned.1.call-update) | async-done | bytes 12582928 | tf_op jit(solution)/shard_map/psum | solution.py:158
  623.5 21.7 %all-gather.33.cloned.1.call-done = bf16[2048,512]{1,0:T(8,128)(2,1)} async-done(((bf16[512,512]{1,0:T(8,128)(2,1)}), bf16[2048,512]{1,0:T(8,128)(2,1)}) %all-gather.33.cloned.1.call-update) | async-done | bytes 2097168 | tf_op jit(solution)/shard_map/all_gather | solution.py:125
  645.2 8.5 fusion.64
  653.7 29.3 %all-gather.31.cloned.1.call-done = bf16[2048,512]{1,0:T(8,128)(2,1)} async-done(((bf16[512,512]{1,0:T(8,128)(2,1)}), bf16[2048,512]{1,0:T(8,128)(2,1)}) %all-gather.31.cloned.1.call-update) | async-done | bytes 2097168 | tf_op jit(solution)/shard_map/all_gather | solution.py:124
  683.0 8.6 fusion.63
  691.6 28.8 %all-gather.35.cloned.1.call-done = bf16[512,2048]{1,0:T(8,128)(2,1)} async-done(((bf16[512,512]{1,0:T(8,128)(2,1)}), bf16[512,2048]{1,0:T(8,128)(2,1)}) %all-gather.35.cloned.1.call-update) | async-done | bytes 2097168 | tf_op jit(solution)/shard_map/all_gather | solution.py:126
  720.5 67.4 %all-gather.41.cloned.1.call-done = bf16[1536,2048]{1,0:T(8,128)(2,1)} async-done(((bf16[1536,256]{1,0:T(8,128)(2,1)}), bf16[1536,2048]{1,0:T(8,128)(2,1)}) %all-gather.41.cloned.1.call-update) | async-done | bytes 6291472 | tf_op jit(solution)/shard_map/all_gather | solution.py:116
  787.8 11.9 multiply_convert_fusion.4
  812.6 252.9 %all-reduce.9.cloned.1.call-done = f32[1536,2048]{1,0:T(8,128)} async-done(((f32[1536,2048]{1,0:T(8,128)}), f32[1536,2048]{1,0:T(8,128)}) %all-reduce.9.cloned.1.call-update) | async-done | bytes 12582928 | tf_op jit(solution)/shard_map/psum | solution.py:192
  1065.5 10.9 multiply_reduce_fusion
  1077.3 14.4 multiply_add_fusion
  1091.7 10.9 fusion.58
  1104.6 44.9 %while.26 = (s32[]{:T(128)}, f32[1536,256]{1,0:T(8,128)S(1)}, f32[1536,512]{1,0:T(8,128)}, bf16[3,512,256]{2,1,0:T(8,128)(2,1)}, s32[3]{0:T(128)S(1)}, /*index=5...) while((s32[]{:T(128)}, f32[1536,256]{1,0:T(8,128)S(1)}, ...), condition=%wide.region_28.30_spmd.clone, body=%wide.region_27.29_spmd.clone.sunk | while | flops 2838233600 | bytes 22573832 | solution.py:221
  1149.5 10.8 fusion.50
  1174.3 14.9 add_convert_fusion
  1189.3 8.2 convolution_convert_fusion
  1205.4 8.2 convolution_convert_fusion.3
  1233.2 10.1 fusion.43
  1243.3 7.7 convolution_convert_fusion.5
  1251.4 8.2 convolution_convert_fusion.4
  1259.7 65.9 %all-reduce.11.cloned.1.call-done = bf16[1536,2048]{1,0:T(8,128)(2,1)} async-done(((bf16[1536,2048]{1,0:T(8,128)(2,1)}), bf16[1536,2048]{1,0:T(8,128)(2,1)}) %all-reduce.11.cloned.1.call-update) | async-done | bytes 6291472 | tf_op jit(solution)/shard_map/psum | solution.py:237
  1325.6 9.5 fusion.29
  1338.2 59.5 %reduce-scatter.10.cloned.1.call-done = bf16[1536,256]{1,0:T(8,128)(2,1)} async-done(((bf16[1536,2048]{1,0:T(8,128)(2,1)}), bf16[1536,256]{1,0:T(8,128)(2,1)}) %reduce-scatter.10.cloned.1.call-update) | async-done | bytes 786448 | tf_op jit(solution)/shard_map/reduce_scatter | solution.py:165
  1402.7 31.5 %reduce-scatter.24.cloned.1.call-done = bf16[512,512]{1,0:T(8,128)(2,1)} async-done(((bf16[2048,512]{1,0:T(8,128)(2,1)}), bf16[512,512]{1,0:T(8,128)(2,1)}) %reduce-scatter.24.cloned.1.call-update) | async-done | bytes 524304 | tf_op jit(solution)/shard_map/reduce_scatter | solution.py:264
  1436.3 36.2 %reduce-scatter.22.cloned.1.call-done = bf16[512,512]{1,0:T(8,128)(2,1)} async-done(((bf16[2048,512]{1,0:T(8,128)(2,1)}), bf16[512,512]{1,0:T(8,128)(2,1)}) %reduce-scatter.22.cloned.1.call-update) | async-done | bytes 524304 | tf_op jit(solution)/shard_map/reduce_scatter | solution.py:261
  1474.6 36.0 %reduce-scatter.26.cloned.1.call-done = bf16[512,512]{1,0:T(8,128)(2,1)} async-done(((bf16[512,2048]{1,0:T(8,128)(2,1)}), bf16[512,512]{1,0:T(8,128)(2,1)}) %reduce-scatter.26.cloned.1.call-update) | async-done | bytes 524304 | tf_op jit(solution)/shard_map/reduce_scatter | solution.py:267
  1512.8 29.2 %reduce-scatter.12.cloned.1.call-done = bf16[512,256]{1,0:T(8,128)(2,1)} async-done(((bf16[2048,256]{1,0:T(8,128)(2,1)}), bf16[512,256]{1,0:T(8,128)(2,1)}) %reduce-scatter.12.cloned.1.call-update) | async-done | bytes 262160 | tf_op jit(solution)/shard_map/reduce_scatter | solution.py:246
  1543.7 29.5 %reduce-scatter.14.cloned.1.call-done = bf16[512,256]{1,0:T(8,128)(2,1)} async-done(((bf16[2048,256]{1,0:T(8,128)(2,1)}), bf16[512,256]{1,0:T(8,128)(2,1)}) %reduce-scatter.14.cloned.1.call-update) | async-done | bytes 262160 | tf_op jit(solution)/shard_map/reduce_scatter | solution.py:249
  1575.0 9.1 all-reduce.2
  1585.3 26.3 %reduce-scatter.20.cloned.1.call-done = bf16[512,512]{1,0:T(8,128)(2,1)} async-done(((bf16[512,2048]{1,0:T(8,128)(2,1)}), bf16[512,512]{1,0:T(8,128)(2,1)}) %reduce-scatter.20.cloned.1.call-update) | async-done | bytes 524304 | tf_op jit(solution)/shard_map/reduce_scatter | solution.py:258
  1613.8 36.1 %reduce-scatter.16.cloned.1.call-done = bf16[512,512]{1,0:T(8,128)(2,1)} async-done(((bf16[2048,512]{1,0:T(8,128)(2,1)}), bf16[512,512]{1,0:T(8,128)(2,1)}) %reduce-scatter.16.cloned.1.call-update) | async-done | bytes 524304 | tf_op jit(solution)/shard_map/reduce_scatter | solution.py:252
  1652.0 36.2 %reduce-scatter.18.cloned.1.call-done = bf16[512,512]{1,0:T(8,128)(2,1)} async-done(((bf16[2048,512]{1,0:T(8,128)(2,1)}), bf16[512,512]{1,0:T(8,128)(2,1)}) %reduce-scatter.18.cloned.1.call-update) | async-done | bytes 524304 | tf_op jit(solution)/shard_map/reduce_scatter | solution.py:255
  1690.3 44.3 %all-gather.43.cloned.1.call-done = bf16[6144,256]{1,0:T(8,128)(2,1)} async-done(((bf16[1536,256]{1,0:T(8,128)(2,1)}), bf16[6144,256]{1,0:T(8,128)(2,1)}) %all-gather.43.cloned.1.call-update) | async-done | bytes 3145744 | tf_op jit(solution)/shard_map/all_gather | solution.py:295
  1740.5 40.3 %all-gather.37.cloned.1.call-done = bf16[6144,256]{1,0:T(8,128)(2,1)} async-done(((bf16[1536,256]{1,0:T(8,128)(2,1)}), bf16[6144,256]{1,0:T(8,128)(2,1)}) %all-gather.37.cloned.1.call-update) | async-done | bytes 3145744 | tf_op jit(solution)/shard_map/all_gather | solution.py:294
  (253 shorter events, 225.9 us)
Async XLA Ops:
  7.2 49.4 %all-gather.39.cloned.1.call-start = ((), (), s32[]{:S(2)}) async-start(), calls=%async_computation.22 | async-start | bytes 3932160 | tf_op jit(solution)/shard_map/all_gather | solution.py:111
  7.9 94.5 %all-gather.17.cloned.1.call-start = ((), (), s32[]{:S(2)}) async-start(), calls=%async_computation.9 | async-start | bytes 3932160 | tf_op jit(solution)/shard_map/all_gather | solution.py:110
  8.7 167.1 %all-gather.19.cloned.1.call-start = ((), (), s32[]{:S(2)}) async-start(), calls=%async_computation.10 | async-start | bytes 7077888 | tf_op jit(solution)/shard_map/all_gather | solution.py:115
  108.4 4.8 copy-start.6
  110.4 92.5 %all-gather.25.cloned.1.call-start = ((), (), s32[]{:S(2)}) async-start(), calls=%async_computation.13 | async-start | bytes 1310720 | tf_op jit(solution)/shard_map/all_gather | solution.py:120
  111.2 120.6 %all-gather.23.cloned.1.call-start = ((), (), s32[]{:S(2)}) async-start(), calls=%async_computation.12 | async-start | bytes 1310720 | tf_op jit(solution)/shard_map/all_gather | solution.py:119
  113.1 156.3 %all-gather.27.cloned.1.call-start = ((), (), s32[]{:S(2)}) async-start(), calls=%async_computation.14 | async-start | bytes 2621440 | tf_op jit(solution)/shard_map/all_gather | solution.py:121
  114.0 193.1 %all-gather.21.cloned.1.call-start = ((), (), s32[]{:S(2)}) async-start(), calls=%async_computation.11 | async-start | bytes 2621440 | tf_op jit(solution)/shard_map/all_gather | solution.py:122
  115.0 229.8 %all-gather.29.cloned.1.call-start = ((), (), s32[]{:S(2)}) async-start(), calls=%async_computation.15 | async-start | bytes 2621440 | tf_op jit(solution)/shard_map/all_gather | solution.py:123
  117.1 490.3 %all-reduce.7.cloned.1.call-start = ((), (), s32[]{:S(2)}) async-start(), calls=%async_computation.16 | async-start | bytes 25165824 | tf_op jit(solution)/shard_map/psum | solution.py:158
  125.4 56.8 %copy-start.16 = (f32[4,1,512]{2,1,0:T(1,128)}, f32[4,1,512]{2,1,0:T(1,128)S(1)}, u32[]{:S(2)}) copy-start(f32[4,1,512]{2,1,0:T(1,128)S(1)} %convert_element_type.263) | copy-start | bytes 24580
  317.2 35.5 %copy-start.30 = (bf16[1536,512]{0,1:T(8,128)(2,1)}, bf16[1536,512]{0,1:T(8,128)(2,1)S(1)}, u32[]{:S(2)}) copy-start(bf16[1536,512]{0,1:T(8,128)(2,1)S(1)} %get-tuple-element.270) | copy-start | bytes 4718596
  352.7 292.5 %all-gather.33.cloned.1.call-start = ((), (), s32[]{:S(2)}) async-start(), calls=%async_computation.18 | async-start | bytes 2621440 | tf_op jit(solution)/shard_map/all_gather | solution.py:125
  354.8 328.2 %all-gather.31.cloned.1.call-start = ((), (), s32[]{:S(2)}) async-start(), calls=%async_computation.17 | async-start | bytes 2621440 | tf_op jit(solution)/shard_map/all_gather | solution.py:124
  355.7 364.7 %all-gather.35.cloned.1.call-start = ((), (), s32[]{:S(2)}) async-start(), calls=%async_computation.19 | async-start | bytes 2621440 | tf_op jit(solution)/shard_map/all_gather | solution.py:126
  356.7 431.2 %all-gather.41.cloned.1.call-start = ((), (), s32[]{:S(2)}) async-start(), calls=%async_computation.23 | async-start | bytes 7077888 | tf_op jit(solution)/shard_map/all_gather | solution.py:116
  357.4 708.1 %all-reduce.9.cloned.1.call-start = ((), (), s32[]{:S(2)}) async-start(), calls=%async_computation.24 | async-start | bytes 25165824 | tf_op jit(solution)/shard_map/psum | solution.py:192
  614.6 4.7 copy-start
  799.7 6.0 copy-start.32
  799.7 6.0 copy-start.4
  812.5 513.1 %all-reduce.11.cloned.1.call-start = ((), (), s32[]{:S(2)}) async-start(), calls=%async_computation.25 | async-start | bytes 12582912 | tf_op jit(solution)/shard_map/psum | solution.py:237
  1065.5 11.8 copy-start.2
  1077.3 14.4 copy-start.3
  1077.3 14.4 copy-start.26
  1149.5 10.8 copy-start.25
  1149.5 10.8 copy-start.31
  1160.3 6.6 copy-start.5
  1189.2 208.5 %reduce-scatter.10.cloned.1.call-start = ((), (), s32[]{:S(2)}) async-start(), calls=%async_computation.20 | async-start | bytes 7077888 | tf_op jit(solution)/shard_map/reduce_scatter | solution.py:165
  1197.6 236.6 %reduce-scatter.24.cloned.1.call-start = ((), (), s32[]{:S(2)}) async-start(), calls=%async_computation.33 | async-start | bytes 2621440 | tf_op jit(solution)/shard_map/reduce_scatter | solution.py:264
  1205.3 8.3 copy-start.33
  1205.3 267.1 %reduce-scatter.22.cloned.1.call-start = ((), (), s32[]{:S(2)}) async-start(), calls=%async_computation.32 | async-start | bytes 2621440 | tf_op jit(solution)/shard_map/reduce_scatter | solution.py:261
  1213.6 297.0 %reduce-scatter.26.cloned.1.call-start = ((), (), s32[]{:S(2)}) async-start(), calls=%async_computation.34 | async-start | bytes 2621440 | tf_op jit(solution)/shard_map/reduce_scatter | solution.py:267
  1221.3 320.6 %reduce-scatter.12.cloned.1.call-start = ((), (), s32[]{:S(2)}) async-start(), calls=%async_computation.27 | async-start | bytes 1310720 | tf_op jit(solution)/shard_map/reduce_scatter | solution.py:246
  1227.3 345.9 %reduce-scatter.14.cloned.1.call-start = ((), (), s32[]{:S(2)}) async-start(), calls=%async_computation.28 | async-start | bytes 1310720 | tf_op jit(solution)/shard_map/reduce_scatter | solution.py:249
  1233.1 10.2 copy-start.27
  1233.1 378.5 %reduce-scatter.20.cloned.1.call-start = ((), (), s32[]{:S(2)}) async-start(), calls=%async_computation.31 | async-start | bytes 2621440 | tf_op jit(solution)/shard_map/reduce_scatter | solution.py:258
  1243.3 406.6 %reduce-scatter.16.cloned.1.call-start = ((), (), s32[]{:S(2)}) async-start(), calls=%async_computation.29 | async-start | bytes 2621440 | tf_op jit(solution)/shard_map/reduce_scatter | solution.py:252
  1251.1 74.5 %copy-start.13 = (f32[1536]{0:T(1024)S(1)}, f32[1536]{0:T(1024)}, u32[]{:S(2)}) copy-start(f32[1536]{0:T(1024)} %copy-done.12) | copy-start | bytes 18436
  1251.1 74.5 %copy-start.15 = (f32[1536]{0:T(1024)S(1)}, f32[1536]{0:T(1024)}, u32[]{:S(2)}) copy-start(f32[1536]{0:T(1024)} %copy-done.14) | copy-start | bytes 18436
  1251.1 74.5 %copy-start.17 = (f32[4,1,512]{2,1,0:T(1,128)S(1)}, f32[4,1,512]{2,1,0:T(1,128)}, u32[]{:S(2)}) copy-start(f32[4,1,512]{2,1,0:T(1,128)} %copy-done.16) | copy-start | bytes 24580
  1251.1 437.0 %reduce-scatter.18.cloned.1.call-start = ((), (), s32[]{:S(2)}) async-start(), calls=%async_computation.30 | async-start | bytes 2621440 | tf_op jit(solution)/shard_map/reduce_scatter | solution.py:255
  1259.6 474.9 %all-gather.43.cloned.1.call-start = ((), (), s32[]{:S(2)}) async-start(), calls=%async_computation.26 | async-start | bytes 3932160 | tf_op jit(solution)/shard_map/all_gather | solution.py:295
  1338.2 62.3 %copy-start.20 = (s32[12]{0:T(128)S(1)}, s32[12]{0:T(128)}, u32[]{:S(2)}) copy-start(s32[12]{0:T(128)} %copy-done.19) | copy-start | bytes 148
  1338.2 62.3 %copy-start.21 = (s32[12]{0:T(128)S(1)}, s32[12]{0:T(128)}, u32[]{:S(2)}) copy-start(s32[12]{0:T(128)} %param.22) | copy-start | bytes 148
  1338.2 62.3 %copy-start.24 = (s32[12]{0:T(128)S(1)}, s32[12]{0:T(128)}, u32[]{:S(2)}) copy-start(s32[12]{0:T(128)} %param.23) | copy-start | bytes 148
  1338.2 62.8 %copy-start.29 = (u32[32]{0:T(128)S(1)}, u32[32]{0:T(128)}, u32[]{:S(2)}) copy-start(u32[32]{0:T(128)} %constant.142) | copy-start | bytes 388
  1338.2 442.6 %all-gather.37.cloned.1.call-start = ((), (), s32[]{:S(2)}) async-start(), calls=%async_computation.21 | async-start | bytes 3932160 | tf_op jit(solution)/shard_map/all_gather | solution.py:294
  1402.6 172.3 %copy-start.18 = (bf16[2048]{0:T(1024)(128)(2,1)S(1)}, bf16[2048]{0:T(1024)(128)(2,1)}, u32[]{:S(2)}) copy-start(bf16[2048]{0:T(1024)(128)(2,1)} %get-tuple-element.198) | copy-start | bytes 12292
  (14 other events, 42.8 us)
Sparse Core Ops, SparseCore 0:
  9.8 46.6 all-gather.38
  58.4 43.9 all-gather.16
  110.5 65.1 all-gather.18
  178.0 24.8 all-gather.24
  205.1 26.6 all-gather.22
  234.1 35.2 all-gather.26
  271.8 35.2 all-gather.20
  309.6 35.1 all-gather.28
  352.8 254.5 all-reduce.6
  609.7 35.4 all-gather.32
  647.7 35.2 all-gather.30
  685.3 35.1 all-gather.34
  722.6 65.1 all-gather.40
  812.7 252.7 all-reduce.8
  1189.4 136.2 all-reduce.10
  1327.8 69.8 reduce-scatter.9
  1400.5 33.5 reduce-scatter.23
  1437.2 35.1 reduce-scatter.21
  1475.4 35.1 reduce-scatter.25
  1514.2 27.7 reduce-scatter.11
  1545.4 27.7 reduce-scatter.13
  1576.4 35.1 reduce-scatter.19
  1614.6 35.1 reduce-scatter.15
  1652.9 35.1 reduce-scatter.17
  1690.5 43.9 all-gather.42
  1736.8 43.9 all-gather.36
where the time goes:
time: 1800 us
  waiting for transfers between devices  1360 us (76%)
  matrix products  252 us (14%)
  other arithmetic  100 us (6%)
  local copies, waits for them, and re-layouts  38.8 us (2%)
  blocking collectives  25.1 us (1%)
    psum x1, waiting for transfers between devices, shards(): lax.psum(inner_rows(delta_gate, gate_w) + inner_rows(delta_up, up_w), ('h...  253 us
    psum x1, waiting for transfers between devices, shards(): resid = inputs + lax.psum(branch_part, ('heads', 'tensor'))  242 us
    dot_general x11, matrix products, inner_rows(): lax.dot_general(left, right, (((1,), (1,)), ((), ())), preferred_element_...  87.3 us
    dot_general x14, matrix products, inner_cols(): lax.dot_general(left, right, (((0,), (0,)), ((), ())), preferred_element_...  85.7 us
    dot_general x14, matrix products, product(): return jnp.dot(left, right, preferred_element_type=jnp.float32)  78.6 us
    all_gather x1, waiting for transfers between devices, shards(): lax.all_gather(dy_part, ('heads', 'tensor'), axis=1, tiled=True)  67.4 us
    psum x1, waiting for transfers between devices, shards(): lax.psum(delta_part.astype(jnp.bfloat16), ('heads', 'tensor'))  65.9 us
    reduce_scatter x1, waiting for transfers between devices, shards(): lax.psum_scatter(product(hidden, down_w).astype(jnp.bfloat16), ('heads',...  59.5 us
  transfers between devices with their start and end apart: 26, of which 26 were waited for; matrix products, arithmetic and copies ran while one was open for 12% of the time, Pallas kernels for 0%

commit v1 on v0

v1 whole, which is shorter than its diff:
```python
import functools

import jax
import jax.numpy as jnp
from jax import lax
from jax.experimental import pallas as pl
from jax.experimental.pallas import tpu as pltpu
from jax.sharding import PartitionSpec as P

QK_DIM = 256
SEQ_DEV = 3
QBLOCK = 512
PIECE = 32
AXES = ("dp", "heads", "tensor")
TP = ("heads", "tensor")
SWAP_AXES = (0, 0, 0, 0, 1)
MESH = pl.DeviceIdType.MESH


EPSILON = 1e-05
GROUP_EPS = 1.0


def layer_norm(values, epsilon):
    center = values - jnp.mean(values, -1, keepdims=True)
    scale = lax.rsqrt(jnp.mean(center * center, -1, keepdims=True) + epsilon)
    return (center * scale, scale)


def norm_back(grad, normed, scale):
    return scale * (
        grad
        - jnp.mean(grad, -1, keepdims=True)
        - normed * jnp.mean(grad * normed, -1, keepdims=True)
    )


def product(left, right):
    return jnp.dot(left, right, preferred_element_type=jnp.float32)


def inner_rows(left, right):
    return lax.dot_general(
        left, right, (((1,), (1,)), ((), ())), preferred_element_type=jnp.float32
    )


def inner_cols(left, right):
    return lax.dot_general(
        left, right, (((0,), (0,)), ((), ())), preferred_element_type=jnp.float32
    )


def lowered(value):
    return value.astype(jnp.bfloat16)


def around(axes):
    return tuple(lax.axis_index(name) for name in axes)


def wide(value):
    return value.astype(jnp.float32)


def within(number, count):
    return (number >= 0) & (number < count)


def greet(others):
    barrier = pltpu.get_barrier_semaphore()
    for other in others:
        pl.semaphore_signal(barrier, inc=1, device_id=other, device_id_type=MESH)
    pl.semaphore_wait(barrier, len(others))


def plane_peers(at, sizes):
    group, level, core = at
    return [(lax.rem(group + k, sizes[0]), level, core) for k in range(1, sizes[0])]


def column_peers(at, sizes):
    group, level, core = at
    return [(group, lax.rem(level + k, sizes[1]), core) for k in range(1, sizes[1])] + [
        (group, level, 1 - core)
    ]


class Spread:
    def __init__(self, at, sizes, items, sems):
        self.at, self.count, self.items = at, sizes[0], items
        self.local, self.sent, self.got = sems

    @staticmethod
    def scratch(items, sizes):
        return [
            pltpu.SemaphoreType.DMA((items,)),
            pltpu.SemaphoreType.DMA((items, sizes[0] - 1)),
            pltpu.SemaphoreType.DMA((items, sizes[0] - 1)),
        ]

    def place(self, number, owner):
        source, target, axis = self.items[number]
        size = source.shape[axis]
        span = pl.ds(pl.multiple_of(owner * size, size), size)
        return target.at[span] if axis == 0 else target.at[:, span]

    def own(self, number):
        return pltpu.make_async_copy(
            self.items[number][0], self.place(number, self.at[0]), self.local.at[number]
        )

    def away(self, number, k):
        return pltpu.make_async_remote_copy(
            src_ref=self.items[number][0],
            dst_ref=self.place(number, self.at[0]),
            send_sem=self.sent.at[number, k - 1],
            recv_sem=self.got.at[number, k - 1],
            device_id=(lax.rem(self.at[0] + k, self.count),) + self.at[1:],
            device_id_type=MESH,
        )

    def landed(self, number, k):
        owner = lax.rem(self.at[0] + self.count - k, self.count)
        return pltpu.make_async_remote_copy(
            src_ref=self.items[number][0],
            dst_ref=self.place(number, owner),
            send_sem=self.sent.at[number, k - 1],
            recv_sem=self.got.at[number, k - 1],
            device_id=(owner,) + self.at[1:],
            device_id_type=MESH,
        )

    def start(self, number):
        self.own(number).start()
        for k in range(1, self.count):
            self.away(number, k).start()

    def wait(self, number):
        self.own(number).wait()
        for k in range(1, self.count):
            self.landed(number, k).wait_recv()

    def drain(self, number):
        for k in range(1, self.count):
            self.away(number, k).wait_send()


class Gather:
    def __init__(self, at, sizes, count, full, sems):
        self.at, self.levels, self.count, self.full = at, sizes[1], count, full
        self.sent_up, self.got_up, self.sent_down, self.got_down, self.sent_core, self.got_core = sems

    @staticmethod
    def scratch(count, sizes, piece):
        levels = sizes[1]
        dma = pltpu.SemaphoreType.DMA
        return [pltpu.VMEM((count, levels, 2) + piece, jnp.bfloat16)] + [
            dma((levels - 1, count)) for _ in range(4)
        ] + [dma((2 * levels - 1, count)) for _ in range(2)]

    def copy(self, ref, sent, got, target):
        return pltpu.make_async_remote_copy(
            src_ref=ref, dst_ref=ref, send_sem=sent, recv_sem=got, device_id=target, device_id_type=MESH
        )

    def up(self, k, hop, origin, sem):
        group, level, core = self.at
        target = (group, lax.rem(level + 1, self.levels), core)
        return self.copy(self.full.at[k, origin, core], self.sent_up.at[sem, k], self.got_up.at[sem, k], target)

    def down(self, k, hop, origin, sem):
        group, level, core = self.at
        target = (group, lax.rem(level + self.levels - 1, self.levels), core)
        return self.copy(
            self.full.at[k, origin, core], self.sent_down.at[sem, k], self.got_down.at[sem, k], target
        )

    def across(self, k, origin, side, sem):
        group, level, core = self.at
        return self.copy(
            self.full.at[k, origin, side], self.sent_core.at[sem, k], self.got_core.at[sem, k], (group, level, 1 - core)
        )

    def start(self, k):
        group, level, core = self.at

        @pl.when(level < self.levels - 1)
        def _():
            self.up(k, 0, level, 0).start()

        @pl.when(level > 0)
        def _():
            self.down(k, 0, level, 0).start()

        self.across(k, level, core, 0).start()

    def hop(self, k, hop):
        group, level, core = self.at
        last = self.levels - 1

        @pl.when(level >= hop)
        def _():
            origin = level - hop
            self.up(k, hop, origin, hop - 1).wait_recv()
            if hop < last:

                @pl.when(level < last)
                def _():
                    self.up(k, hop, origin, hop).start()

            self.across(k, origin, core, hop).start()

        @pl.when(level + hop <= last)
        def _():
            origin = level + hop
            self.down(k, hop, origin, hop - 1).wait_recv()
            if hop < last:

                @pl.when(level > 0)
                def _():
                    self.down(k, hop, origin, hop).start()

            self.across(k, origin, core, last + hop).start()

    def ready(self, k):
        group, level, core = self.at
        last = self.levels - 1
        self.across(k, level, 1 - core, 0).wait_recv()
        for hop in range(1, self.levels):

            @pl.when(level >= hop)
            def _():
                self.across(k, level - hop, 1 - core, hop).wait_recv()

            @pl.when(level + hop <= last)
            def _():
                self.across(k, level + hop, 1 - core, last + hop).wait_recv()

    def drain(self):
        group, level, core = self.at
        last = self.levels - 1

        def one(k, _):
            self.across(k, level, core, 0).wait_send()
            for hop in range(self.levels):
                if hop < last:

                    @pl.when((level >= hop) & (level < last))
                    def _():
                        self.up(k, hop, level - hop, hop).wait_send()

                    @pl.when((level + hop <= last) & (level > 0))
                    def _():
                        self.down(k, hop, level + hop, hop).wait_send()

                if hop > 0:

                    @pl.when(level >= hop)
                    def _():
                        self.across(k, level - hop, core, hop).wait_send()

                    @pl.when(level + hop <= last)
                    def _():
                        self.across(k, level + hop, core, last + hop).wait_send()

            return 0

        lax.fori_loop(0, self.count, one, 0)


class Scatter:
    def __init__(self, at, sizes, count, part, cross, from_below, from_above, total, sems):
        self.at, self.levels, self.count = at, sizes[1], count
        self.part, self.cross, self.from_below, self.from_above, self.total = (
            part,
            cross,
            from_below,
            from_above,
            total,
        )
        self.sent_core, self.got_core, self.sent_up, self.got_up, self.sent_down, self.got_down = sems

    @staticmethod
    def scratch(count, sizes, piece):
        levels = sizes[1]
        dma = pltpu.SemaphoreType.DMA
        return (
            [pltpu.VMEM((count, levels, 2) + piece, jnp.bfloat16)]
            + [pltpu.VMEM((count, levels) + piece, jnp.bfloat16) for _ in range(3)]
            + [pltpu.VMEM(piece, jnp.float32)]
            + [dma((count,)) for _ in range(2)]
            + [dma((levels, count)) for _ in range(4)]
        )

    def across(self, k):
        group, level, core = self.at
        return pltpu.make_async_remote_copy(
            src_ref=self.part.at[k, :, 1 - core],
            dst_ref=self.cross.at[k],
            send_sem=self.sent_core.at[k],
            recv_sem=self.got_core.at[k],
            device_id=(group, level, 1 - core),
            device_id_type=MESH,
        )

    def up(self, k, owner):
        group, level, core = self.at
        return pltpu.make_async_remote_copy(
            src_ref=self.cross.at[k, owner],
            dst_ref=self.from_below.at[k, owner],
            send_sem=self.sent_up.at[owner, k],
            recv_sem=self.got_up.at[owner, k],
            device_id=(group, lax.rem(level + 1, self.levels), core),
            device_id_type=MESH,
        )

    def down(self, k, owner):
        group, level, core = self.at
        return pltpu.make_async_remote_copy(
            src_ref=self.cross.at[k, owner],
            dst_ref=self.from_above.at[k, owner],
            send_sem=self.sent_down.at[owner, k],
            recv_sem=self.got_down.at[owner, k],
            device_id=(group, lax.rem(level + self.levels - 1, self.levels), core),
            device_id_type=MESH,
        )

    def start(self, k):
        self.across(k).start()

    def join(self, k):
        core = self.at[2]
        self.across(k).wait_recv()
        for owner in range(self.levels):
            self.cross[k, owner] = lowered(wide(self.part[k, owner, core]) + wide(self.cross[k, owner]))

    def step_up(self, k):
        level = self.at[1]
        for owner in range(self.levels - 1, 0, -1):

            @pl.when(level < owner)
            def _():
                @pl.when(level > 0)
                def _():
                    self.up(k, owner).wait_recv()
                    self.cross[k, owner] = lowered(wide(self.cross[k, owner]) + wide(self.from_below[k, owner]))

                self.up(k, owner).start()

    def step_down(self, k):
        level = self.at[1]
        for owner in range(self.levels - 1):

            @pl.when(level > owner)
            def _():
                @pl.when(level < self.levels - 1)
                def _():
                    self.down(k, owner).wait_recv()
                    self.cross[k, owner] = lowered(wide(self.cross[k, owner]) + wide(self.from_above[k, owner]))

                self.down(k, owner).start()

    def steps(self, wave):
        level = self.at[1]
        above = wave - level
        below = wave - (self.levels - 1 - level)

        @pl.when(within(above, self.count))
        def _():
            self.step_up(above)

        @pl.when(within(below, self.count))
        def _():
            self.step_down(below)

    def finish(self, k):
        level = self.at[1]
        self.total[...] = wide(self.cross[k, level])

        @pl.when(level > 0)
        def _():
            self.up(k, level).wait_recv()
            self.total[...] += wide(self.from_below[k, level])

        @pl.when(level < self.levels - 1)
        def _():
            self.down(k, level).wait_recv()
            self.total[...] += wide(self.from_above[k, level])

    def drain(self):
        level = self.at[1]

        def one(k, _):
            self.across(k).wait_send()
            for owner in range(self.levels):

                @pl.when(level < owner)
                def _():
                    self.up(k, owner).wait_send()

                @pl.when(level > owner)
                def _():
                    self.down(k, owner).wait_send()

            return 0

        lax.fori_loop(0, self.count, one, 0)


def in_order(count, step):
    def body(number, carry):
        step(number)
        return carry

    lax.fori_loop(0, count, body, 0)


def span(number, size):
    return pl.ds(pl.multiple_of(number * size, size), size)


class Swap:
    def __init__(self, at, sizes, items, sems):
        self.at, self.count, self.items = at, sizes[0], items
        self.local, self.sent, self.got = sems

    scratch = Spread.scratch

    def block(self, number, owner):
        source, target, axis = self.items[number]
        size = source.shape[axis] // self.count
        window = pl.ds(pl.multiple_of(owner * size, size), size)
        return source.at[window] if axis == 0 else source.at[:, window]

    def own(self, number):
        return pltpu.make_async_copy(
            self.block(number, self.at[0]), self.items[number][1].at[0], self.local.at[number]
        )

    def away(self, number, k):
        peer = lax.rem(self.at[0] + k, self.count)
        return pltpu.make_async_remote_copy(
            src_ref=self.block(number, peer),
            dst_ref=self.items[number][1].at[k],
            send_sem=self.sent.at[number, k - 1],
            recv_sem=self.got.at[number, k - 1],
            device_id=(peer,) + self.at[1:],
            device_id_type=MESH,
        )

    def start(self, number):
        self.own(number).start()
        for k in range(1, self.count):
            self.away(number, k).start()

    def wait(self, number):
        self.own(number).wait()
        for k in range(1, self.count):
            self.away(number, k).wait()


def matmul(left, right):
    return jnp.dot(left, right, preferred_element_type=jnp.float32)


def open_kernel(sizes, shards, gain, *refs):
    x_part, gain, *refs = (shards, gain) + refs
    sources, refs = refs[:5], refs[5:]
    normed_out, query_out, key_out, value_out, swish_out, *refs = refs
    weight_outs, refs = refs[:5], refs[5:]
    rows_out, unit_out, scale_out, *refs = refs
    full, *refs = refs
    gather_sems, refs = refs[:6], refs[6:]
    spread_sems, refs = refs[:3], refs[3:]
    weights, refs = refs[:4], refs[4:]
    normed, query, keys, values, swish, load_sem, out_sem, weight_sem, normed_sem = refs
    at = around(AXES)
    group, level, core = at
    place = 2 * level + core
    count, levels, _, chunk, width = full.shape
    ranks = 2 * levels
    load = pltpu.make_async_copy(x_part, full.at[:, level, core], load_sem)
    load.start()
    greet(plane_peers(at, sizes) + column_peers(at, sizes))
    items = [(s, t, 0) for s, t in zip(sources[:4], weights)] + [(sources[4], weight_outs[4], 1)]
    spread = Spread(at, sizes, items, spread_sems)
    gather = Gather(at, sizes, count, full, gather_sems)
    load.wait()
    gather.start(0)
    for number in range(5):
        spread.start(number)
    piece = chunk // ranks

    def norm(k):
        def block(number, carry):
            rows = span(number, 16)
            value = jnp.concatenate(
                [wide(full[k, q, c, rows, :]) for q in range(levels) for c in range(2)], axis=1
            )
            unit, scale = layer_norm(value, EPSILON)
            where = pl.ds(pl.multiple_of(k * chunk + number * 16, 16), 16)
            normed[where, :] = lowered(unit * gain[...])
            mine = wide(full[k, level, core, rows, :])
            mean = jnp.mean(value, -1, keepdims=True)
            unit_out[where, :] = (mine - mean) * scale
            scale_out[where, :] = jnp.broadcast_to(scale, (16, 128))
            return carry

        lax.fori_loop(0, chunk // 16, block, 0)
        mine = span(place, piece)
        rows_out[span(k, piece), :] = jnp.concatenate(
            [full[k, q, c, mine, :] for q in range(levels) for c in range(2)], axis=1
        )
        pltpu.make_async_copy(
            normed.at[span(k, chunk)], normed_out.at[span(k, chunk)], normed_sem.at[k]
        ).start()

    def wave(number):
        @pl.when(number + 1 < count)
        def _():
            gather.start(number + 1)

        for hop in range(1, levels):

            @pl.when(within(number - hop, count))
            def _():
                gather.hop(number - hop, hop)

        @pl.when(within(number - levels, count))
        def _():
            gather.ready(number - levels)
            norm(number - levels)

    in_order(count + levels, wave)
    outs = [(query, query_out), (keys, key_out), (values, value_out), (swish, swish_out)]
    for number, (held, out) in enumerate(outs):
        spread.wait(number)
        pltpu.make_async_copy(weights[number], weight_outs[number], weight_sem.at[number]).start()

        def rows(k):
            where = span(k, chunk)
            held[where, :] = matmul(normed[where, :], weights[number][...]).astype(held.dtype)

        in_order(count, rows)
        pltpu.make_async_copy(held, out, out_sem.at[number]).start()
    spread.wait(4)
    for number, (held, out) in enumerate(outs):
        pltpu.make_async_copy(held, out, out_sem.at[number]).wait()
        pltpu.make_async_copy(weights[number], weight_outs[number], weight_sem.at[number]).wait()
    for number in range(5):
        spread.drain(number)
    gather.drain()

    def stored(k):
        pltpu.make_async_copy(
            normed.at[span(k, chunk)], normed_out.at[span(k, chunk)], normed_sem.at[k]
        ).wait()

    in_order(count, stored)


def middle_kernel(sizes, mixed_in, out_w, x_rows, gain, gate_src, up_src, down_src, dy_src, *refs):
    normed_out, gate_out, up_out, hidden_out, resid_out, gate_w_out, up_w_out, down_w_out, dy_out, *refs = refs
    scatter_refs, refs = refs[:11], refs[11:]
    full, *refs = refs
    gather_sems, refs = refs[:6], refs[6:]
    spread_sems, refs = refs[:3], refs[3:]
    gate_w, up_w, gate, up, store_sem, weight_sem = refs
    at = around(AXES)
    group, level, core = at
    count, levels, _, piece, width = full.shape
    chunk = 2 * levels * piece
    greet(plane_peers(at, sizes) + column_peers(at, sizes))
    spread = Spread(
        at,
        sizes,
        [(gate_src, gate_w, 0), (up_src, up_w, 0), (down_src, down_w_out, 1), (dy_src, dy_out, 0)],
        spread_sems,
    )
    for number in range(4):
        spread.start(number)
    part = scatter_refs[0]
    scatter = Scatter(at, sizes, count, *scatter_refs[:5], scatter_refs[5:])
    gather = Gather(at, sizes, count, full, gather_sems)
    tile = 512

    def stores(k):
        where = span(k, chunk)
        copies = [
            pltpu.make_async_copy(held.at[where], out.at[where], store_sem.at[number, k])
            for number, (held, out) in enumerate(((gate, gate_out), (up, up_out)))
        ]
        for q in range(levels):
            for c in range(2):
                rows = pl.ds(pl.multiple_of(k * chunk + (2 * q + c) * piece, piece), piece)
                copies.append(
                    pltpu.make_async_copy(full.at[k, q, c], normed_out.at[rows], store_sem.at[2 + 2 * q + c, k])
                )
        return copies

    def first(k):
        rows = mixed_in[span(k, chunk), :]
        for column in range(0, width, tile):
            value = matmul(rows, out_w[:, column : column + tile])
            part[k, :, :, :, column : column + tile] = lowered(value).reshape(levels, 2, piece, tile)
        scatter.start(k)

    def norm(k):
        scatter.finish(k)
        rows = span(k, piece)

        def block(number, carry):
            sub = span(number, 16)
            where = pl.ds(pl.multiple_of(k * piece + number * 16, 16), 16)
            resid = wide(x_rows[where, :]) + scatter.total[sub, :]
            resid_out[where, :] = resid
            unit, _ = layer_norm(resid, EPSILON)
            full[k, level, core, sub, :] = lowered(unit * gain[...])
            return carry

        lax.fori_loop(0, piece // 16, block, 0)
        gather.start(k)

    def last(k):
        gather.ready(k)
        rows = full[k].reshape(chunk, width)
        where = span(k, chunk)
        gate[where, :] = matmul(rows, gate_w[...])
        up[where, :] = matmul(rows, up_w[...])
        for copy in stores(k):
            copy.start()
        hidden_out[where, :] = lowered(jax.nn.gelu(gate[where, :]) * up[where, :])

    lag = levels - 1

    def wave(number):
        @pl.when(number < count)
        def _():
            first(number)

        for hop in range(1, levels):

            @pl.when(within(number - lag - hop, count))
            def _():
                gather.hop(number - lag - hop, hop)

        @pl.when(number == 2 * lag + 1)
        def _():
            spread.wait(0)
            spread.wait(1)
            pltpu.make_async_copy(gate_w, gate_w_out, weight_sem.at[0]).start()
            pltpu.make_async_copy(up_w, up_w_out, weight_sem.at[1]).start()

        @pl.when(within(number - 2 * lag - 1, count))
        def _():
            last(number - 2 * lag - 1)

        @pl.when(number < count)
        def _():
            scatter.join(number)

        scatter.steps(number)

        @pl.when(within(number - lag, count))
        def _():
            norm(number - lag)

    in_order(count + 2 * lag + 1, wave)
    spread.wait(2)
    spread.wait(3)
    pltpu.make_async_copy(gate_w, gate_w_out, weight_sem.at[0]).wait()
    pltpu.make_async_copy(up_w, up_w_out, weight_sem.at[1]).wait()
    for number in range(4):
        spread.drain(number)
    scatter.drain()
    gather.drain()

    def stored(k):
        for copy in stores(k):
            copy.wait()

    in_order(count, stored)


def feed_kernel(sizes, dy_part, hidden, gate, up, down_w, resid, *refs):
    mixed_out, dy_out, gate_grad, up_grad, dy_rows, *refs = refs
    scatter_refs, refs = refs[:11], refs[11:]
    full, *refs = refs
    gather_sems, refs = refs[:6], refs[6:]
    tile_acc, load_sem, store_sem = refs
    at = around(AXES)
    group, level, core = at
    place = 2 * level + core
    count, levels, _, chunk, width = full.shape
    ranks = 2 * levels
    piece = chunk // ranks
    load = pltpu.make_async_copy(dy_part, full.at[:, level, core], load_sem)
    load.start()
    greet(column_peers(at, sizes))
    part = scatter_refs[0]
    scatter = Scatter(at, sizes, count, *scatter_refs[:5], scatter_refs[5:])
    gather = Gather(at, sizes, count, full, gather_sems)
    load.wait()
    gather.start(0)

    def stores(k):
        return [
            pltpu.make_async_copy(
                full.at[k, q, c],
                dy_out.at[span(k, chunk), (2 * q + c) * width : (2 * q + c + 1) * width],
                store_sem.at[2 * q + c, k],
            )
            for q in range(levels)
            for c in range(2)
        ]

    def first(k):
        rows = hidden[span(k, chunk), :]
        mine = span(place, piece)
        for rank in range(ranks):
            columns = slice(rank * width, (rank + 1) * width)
            tile_acc[...] = matmul(rows, down_w[:, columns])
            tile_acc[mine, :] += resid[span(k, piece), columns]
            part[k, rank // 2, rank % 2] = lowered(tile_acc[...])
        scatter.start(k)

    def last(k):
        gather.ready(k)
        for copy in stores(k):
            copy.start()
        where = span(k, chunk)
        rows = jnp.concatenate([full[k, q, c] for q in range(levels) for c in range(2)], axis=1)
        back = inner_rows(rows, down_w[...])
        mine = span(place, piece)
        dy_rows[span(k, piece), :] = jnp.concatenate(
            [full[k, q, c, mine, :] for q in range(levels) for c in range(2)], axis=1
        )
        g, u = gate[where, :], up[where, :]
        root = 0.7978845608028654
        bend = jnp.tanh(root * (g + 0.044715 * g * g * g))
        curve = 0.5 * (1.0 + bend)
        slope = curve + 0.5 * g * (1.0 - bend * bend) * root * (1.0 + 0.134145 * g * g)
        gate_grad[where, :] = lowered(back * u * slope)
        up_grad[where, :] = lowered(back * g * curve)

    lag = levels - 1

    def wave(number):
        @pl.when(number + 1 < count)
        def _():
            gather.start(number + 1)

        @pl.when(number < count)
        def _():
            first(number)

        for hop in range(1, levels):

            @pl.when(within(number - hop, count))
            def _():
                gather.hop(number - hop, hop)

        @pl.when(number < count)
        def _():
            scatter.join(number)

        scatter.steps(number)

        @pl.when(within(number - lag, count))
        def _():
            scatter.finish(number - lag)
            mixed_out[span(number - lag, chunk), :] = lowered(scatter.total[...])

        @pl.when(within(number - levels, count))
        def _():
            last(number - levels)

    in_order(count + levels, wave)
    scatter.drain()
    gather.drain()

    def stored(k):
        for copy in stores(k):
            copy.wait()

    in_order(count, stored)


def back_kernel(sizes, gate_grad, up_grad, gate_w, up_w, resid, dy_rows, gain, out_w, retained, swish, *refs):
    sources, refs = refs[:4], refs[4:]
    branch_out, swish_grad, retained_grad, gain_out, *refs = refs
    targets, refs = refs[:4], refs[4:]
    scatter_refs, refs = refs[:11], refs[11:]
    full, *refs = refs
    gather_sems, refs = refs[:6], refs[6:]
    spread_sems, refs = refs[:3], refs[3:]
    swap_sems, refs = refs[:3], refs[3:]
    (store_sem,) = refs
    at = around(AXES)
    group, level, core = at
    count, levels, _, piece, width = full.shape
    chunk = 2 * levels * piece
    greet(plane_peers(at, sizes) + column_peers(at, sizes))
    spread = Spread(at, sizes, [(sources[0], targets[0], 0)], spread_sems)
    swap = Swap(at, sizes, list(zip(sources[1:], targets[1:], (1, 0, 0))), swap_sems)
    spread.start(0)
    for number in range(3):
        swap.start(number)
    part = scatter_refs[0]
    scatter = Scatter(at, sizes, count, *scatter_refs[:5], scatter_refs[5:])
    gather = Gather(at, sizes, count, full, gather_sems)
    gain_out[...] = jnp.zeros(gain_out.shape, jnp.float32)
    tile = 512

    def stores(k):
        copies = []
        for q in range(levels):
            for c in range(2):
                rows = pl.ds(pl.multiple_of(k * chunk + (2 * q + c) * piece, piece), piece)
                copies.append(
                    pltpu.make_async_copy(full.at[k, q, c], branch_out.at[rows], store_sem.at[2 * q + c, k])
                )
        return copies

    def first(k):
        where = span(k, chunk)
        for column in range(0, width, tile):
            columns = slice(column, column + tile)
            value = inner_rows(gate_grad[where, :], gate_w[columns, :])
            value += inner_rows(up_grad[where, :], up_w[columns, :])
            part[k, :, :, :, columns] = lowered(value).reshape(levels, 2, piece, tile)
        scatter.start(k)

    def norm(k):
        scatter.finish(k)

        def block(number, carry):
            sub = span(number, 16)
            where = pl.ds(pl.multiple_of(k * piece + number * 16, 16), 16)
            unit, scale = layer_norm(resid[where, :], EPSILON)
            delta = scatter.total[sub, :]
            outer = delta * unit
            gain_out[...] += outer[:8] + outer[8:]
            value = wide(dy_rows[where, :]) + norm_back(delta * gain[...], unit, scale)
            full[k, level, core, sub, :] = lowered(value)
            return carry

        lax.fori_loop(0, piece // 16, block, 0)
        gather.start(k)

    def last(k):
        gather.ready(k)
        for copy in stores(k):
            copy.start()
        rows = full[k].reshape(chunk, width)
        where = span(k, chunk)
        delta = inner_rows(rows, out_w[...])
        normed, scale = layer_norm(retained[where, :], GROUP_EPS)
        value = swish[where, :]
        gated = jax.nn.sigmoid(value)
        swish_grad[where, :] = lowered(delta * normed * gated * (1.0 + value * (1.0 - gated)))
        retained_grad[where, :] = lowered(norm_back(delta * value * gated, normed, scale))

    lag = levels - 1

    def wave(number):
        @pl.when(number < count)
        def _():
            first(number)

        for hop in range(1, levels):

            @pl.when(within(number - lag - hop, count))
            def _():
                gather.hop(number - lag - hop, hop)

        @pl.when(within(number - 2 * lag - 1, count))
        def _():
            last(number - 2 * lag - 1)

        @pl.when(number < count)
        def _():
            scatter.join(number)

        scatter.steps(number)

        @pl.when(within(number - lag, count))
        def _():
            norm(number - lag)

    in_order(count + 2 * lag + 1, wave)
    spread.wait(0)
    for number in range(3):
        swap.wait(number)
    spread.drain(0)
    scatter.drain()
    gather.drain()

    def stored(k):
        for copy in stores(k):
            copy.wait()

    in_order(count, stored)


def close_kernel(sizes, gain, normed_in, *refs):
    deltas, refs = refs[:4], refs[4:]
    weights, refs = refs[:4], refs[4:]
    number_of = len(SWAP_AXES)
    sources, refs = refs[:number_of], refs[number_of:]
    delta_out, sums_out, *refs = refs
    targets, refs = refs[:number_of], refs[number_of:]
    scatter_refs, refs = refs[:11], refs[11:]
    swap_sems, refs = refs[:3], refs[3:]
    sums, sums_sent, sums_got = refs
    at = around(AXES)
    group, level, core = at
    place = 2 * level + core
    part = scatter_refs[0]
    count, levels, _, chunk, width = part.shape
    ranks = 2 * levels
    greet(plane_peers(at, sizes) + column_all(at, sizes))
    swap = Swap(at, sizes, [(s, t, a) for s, t, a in zip(sources, targets, SWAP_AXES)], swap_sems)
    for number in range(number_of):
        swap.start(number)
    scatter = Scatter(at, sizes, count, *scatter_refs[:5], scatter_refs[5:])

    def first(k):
        where = span(k, chunk)
        rows = [d[where, :] for d in deltas]
        one = jnp.zeros((chunk, width), jnp.float32)
        two = jnp.zeros((chunk, width), jnp.float32)
        for rank in range(ranks):
            columns = slice(rank * width, (rank + 1) * width)
            value = inner_rows(rows[0], weights[0][columns, :])
            for row, weight in zip(rows[1:], weights[1:]):
                value += inner_rows(row, weight[columns, :])
            part[k, rank // 2, rank % 2] = lowered(value)
            one += value * gain[:, columns]
            two += value * wide(normed_in[where, columns])
        scatter.start(k)
        ones = jnp.ones((8, width), jnp.float32)
        flat = [
            lax.dot_general(
                ones,
                item,
                (((1,), (1,)), ((), ())),
                precision=lax.Precision.HIGHEST,
                preferred_element_type=jnp.float32,
            )
            for item in (one, two)
        ]
        line = lax.broadcasted_iota(jnp.int32, (8, chunk), 0)
        sums[place, k] = jnp.where(line == 0, flat[0], flat[1])

    def sums_copy(k):
        peer = lax.rem(place + k, ranks)
        return pltpu.make_async_remote_copy(
            src_ref=sums.at[place],
            dst_ref=sums.at[place],
            send_sem=sums_sent.at[k - 1],
            recv_sem=sums_got.at[k - 1],
            device_id=(group, peer // 2, lax.rem(peer, 2)),
            device_id_type=MESH,
        )

    def sums_landed(k):
        peer = lax.rem(place + ranks - k, ranks)
        return pltpu.make_async_remote_copy(
            src_ref=sums.at[peer],
            dst_ref=sums.at[peer],
            send_sem=sums_sent.at[k - 1],
            recv_sem=sums_got.at[k - 1],
            device_id=(group, peer // 2, lax.rem(peer, 2)),
            device_id_type=MESH,
        )

    lag = levels - 1

    def wave(number):
        @pl.when(number < count)
        def _():
            first(number)
            scatter.join(number)

        scatter.steps(number)

        @pl.when(number == count - 1)
        def _():
            for k in range(1, ranks):
                sums_copy(k).start()

        @pl.when(within(number - lag, count))
        def _():
            scatter.finish(number - lag)
            delta_out[span(number - lag, chunk), :] = scatter.total[...]

    in_order(count + lag, wave)
    for k in range(1, ranks):
        sums_landed(k).wait_recv()
    sums_out[...] = jnp.sum(sums[...], 0)
    for k in range(1, ranks):
        sums_copy(k).wait_send()
    for number in range(number_of):
        swap.wait(number)
    scatter.drain()


def spread_kernel(sizes, number_of, axes, *refs):
    sources, refs = refs[:number_of], refs[number_of:]
    targets, sems = refs[:number_of], refs[number_of:]
    at = around(AXES)
    greet(plane_peers(at, sizes))
    spread = Spread(at, sizes, list(zip(sources, targets, axes)), sems)
    for number in range(number_of):
        spread.start(number)
    for number in range(number_of):
        spread.wait(number)
    for number in range(number_of):
        spread.drain(number)


def column_all(at, sizes):
    group, level, core = at
    return column_peers(at, sizes) + [
        (group, lax.rem(level + k, sizes[1]), 1 - core) for k in range(1, sizes[1])
    ]


def struct(shape, kind=jnp.bfloat16):
    return jax.ShapeDtypeStruct(shape, kind)


VMEM = pltpu.VMEM
DMA = pltpu.SemaphoreType.DMA


def kernel_call(body, number, ins, outs, scratch):
    places = {True: pl.BlockSpec(memory_space=pltpu.VMEM), False: pl.BlockSpec(memory_space=pl.ANY)}
    return pl.pallas_call(
        body,
        out_shape=[shape for _, shape in outs],
        in_specs=[places[inside] for inside, _ in ins],
        out_specs=[places[inside] for inside, _ in outs],
        scratch_shapes=scratch,
        compiler_params=pltpu.CompilerParams(
            collective_id=number, has_side_effects=True, vmem_limit_bytes=60 * 2**20
        ),
    )(*[array for _, array in ins])


def spread_shape(shard, axis, sizes):
    shape = list(shard.shape)
    shape[axis] *= sizes[0]
    return struct(tuple(shape), shard.dtype)


def swap_shape(whole, axis, sizes):
    shape = list(whole.shape)
    shape[axis] //= sizes[0]
    return struct((sizes[0],) + tuple(shape), whole.dtype)


def spread_call(number, shards, axes, sizes):
    count = len(shards)
    return kernel_call(
        functools.partial(spread_kernel, sizes, count, axes),
        number,
        [(False, s) for s in shards],
        [(False, spread_shape(s, a, sizes)) for s, a in zip(shards, axes)],
        Spread.scratch(count, sizes),
    )


def pick_rows(targets, carry, pieces):
    count = pieces[0].shape[0]
    inside = ((targets >= 0) & (targets < count))[:, None]
    position = jnp.clip(targets, 0, count - 1)
    return tuple(
        (
            jnp.where(inside, jnp.take(piece, position, axis=0), held)
            for piece, held in zip(pieces, carry)
        )
    )


def decay_block(start, seq_ids, log_decay, block, factor):
    every = jnp.arange(seq_ids.shape[0], dtype=jnp.int32)
    near = start + jnp.arange(block, dtype=jnp.int32)
    distance = near[:, None] - every[None, :]
    own = lax.dynamic_slice_in_dim(seq_ids, start, block)
    valid = (distance >= 0) & (own[:, None] == seq_ids[None, :])
    return (
        jnp.where(valid, jnp.exp(jnp.maximum(distance, 0).astype(jnp.float32) * log_decay), 0.0)
        * factor
    )


def shards(
    tokens,
    cotangent,
    lengths,
    dealing,
    w_query,
    w_key,
    w_value,
    w_swish,
    w_out,
    w_gate,
    w_up,
    w_down,
    gain_attn,
    gain_mlp,
):
    group = lax.axis_index("dp")
    place = lax.axis_index(("heads", "tensor"))
    rows_dev = tokens.shape[0]
    slice_width = tokens.shape[1]
    seq_count = lengths.shape[0]
    ident = jnp.arange(seq_count, dtype=jnp.int32)
    starts = jnp.cumsum(lengths) - lengths
    picked = lax.dynamic_slice_in_dim(dealing, group * SEQ_DEV, SEQ_DEV)
    match = picked[:, None] == ident[None, :]
    dealt_len = jnp.sum(jnp.where(match, lengths[None, :], 0), 1)
    home_start = jnp.sum(jnp.where(match, starts[None, :], 0), 1)
    dealt_start = jnp.cumsum(dealt_len) - dealt_len
    rows = jnp.arange(rows_dev, dtype=jnp.int32)
    seq_ids = jnp.sum((rows[:, None] >= dealt_start[None, :]).astype(jnp.int32), 1) - 1
    member = seq_ids[:, None] == jnp.arange(SEQ_DEV, dtype=jnp.int32)[None, :]
    source = jnp.sum(jnp.where(member, (home_start - dealt_start)[None, :], 0), 1) + rows
    sizes = (lax.axis_size("dp"), lax.axis_size("heads"))
    ranks = sizes[1] * lax.axis_size("tensor")
    chunk = ranks * PIECE
    chunks = rows_dev // chunk
    width = slice_width * ranks
    query_s, key_s, value_s, swish_s, out_s, gate_s, up_s, down_s = (
        lowered(w) for w in (w_query, w_key, w_value, w_swish, w_out, w_gate, w_up, w_down)
    )
    gain_rows = jnp.pad(jnp.stack([gain_attn, gain_mlp]), ((0, 6), (0, 0)))
    x_all, gains_all = spread_call(0, (tokens, gain_rows), (0, 0), sizes)
    gains_all = wide(lowered(gains_all.reshape(sizes[0], 8, -1)))
    wide_one = gains_all[:, 0].reshape(1, width)
    wide_two = gains_all[:, 1].reshape(1, width)
    empty = jnp.zeros(tokens.shape, jnp.bfloat16)
    (x_part,) = pick_rows(source, (empty,), (x_all,))
    qk_dim, v_dim = w_query.shape[1], w_value.shape[1]
    own = rows_dev // ranks
    first_shards = (query_s, key_s, value_s, swish_s, out_s)
    first_axes = (0, 0, 0, 0, 1)
    full_shapes = [spread_shape(s, a, sizes) for s, a in zip(first_shards, first_axes)]
    (
        normed_in,
        query,
        keys,
        values,
        swish_in,
        query_w,
        key_w,
        value_w,
        swish_w,
        out_w,
        x_rows,
        unit_share,
        scale_one,
    ) = kernel_call(
        functools.partial(open_kernel, sizes),
        1,
        [(False, x_part.reshape(chunks, chunk, slice_width)), (True, wide_one)]
        + [(False, s) for s in first_shards],
        [
            (False, struct((rows_dev, width))),
            (False, struct((rows_dev, qk_dim))),
            (False, struct((rows_dev, qk_dim))),
            (False, struct((rows_dev, v_dim))),
            (False, struct((rows_dev, v_dim), jnp.float32)),
        ]
        + [(False, s) for s in full_shapes]
        + [
            (True, struct((own, width))),
            (True, struct((rows_dev, slice_width), jnp.float32)),
            (True, struct((rows_dev, 128), jnp.float32)),
        ],
        Gather.scratch(chunks, sizes, (chunk, slice_width))
        + Spread.scratch(5, sizes)
        + [VMEM(s.shape, s.dtype) for s in full_shapes[:4]]
        + [
            VMEM((rows_dev, width), jnp.bfloat16),
            VMEM((rows_dev, qk_dim), jnp.bfloat16),
            VMEM((rows_dev, qk_dim), jnp.bfloat16),
            VMEM((rows_dev, v_dim), jnp.bfloat16),
            VMEM((rows_dev, v_dim), jnp.float32),
            DMA,
            DMA((4,)),
            DMA((4,)),
            DMA((chunks,)),
        ],
    )
    log_decay = jnp.log1p(-jnp.exp2(-5.0 - place.astype(jnp.float32)))
    score_factor = QK_DIM ** (-0.5)
    blocks = rows_dev // QBLOCK

    def forward_block(number):
        start = number * QBLOCK
        decay = decay_block(start, seq_ids, log_decay, QBLOCK, score_factor)
        weight = (inner_rows(lax.dynamic_slice_in_dim(query, start, QBLOCK), keys) * decay).astype(
            jnp.bfloat16
        )
        return product(weight, values)

    retained = lax.map(forward_block, jnp.arange(blocks, dtype=jnp.int32)).reshape(
        rows_dev, values.shape[1]
    )
    normed, _ = layer_norm(retained, GROUP_EPS)
    mixed_in = (swish_in * jax.nn.sigmoid(swish_in) * normed).astype(jnp.bfloat16)
    ff_dim = w_gate.shape[1]
    middle_shards = (gate_s, up_s, down_s, cotangent)
    middle_axes = (0, 0, 1, 0)
    middle_shapes = [spread_shape(s, a, sizes) for s, a in zip(middle_shards, middle_axes)]
    normed_mid, gate, up_proj, hidden, resid, gate_w, up_w, down_w, dy_all = kernel_call(
        functools.partial(middle_kernel, sizes),
        2,
        [(True, mixed_in), (True, out_w), (True, x_rows), (True, wide_two)]
        + [(False, s) for s in middle_shards],
        [
            (False, struct((rows_dev, width))),
            (False, struct((rows_dev, ff_dim), jnp.float32)),
            (False, struct((rows_dev, ff_dim), jnp.float32)),
            (True, struct((rows_dev, ff_dim))),
            (True, struct((own, width), jnp.float32)),
        ]
        + [(False, s) for s in middle_shapes],
        Scatter.scratch(chunks, sizes, (PIECE, width))
        + Gather.scratch(chunks, sizes, (PIECE, width))
        + Spread.scratch(4, sizes)
        + [
            VMEM(middle_shapes[0].shape, jnp.bfloat16),
            VMEM(middle_shapes[1].shape, jnp.bfloat16),
            VMEM((rows_dev, ff_dim), jnp.float32),
            VMEM((rows_dev, ff_dim), jnp.float32),
            DMA((2 + ranks, chunks)),
            DMA((2,)),
        ],
    )
    (dy_part,) = pick_rows(source, (empty,), (dy_all,))
    mixed_share, dy_full, delta_gate, delta_up, dy_rows = kernel_call(
        functools.partial(feed_kernel, sizes),
        3,
        [
            (False, dy_part.reshape(chunks, chunk, slice_width)),
            (True, hidden),
            (True, gate),
            (True, up_proj),
            (True, down_w),
            (True, resid),
        ],
        [
            (True, struct((rows_dev, slice_width))),
            (False, struct((rows_dev, width))),
            (True, struct((rows_dev, ff_dim))),
            (True, struct((rows_dev, ff_dim))),
            (True, struct((own, width))),
        ],
        Scatter.scratch(chunks, sizes, (chunk, slice_width))
        + Gather.scratch(chunks, sizes, (chunk, slice_width))
        + [VMEM((chunk, slice_width), jnp.float32), DMA, DMA((ranks, chunks))],
    )
    grad_down = lowered(inner_cols(hidden, dy_full))
    grad_gate = lowered(inner_cols(normed_mid, delta_gate))
    grad_up = lowered(inner_cols(normed_mid, delta_up))
    back_swaps = ((grad_down, 1), (grad_gate, 0), (grad_up, 0))
    delta_branch, delta_swish, delta_retained, gain_two_part, mixed_all, *ff_grads = kernel_call(
        functools.partial(back_kernel, sizes),
        4,
        [
            (True, delta_gate),
            (True, delta_up),
            (True, gate_w),
            (True, up_w),
            (True, resid),
            (True, dy_rows),
            (True, wide_two),
            (True, out_w),
            (True, retained),
            (True, swish_in),
            (False, mixed_share),
        ]
        + [(False, g) for g, _ in back_swaps],
        [
            (False, struct((rows_dev, width))),
            (True, struct((rows_dev, v_dim))),
            (True, struct((rows_dev, v_dim))),
            (True, struct((8, width), jnp.float32)),
            (False, spread_shape(mixed_share, 0, sizes)),
        ]
        + [(False, swap_shape(g, a, sizes)) for g, a in back_swaps],
        Scatter.scratch(chunks, sizes, (PIECE, width))
        + Gather.scratch(chunks, sizes, (PIECE, width))
        + Spread.scratch(1, sizes)
        + Swap.scratch(3, sizes)
        + [DMA((ranks, chunks))],
    )
    grad_out = lowered(inner_cols(mixed_in, delta_branch))

    def backward_block(carry, number):
        delta_keys, delta_values = carry
        start = number * QBLOCK
        decay = decay_block(start, seq_ids, log_decay, QBLOCK, score_factor)
        query_block = lax.dynamic_slice_in_dim(query, start, QBLOCK)
        grad_block = lax.dynamic_slice_in_dim(delta_retained, start, QBLOCK)
        weight = (inner_rows(query_block, keys) * decay).astype(jnp.bfloat16)
        delta_score = (inner_rows(grad_block, values) * decay).astype(jnp.bfloat16)
        delta_keys = delta_keys + inner_cols(delta_score, query_block)
        delta_values = delta_values + inner_cols(weight, grad_block)
        return ((delta_keys, delta_values), product(delta_score, keys))

    start_carry = (jnp.zeros(keys.shape, jnp.float32), jnp.zeros(values.shape, jnp.float32))
    (delta_keys, delta_values), delta_query = lax.scan(
        backward_block, start_carry, jnp.arange(blocks, dtype=jnp.int32)
    )
    delta_query = delta_query.reshape(rows_dev, query.shape[1]).astype(jnp.bfloat16)
    delta_keys = delta_keys.astype(jnp.bfloat16)
    delta_values = delta_values.astype(jnp.bfloat16)
    grad_query = lowered(inner_cols(normed_in, delta_query))
    grad_key = lowered(inner_cols(normed_in, delta_keys))
    grad_value = lowered(inner_cols(normed_in, delta_values))
    grad_swish = lowered(inner_cols(normed_in, delta_swish))
    close_swaps = tuple(zip((grad_query, grad_key, grad_value, grad_swish, grad_out), SWAP_AXES))
    delta_in, sums, *attn_grads = kernel_call(
        functools.partial(close_kernel, sizes),
        5,
        [(True, wide_one), (True, normed_in)]
        + [(True, d) for d in (delta_query, delta_keys, delta_values, delta_swish)]
        + [(True, w) for w in (query_w, key_w, value_w, swish_w)]
        + [(False, g) for g, _ in close_swaps],
        [
            (True, struct((rows_dev, slice_width), jnp.float32)),
            (True, struct((chunks, 8, chunk), jnp.float32)),
        ]
        + [(False, swap_shape(g, a, sizes)) for g, a in close_swaps],
        Scatter.scratch(chunks, sizes, (chunk, slice_width))
        + Swap.scratch(len(SWAP_AXES), sizes)
        + [VMEM((ranks, chunks, 8, chunk), jnp.float32), DMA((ranks - 1,)), DMA((ranks - 1,))],
    )
    col_start = place * slice_width
    mean_one = sums[:, 0].reshape(rows_dev, 1) / width
    mean_two = sums[:, 1].reshape(rows_dev, 1) / width
    gain_share = lax.dynamic_slice_in_dim(wide_one, col_start, slice_width, 1)
    resid_share = wide(lax.dynamic_slice_in_dim(delta_branch, col_start, slice_width, 1))
    grad_share = lowered(
        resid_share + scale_one[:, :1] * (delta_in * gain_share - mean_one - unit_share * mean_two)
    )
    gain_one_part = lax.dynamic_update_slice_in_dim(
        jnp.zeros((width,), jnp.float32), jnp.sum(delta_in * unit_share, 0), col_start, 0
    )
    gains = lax.psum(jnp.stack([gain_one_part, jnp.sum(gain_two_part, 0)]), AXES)
    gain_width = gain_attn.shape[0]
    gains = lax.dynamic_slice_in_dim(gains, group * gain_width, gain_width, 1)
    (grad_all,) = spread_call(6, (grad_share,), (0,), sizes)
    grads = [jnp.sum(wide(g), 0) for g in attn_grads + ff_grads[1:] + ff_grads[:1]]
    slot_match = dealing[:, None] == ident[None, :]
    slot_len = jnp.sum(jnp.where(slot_match, lengths[None, :], 0), 1)
    slot_home = jnp.sum(jnp.where(slot_match, starts[None, :], 0), 1)
    per_group = slot_len.reshape(-1, SEQ_DEV)
    slot_start = (jnp.cumsum(per_group, 1) - per_group).reshape(-1)
    slot_base = ident // SEQ_DEV * rows_dev + slot_start - slot_home
    owner_base = jnp.sum(jnp.where(dealing[None, :] == ident[:, None], slot_base[None, :], 0), 1)
    global_rows = group * rows_dev + rows
    seq_of = jnp.sum((global_rows[:, None] >= starts[None, :]).astype(jnp.int32), 1) - 1
    targets = (
        jnp.sum(jnp.where(seq_of[:, None] == ident[None, :], owner_base[None, :], 0), 1)
        + global_rows
    )
    mixed_rows, grad_rows = pick_rows(targets, (empty, empty), (mixed_all, grad_all))
    return (
        mixed_rows,
        grad_rows,
        grads[0],
        grads[1],
        grads[2],
        grads[3],
        grads[4],
        grads[5],
        grads[6],
        grads[7],
        gains[0],
        gains[1],
    )


def solution(mesh):
    in_specs = (
        P("dp", ("heads", "tensor")),
        P("dp", ("heads", "tensor")),
        P(),
        P(),
        P("dp", ("heads", "tensor")),
        P("dp", ("heads", "tensor")),
        P("dp", ("heads", "tensor")),
        P("dp", ("heads", "tensor")),
        P(("heads", "tensor"), "dp"),
        P("dp", ("heads", "tensor")),
        P("dp", ("heads", "tensor")),
        P(("heads", "tensor"), "dp"),
        P("dp"),
        P("dp"),
    )
    out_specs = (
        P("dp", ("heads", "tensor")),
        P("dp", ("heads", "tensor")),
        P("dp", ("heads", "tensor")),
        P("dp", ("heads", "tensor")),
        P("dp", ("heads", "tensor")),
        P("dp", ("heads", "tensor")),
        P(("heads", "tensor"), "dp"),
        P("dp", ("heads", "tensor")),
        P("dp", ("heads", "tensor")),
        P(("heads", "tensor"), "dp"),
        P("dp"),
        P("dp"),
    )
    return jax.shard_map(shards, mesh=mesh, in_specs=in_specs, out_specs=out_specs, check_vma=False)
```

time: 1800 us -> 837 us (0.47)
  waiting for transfers between devices: 1360 us -> 0 us
  Pallas kernels: 0 us -> 613 us
  matrix products: 252 us -> 95.4 us
  other arithmetic: 100 us -> 39.9 us
    pallas_call x0 -> x7, Pallas kernels: none -> 613 us  [kernel_call(): pl.pallas_call(body, out_shape=[shape for _, shape in outs], in_specs=[pl...]
    psum x3 -> x0, waiting for transfers between devices: 561 us -> none  [the longest x1 253 us: shards(): lax.psum(inner_rows(delta_gate, gate_w) + inner_rows(delta_up, up_w), ('h...]
    all_gather x14 -> x0, waiting for transfers between devices: 475 us -> none  [the longest x1 67.4 us: shards(): lax.all_gather(dy_part, ('heads', 'tensor'), axis=1, tiled=True)]
    reduce_scatter x9 -> x0, waiting for transfers between devices: 320 us -> none  [the longest x1 59.5 us: shards(): lax.psum_scatter(product(hidden, down_w).astype(jnp.bfloat16), ('heads',...]
    dot_general x11 -> x3, matrix products: 87.3 us -> 10.2 us  [inner_rows(): lax.dot_general(left, right, (((1,), (1,)), ((), ())), preferred_element_...]
    dot_general x14 -> x6, matrix products: 78.6 us -> 13.6 us  [product(): return jnp.dot(left, right, preferred_element_type=jnp.float32)]
    psum x0 -> x1, blocking collectives: none -> 38.9 us  [shards(): lax.psum(jnp.stack([gain_one_part, jnp.sum(gain_two_part, 0)]), AXES)]
    convert_element_type x17 -> x4, other arithmetic: 34.1 us -> 6.02 us  [the longest x1 3.69 us: shards(): (swish_in * jax.nn.sigmoid(swish_in) * normed).astype(jnp.bfloat16)]
  transfers between devices with their start and end apart: 26 -> 0, of which waited for: 26 -> 0; matrix products, arithmetic and copies ran while one was open for 12% -> 0% of each run, Pallas kernels for 0% -> 0%
where the time goes in v1:
time: 837 us; the launch traced here: 828 us
  Pallas kernels  613 us (73%)
  matrix products  95.4 us (11%)
  other arithmetic  39.9 us (5%)
  blocking collectives  38.9 us (5%)
  local copies, waits for them, and re-layouts  35.2 us (4%)
    pallas_call x7, Pallas kernels, kernel_call(): pl.pallas_call(body, out_shape=[shape for _, shape in outs], in_specs=[pl...  613 us
    dot_general x14, matrix products, inner_cols(): lax.dot_general(left, right, (((0,), (0,)), ((), ())), preferred_element_...  71.7 us
    psum x1, blocking collectives, shards(): lax.psum(jnp.stack([gain_one_part, jnp.sum(gain_two_part, 0)]), AXES)  38.9 us
    gather x4, local copies, waits for them, and re-layouts, pick_rows(): jnp.take(piece, position, axis=0)  25.2 us

profile of v1, /device:TPU:0, one launch (start us, length us, event | category | flops | bytes accessed | tf_op | source)
XLA Modules:
  0.0 828.1 jit_solution(16496582475291090815)
XLA Ops:
  4.7 1.3 select_maximum_fusion.refs_1_
  6.0 39.8 %shard_map.229 = (bf16[6144,256]{1,0:T(8,128)(2,1)}, f32[32,512]{1,0:T(8,128)}) custom-call(bf16[1536,256]{1,0:T(8,128)(2,1)} %refs_0_.1, f32[8,512]{1,0:T(8,128)} %select_maximum_fusion.refs_1_), custom_call_target="tpu_custom_call" | custom-call | tf_op jit(solution)/shard_map/pallas_call | solution.py:1041
  45.8 6.0 gather_fusion
  51.9 1.8 select_select_fusion.3
  58.4 100.1 %shard_map.230 = (bf16[1536,2048]{1,0:T(8,128)(2,1)}, bf16[1536,256]{1,0:T(8,128)(2,1)}, bf16[1536,256]{1,0:T(8,128)(2,1)}, bf16[1536,512]{1,0:T(8,128)(2,1)}, f...) custom-call(bf16[6,256,256]{2,1,0:T(8,128)(2,1)} %bitcast.83, ...), custom_call_target="tpu_custom_call" | custom-call | tf_op jit(solution)/shard_map/pallas_call | solution.py:1041
  158.7 15.9 %while.25 = (s32[]{:T(128)}, f32[3,512,512]{2,1,0:T(8,128)S(1)}, s32[3]{0:T(128)S(1)}, bf16[1536,256]{1,0:T(8,128)(2,1)}, bf16[1536,256]{1,0:T(8,128)(2,1)}, /*i...) while((s32[]{:T(128)}, f32[3,512,512]{2,1,0:T(8,128)S(1)}, ...), condition=%wide.region_13.15_spmd, body=%wide.region_12.14_spmd.sunk | while | flops 1216610816 | bytes 3689659 | solution.py:1211
  160.0 4.0 fusion.73
  165.3 4.0 fusion.73
  170.6 4.0 fusion.73
  175.5 3.7 multiply_convert_fusion.mixed_in
  181.8 120.6 %shard_map.231 = (bf16[1536,2048]{1,0:T(8,128)(2,1)}, f32[1536,512]{1,0:T(8,128)}, f32[1536,512]{1,0:T(8,128)}, bf16[1536,512]{1,0:T(8,128)(2,1)}, f32[192,2048]...) custom-call(bf16[1536,512]{1,0:T(8,128)(2,1)} %multiply_convert_fusi, ...), custom_call_target="tpu_custom_call" | custom-call | tf_op jit(solution)/shard_map/pallas_call | solution.py:1041
  302.4 6.8 gather_fusion.1
  309.2 3.2 select_select_fusion.2
  312.4 89.0 %shard_map.232 = (bf16[1536,256]{1,0:T(8,128)(2,1)}, bf16[1536,2048]{1,0:T(8,128)(2,1)}, bf16[1536,512]{1,0:T(8,128)(2,1)}, bf16[1536,512]{1,0:T(8,128)(2,1)}, bf16[192,2048]{1,0:T(8,128)(2,1)}) custom-call(bf16[6,256,256]{2,1,0:T(8,128)(2,1)} %bitcast.82, bf16[1536,512]{1,0:T(8,128)(2,1)} %get-tuple-element.168.hidden, ...), custom_call_target="tpu_custom_call" | custom-call | tf_op jit(solution)/shard_map/pallas_call | solution.py:1041
  401.4 8.2 convolution_convert_fusion.3.refs_3_
  409.6 7.8 convolution_convert_fusion.4.refs_2_
  417.5 4.7 convolution_convert_fusion.5.refs_1_
  422.1 123.0 %shard_map.233 = (bf16[1536,2048]{1,0:T(8,128)(2,1)}, bf16[1536,512]{1,0:T(8,128)(2,1)}, bf16[1536,512]{1,0:T(8,128)(2,1)}, f32[8,2048]{1,0:T(8,128)}, bf16[6144...) custom-call(bf16[1536,512]{1,0:T(8,128)(2,1)} %get-tuple-element.173, ...), custom_call_target="tpu_custom_call" | custom-call | tf_op jit(solution)/shard_map/pallas_call | solution.py:1041
  545.2 8.1 convolution_convert_fusion.refs_12_
  553.3 7.7 convolution_convert_fusion.1.refs_11_
  561.0 37.4 %while.26 = (s32[]{:T(128)}, f32[1536,256]{1,0:T(8,128)S(1)}, f32[1536,512]{1,0:T(8,128)}, bf16[3,512,256]{2,1,0:T(8,128)(2,1)S(1)}, s32[3]{0:T(128)S(1)}, /*ind...) while((s32[]{:T(128)}, f32[1536,256]{1,0:T(8,128)S(1)}, ...), condition=%wide.region_17.19_spmd.clone, body=%wide.region_16.18_spmd.clone.sunk | while | flops 2838233600 | bytes 22575872 | solution.py:1318
  562.6 5.2 convolution_add_fusion.5
  567.8 3.4 fusion.83
  571.2 1.2 convolution_add_fusion.4
  574.3 6.2 convolution_add_fusion.5
  580.5 3.4 fusion.83
  583.9 1.2 convolution_add_fusion.4
  587.0 6.2 convolution_add_fusion.5
  593.2 3.4 fusion.83
  596.6 1.2 convolution_add_fusion.4
  598.4 2.2 convert_element_type.150.refs_2_
  600.7 8.3 convolution_convert_fusion.2.refs_10_
  609.1 2.9 convolution_convert_fusion.6.refs_9_
  612.0 2.9 convolution_convert_fusion.7.refs_8_
  614.8 103.1 %shard_map.234 = (f32[1536,256]{1,0:T(8,128)}, f32[6,8,256]{2,1,0:T(8,128)}, bf16[4,512,256]{2,1,0:T(8,128)(2,1)}, bf16[4,512,256]{2,1,0:T(8,128)(2,1)}, bf16[4,...) custom-call(f32[1,2048]{1,0:T(1,128)} %bitcast.87, ...), custom_call_target="tpu_custom_call" | custom-call | tf_op jit(solution)/shard_map/pallas_call | solution.py:1041
  718.0 1.0 multiply_reduce_fusion.3
  719.0 1.4 slice_reduce_fusion
  721.1 3.4 multiply_reduce_fusion.1
  724.6 38.9 %psum.7 = f32[2,2048]{1,0:T(2,128)S(1)} all-reduce(f32[2,2048]{1,0:T(2,128)S(1)} %pad_maximum_fusion), channel_id=1, replica_groups=mesh['dp'=4,'heads'=4,'tensor'=2] {'dp','heads','tensor'}, use_global_device_ids=true, to_apply=%region_28.30 | all-reduce | flops 4096 | bytes 32768 | tf_op jit(solution)/shard_map/psum | solution.py:1356
  764.2 3.9 convert_reduce_fusion
  768.1 1.9 convert_reduce_fusion.3
  770.0 1.1 copy-done.6
  771.1 1.9 convert_reduce_fusion.2
  773.0 1.3 convert_reduce_fusion.6
  774.3 36.9 %shard_map.235 = bf16[6144,256]{1,0:T(8,128)(2,1)} custom-call(bf16[1536,256]{1,0:T(8,128)(2,1)} %get-tuple-element.291.refs_0_), custom_call_target="tpu_custom_call" | custom-call | tf_op jit(solution)/shard_map/pallas_call | solution.py:1041
  812.2 7.0 gather_fusion.3
  819.2 5.4 gather_fusion.2
  824.5 3.1 select_select_fusion
  (147 shorter events, 20.4 us)
Async XLA Ops:
  2.9 0.6 copy-start.24
  45.8 7.9 copy-start.23
  45.8 8.5 %copy-start.14 = (f32[512,512]{1,0:T(8,128)S(1)}, f32[512,512]{1,0:T(8,128)}, u32[]{:S(2)}) copy-start(f32[512,512]{1,0:T(8,128)} %param.26) | copy-start | bytes 3145732
  51.9 3.4 copy-start.15
  51.9 4.2 copy-start.16
  51.9 5.0 copy-start.20
  53.7 4.0 copy-start.21
  175.5 3.7 copy-start.17
  175.5 4.6 copy-start.18
  179.2 1.7 copy-start.19
  401.4 8.2 copy-start.10
  401.4 16.0 %slice-start.2 = ((s8[6291456]{0:T(1024)(128)(4,1)}), s8[4194304]{0:T(1024)(128)(4,1)S(1)}, s32[]{:S(2)}) async-start(s8[6291456]{0:T(1024)(128)(4,1)} %bitcast.100), calls=%async_computation.2 | async-start | bytes 8388608
  409.6 7.8 copy-start.11
  409.6 7.8 slice-start.3
  545.2 8.2 copy-start.9
  553.3 7.7 copy-start.3
  571.1 1.2 copy-start.28
  583.9 1.2 copy-start.28
  596.6 1.2 copy-start.28
  598.4 10.6 %slice-start = ((s8[6291456]{0:T(1024)(128)(4,1)}), s8[4194304]{0:T(1024)(128)(4,1)S(1)}, s32[]{:S(2)}) async-start(s8[6291456]{0:T(1024)(128)(4,1)} %bitcast.80), calls=%async_computation | async-start | bytes 8388608
  600.7 8.3 copy-start.1
  600.7 8.4 %slice-start.1 = ((s8[6291456]{0:T(1024)(128)(4,1)}), s8[2097152]{0:T(1024)(128)(4,1)S(1)}, s32[]{:S(2)}) async-start(s8[6291456]{0:T(1024)(128)(4,1)} %bitcast.80), calls=%async_computation.1 | async-start | bytes 4194304
  609.1 2.9 copy-start.2
  718.0 6.6 copy-start.22
  718.0 46.2 %copy-start.5 = (bf16[4,512,512]{2,1,0:T(8,128)(2,1)S(1)}, bf16[4,512,512]{2,1,0:T(8,128)(2,1)}, u32[]{:S(2)}) copy-start(bf16[4,512,512]{2,1,0:T(8,128)(2,1)} %get-tuple-element.204) | copy-start | bytes 6291460
  764.2 3.9 copy-start.7
  764.2 3.9 copy-start.8
  768.1 1.9 copy-start.4
  768.1 3.0 copy-start.6
  771.1 1.9 copy-start.12
  771.1 1.9 copy-start.13
  773.0 38.2 %copy-start.25 = (s32[12]{0:T(128)S(1)}, s32[12]{0:T(128)}, u32[]{:S(2)}) copy-start(s32[12]{0:T(128)} %copy-done.24) | copy-start | bytes 148
  773.0 38.2 %copy-start.26 = (s32[12]{0:T(128)S(1)}, s32[12]{0:T(128)}, u32[]{:S(2)}) copy-start(s32[12]{0:T(128)} %param.22) | copy-start | bytes 148
  773.0 38.2 %copy-start.27 = (s32[12]{0:T(128)S(1)}, s32[12]{0:T(128)}, u32[]{:S(2)}) copy-start(s32[12]{0:T(128)} %param.23) | copy-start | bytes 148
  812.2 7.0 copy-start

commit v2 on v1

--- a/solution.py
+++ b/solution.py
@@ -9,10 +9,8 @@
 
 QK_DIM = 256
 SEQ_DEV = 3
-QBLOCK = 512
 PIECE = 32
 AXES = ("dp", "heads", "tensor")
-TP = ("heads", "tensor")
 SWAP_AXES = (0, 0, 0, 0, 1)
 MESH = pl.DeviceIdType.MESH
 
@@ -270,25 +268,24 @@
 
 
 class Scatter:
-    def __init__(self, at, sizes, count, part, cross, from_below, from_above, total, sems):
+    REFS = 4
+
+    def __init__(self, at, sizes, count, refs):
         self.at, self.levels, self.count = at, sizes[1], count
-        self.part, self.cross, self.from_below, self.from_above, self.total = (
-            part,
-            cross,
-            from_below,
-            from_above,
-            total,
-        )
-        self.sent_core, self.got_core, self.sent_up, self.got_up, self.sent_down, self.got_down = sems
+        self.part, self.cross, self.inbox, self.total = refs[:4]
+        self.sent_core, self.got_core, self.sent_up, self.got_up, self.sent_down, self.got_down = refs[4:]
 
     @staticmethod
     def scratch(count, sizes, piece):
         levels = sizes[1]
         dma = pltpu.SemaphoreType.DMA
         return (
-            [pltpu.VMEM((count, levels, 2) + piece, jnp.bfloat16)]
-            + [pltpu.VMEM((count, levels) + piece, jnp.bfloat16) for _ in range(3)]
-            + [pltpu.VMEM(piece, jnp.float32)]
+            [
+                pltpu.VMEM((2, levels, 2) + piece, jnp.bfloat16),
+                pltpu.VMEM((count, levels) + piece, jnp.bfloat16),
+                pltpu.VMEM((count, levels + 1) + piece, jnp.bfloat16),
+                pltpu.VMEM(piece, jnp.float32),
+            ]
             + [dma((count,)) for _ in range(2)]
             + [dma((levels, count)) for _ in range(4)]
         )
@@ -296,7 +293,7 @@
     def across(self, k):
         group, level, core = self.at
         return pltpu.make_async_remote_copy(
-            src_ref=self.part.at[k, :, 1 - core],
+            src_ref=self.part.at[lax.rem(k, 2), :, 1 - core],
             dst_ref=self.cross.at[k],
             send_sem=self.sent_core.at[k],
             recv_sem=self.got_core.at[k],
@@ -308,7 +305,7 @@
         group, level, core = self.at
         return pltpu.make_async_remote_copy(
             src_ref=self.cross.at[k, owner],
-            dst_ref=self.from_below.at[k, owner],
+            dst_ref=self.inbox.at[k, owner + 1],
             send_sem=self.sent_up.at[owner, k],
             recv_sem=self.got_up.at[owner, k],
             device_id=(group, lax.rem(level + 1, self.levels), core),
@@ -319,13 +316,18 @@
         group, level, core = self.at
         return pltpu.make_async_remote_copy(
             src_ref=self.cross.at[k, owner],
-            dst_ref=self.from_above.at[k, owner],
+            dst_ref=self.inbox.at[k, owner],
             send_sem=self.sent_down.at[owner, k],
             recv_sem=self.got_down.at[owner, k],
             device_id=(group, lax.rem(level + self.levels - 1, self.levels), core),
             device_id_type=MESH,
         )
 
+    def free(self, k):
+        @pl.when(k >= 2)
+        def _():
+            self.across(k - 2).wait_send()
+
     def start(self, k):
         self.across(k).start()
 
@@ -333,7 +335,9 @@
         core = self.at[2]
         self.across(k).wait_recv()
         for owner in range(self.levels):
-            self.cross[k, owner] = lowered(wide(self.part[k, owner, core]) + wide(self.cross[k, owner]))
+            self.cross[k, owner] = lowered(
+                wide(self.part[lax.rem(k, 2), owner, core]) + wide(self.cross[k, owner])
+            )
 
     def step_up(self, k):
         level = self.at[1]
@@ -344,7 +348,7 @@
                 @pl.when(level > 0)
                 def _():
                     self.up(k, owner).wait_recv()
-                    self.cross[k, owner] = lowered(wide(self.cross[k, owner]) + wide(self.from_below[k, owner]))
+                    self.cross[k, owner] = lowered(wide(self.cross[k, owner]) + wide(self.inbox[k, owner + 1]))
 
                 self.up(k, owner).start()
 
@@ -357,7 +361,7 @@
                 @pl.when(level < self.levels - 1)
                 def _():
                     self.down(k, owner).wait_recv()
-                    self.cross[k, owner] = lowered(wide(self.cross[k, owner]) + wide(self.from_above[k, owner]))
+                    self.cross[k, owner] = lowered(wide(self.cross[k, owner]) + wide(self.inbox[k, owner]))
 
                 self.down(k, owner).start()
 
@@ -381,18 +385,21 @@
         @pl.when(level > 0)
         def _():
             self.up(k, level).wait_recv()
-            self.total[...] += wide(self.from_below[k, level])
+            self.total[...] += wide(self.inbox[k, level + 1])
 
         @pl.when(level < self.levels - 1)
         def _():
             self.down(k, level).wait_recv()
-            self.total[...] += wide(self.from_above[k, level])
+            self.total[...] += wide(self.inbox[k, level])
 
     def drain(self):
         level = self.at[1]
 
         def one(k, _):
-            self.across(k).wait_send()
+            @pl.when(k >= self.count - 2)
+            def _():
+                self.across(k).wait_send()
+
             for owner in range(self.levels):
 
                 @pl.when(level < owner)
@@ -418,6 +425,60 @@
 
 def span(number, size):
     return pl.ds(pl.multiple_of(number * size, size), size)
+
+
+class Moves:
+    def __init__(self, pairs, sems):
+        self.pairs, self.sems = pairs, sems
+
+    def copy(self, number):
+        return pltpu.make_async_copy(*self.pairs[number], self.sems.at[number])
+
+    def start(self, *numbers):
+        for number in numbers:
+            self.copy(number).start()
+
+    def wait(self, *numbers):
+        for number in numbers:
+            self.copy(number).wait()
+
+
+class Chunks:
+    def __init__(self, pairs, size, sems):
+        self.pairs, self.size, self.sems = pairs, size, sems
+
+    def start(self, k):
+        for number, (source, target) in enumerate(self.pairs):
+            rows = span(k, self.size)
+            pltpu.make_async_copy(source.at[rows], target.at[rows], self.sems.at[number, k]).start()
+
+    def wait(self, count):
+        def one(k, carry):
+            for number, (source, target) in enumerate(self.pairs):
+                rows = span(k, self.size)
+                pltpu.make_async_copy(source.at[rows], target.at[rows], self.sems.at[number, k]).wait()
+            return carry
+
+        lax.fori_loop(0, count, one, 0)
+
+
+def matmul(left, right):
+    return jnp.dot(left, right, preferred_element_type=jnp.float32)
+
+
+def decay_tile(near, far, size, bounds, rate):
+    rows = near * size + lax.broadcasted_iota(jnp.int32, (size, 1), 0)
+    columns = far * size + lax.broadcasted_iota(jnp.int32, (1, size), 1)
+    row_seq, column_seq = jnp.zeros((size, 1), jnp.int32), jnp.zeros((1, size), jnp.int32)
+    for number in range(1, SEQ_DEV):
+        row_seq += (rows >= bounds[number]).astype(jnp.int32)
+        column_seq += (columns >= bounds[number]).astype(jnp.int32)
+    distance = rows - columns
+    valid = (distance >= 0) & (row_seq == column_seq)
+    return (
+        jnp.where(valid, jnp.exp(jnp.maximum(distance, 0).astype(jnp.float32) * rate[0]), 0.0)
+        * QK_DIM ** (-0.5)
+    )
 
 
 class Swap:
@@ -460,8 +521,36 @@
             self.away(number, k).wait()
 
 
-def matmul(left, right):
-    return jnp.dot(left, right, preferred_element_type=jnp.float32)
+def deal_kernel(sizes, tokens, gains, *refs):
+    masters, refs = refs[:8], refs[8:]
+    tokens_out, gains_out, *refs = refs
+    rounded_out, refs = refs[:8], refs[8:]
+    spread_sems, refs = refs[:3], refs[3:]
+    held, refs = refs[:8], refs[8:]
+    rounded, refs = refs[:8], refs[8:]
+    load_sems, store_sems = refs
+    at = around(AXES)
+    loads = Moves(list(zip(masters, held)), load_sems)
+    stores = Moves(list(zip(rounded, rounded_out)), store_sems)
+    loads.start(*range(8))
+    greet(plane_peers(at, sizes))
+    spread = Spread(at, sizes, [(tokens, tokens_out, 0), (gains, gains_out, 0)], spread_sems)
+    spread.start(0)
+    spread.start(1)
+    for number in range(8):
+        loads.wait(number)
+
+        def block(k):
+            rows = span(k, 32)
+            rounded[number][rows, :] = lowered(held[number][rows, :])
+
+        in_order(held[number].shape[0] // 32, block)
+        stores.start(number)
+    stores.wait(*range(8))
+    spread.wait(0)
+    spread.wait(1)
+    spread.drain(0)
+    spread.drain(1)
 
 
 def open_kernel(sizes, shards, gain, *refs):
@@ -560,62 +649,91 @@
     in_order(count, stored)
 
 
-def middle_kernel(sizes, mixed_in, out_w, x_rows, gain, gate_src, up_src, down_src, dy_src, *refs):
-    normed_out, gate_out, up_out, hidden_out, resid_out, gate_w_out, up_w_out, down_w_out, dy_out, *refs = refs
-    scatter_refs, refs = refs[:11], refs[11:]
+def middle_kernel(sizes, bounds, rate, gain, *refs):
+    ins, refs = refs[:6], refs[6:]
+    sources, refs = refs[:4], refs[4:]
+    normed_out, gate_out, up_out, hidden_out, resid_out, retained_out, mixed_out, *refs = refs
+    gate_w_out, up_w_out, down_w_out, dy_out, *refs = refs
+    held, refs = refs[:6], refs[6:]
+    query, keys, values, swish, out_w, x_rows = held
+    scatter_refs, refs = refs[:10], refs[10:]
     full, *refs = refs
     gather_sems, refs = refs[:6], refs[6:]
     spread_sems, refs = refs[:3], refs[3:]
-    gate_w, up_w, gate, up, store_sem, weight_sem = refs
+    gate_w, up_w, gate, up, hidden, resid, retained, mixed_in, refs = *refs[:8], refs[8:]
+    load_sems, chunk_sems, normed_sems, weight_sems, resid_sem = refs
     at = around(AXES)
     group, level, core = at
     count, levels, _, piece, width = full.shape
     chunk = 2 * levels * piece
+    loads = Moves(list(zip(ins, held)), load_sems)
+    loads.start(*range(6))
     greet(plane_peers(at, sizes) + column_peers(at, sizes))
     spread = Spread(
         at,
         sizes,
-        [(gate_src, gate_w, 0), (up_src, up_w, 0), (down_src, down_w_out, 1), (dy_src, dy_out, 0)],
+        [
+            (sources[0], gate_w, 0),
+            (sources[1], up_w, 0),
+            (sources[2], down_w_out, 1),
+            (sources[3], dy_out, 0),
+        ],
         spread_sems,
     )
     for number in range(4):
         spread.start(number)
-    part = scatter_refs[0]
-    scatter = Scatter(at, sizes, count, *scatter_refs[:5], scatter_refs[5:])
+    scatter = Scatter(at, sizes, count, scatter_refs)
     gather = Gather(at, sizes, count, full, gather_sems)
+    weights = Moves([(gate_w, gate_w_out), (up_w, up_w_out)], weight_sems)
+    early = Chunks([(retained, retained_out), (mixed_in, mixed_out)], chunk, chunk_sems.at[:2])
+    late = Chunks([(gate, gate_out), (up, up_out), (hidden, hidden_out)], chunk, chunk_sems.at[2:])
+    loads.wait(*range(6))
     tile = 512
 
     def stores(k):
-        where = span(k, chunk)
-        copies = [
-            pltpu.make_async_copy(held.at[where], out.at[where], store_sem.at[number, k])
-            for number, (held, out) in enumerate(((gate, gate_out), (up, up_out)))
-        ]
+        copies = []
         for q in range(levels):
             for c in range(2):
                 rows = pl.ds(pl.multiple_of(k * chunk + (2 * q + c) * piece, piece), piece)
                 copies.append(
-                    pltpu.make_async_copy(full.at[k, q, c], normed_out.at[rows], store_sem.at[2 + 2 * q + c, k])
+                    pltpu.make_async_copy(full.at[k, q, c], normed_out.at[rows], normed_sems.at[2 * q + c, k])
                 )
         return copies
 
     def first(k):
-        rows = mixed_in[span(k, chunk), :]
+        where = span(k, chunk)
+        retained[where, :] = jnp.zeros((chunk, retained.shape[1]), jnp.float32)
+
+        def block(j, carry):
+            there = span(j, chunk)
+            decay = decay_tile(k, j, chunk, bounds, rate)
+            weight = lowered(inner_rows(query[where, :], keys[there, :]) * decay)
+            retained[where, :] += matmul(weight, values[there, :])
+            return carry
+
+        lax.fori_loop(0, k + 1, block, 0)
+        normed, _ = layer_norm(retained[where, :], GROUP_EPS)
+        value = swish[where, :]
+        mixed_in[where, :] = lowered(value * jax.nn.sigmoid(value) * normed)
+        early.start(k)
+        scatter.free(k)
+        rows = mixed_in[where, :]
         for column in range(0, width, tile):
             value = matmul(rows, out_w[:, column : column + tile])
-            part[k, :, :, :, column : column + tile] = lowered(value).reshape(levels, 2, piece, tile)
+            scatter.part[lax.rem(k, 2), :, :, :, column : column + tile] = lowered(value).reshape(
+                levels, 2, piece, tile
+            )
         scatter.start(k)
 
     def norm(k):
         scatter.finish(k)
-        rows = span(k, piece)
 
         def block(number, carry):
             sub = span(number, 16)
             where = pl.ds(pl.multiple_of(k * piece + number * 16, 16), 16)
-            resid = wide(x_rows[where, :]) + scatter.total[sub, :]
-            resid_out[where, :] = resid
-            unit, _ = layer_norm(resid, EPSILON)
+            value = wide(x_rows[where, :]) + scatter.total[sub, :]
+            resid[where, :] = value
+            unit, _ = layer_norm(value, EPSILON)
             full[k, level, core, sub, :] = lowered(unit * gain[...])
             return carry
 
@@ -624,13 +742,14 @@
 
     def last(k):
         gather.ready(k)
+        for copy in stores(k):
+            copy.start()
         rows = full[k].reshape(chunk, width)
         where = span(k, chunk)
         gate[where, :] = matmul(rows, gate_w[...])
         up[where, :] = matmul(rows, up_w[...])
-        for copy in stores(k):
-            copy.start()
-        hidden_out[where, :] = lowered(jax.nn.gelu(gate[where, :]) * up[where, :])
+        hidden[where, :] = lowered(jax.nn.gelu(gate[where, :]) * up[where, :])
+        late.start(k)
 
     lag = levels - 1
 
@@ -649,8 +768,7 @@
         def _():
             spread.wait(0)
             spread.wait(1)
-            pltpu.make_async_copy(gate_w, gate_w_out, weight_sem.at[0]).start()
-            pltpu.make_async_copy(up_w, up_w_out, weight_sem.at[1]).start()
+            weights.start(0, 1)
 
         @pl.when(within(number - 2 * lag - 1, count))
         def _():
@@ -667,14 +785,18 @@
             norm(number - lag)
 
     in_order(count + 2 * lag + 1, wave)
+    store_resid = pltpu.make_async_copy(resid, resid_out, resid_sem)
+    store_resid.start()
     spread.wait(2)
     spread.wait(3)
-    pltpu.make_async_copy(gate_w, gate_w_out, weight_sem.at[0]).wait()
-    pltpu.make_async_copy(up_w, up_w_out, weight_sem.at[1]).wait()
     for number in range(4):
         spread.drain(number)
     scatter.drain()
     gather.drain()
+    weights.wait(0, 1)
+    store_resid.wait()
+    early.wait(count)
+    late.wait(count)
 
     def stored(k):
         for copy in stores(k):
@@ -683,12 +805,16 @@
     in_order(count, stored)
 
 
-def feed_kernel(sizes, dy_part, hidden, gate, up, down_w, resid, *refs):
-    mixed_out, dy_out, gate_grad, up_grad, dy_rows, *refs = refs
-    scatter_refs, refs = refs[:11], refs[11:]
+def feed_kernel(sizes, dy_part, *refs):
+    ins, refs = refs[:5], refs[5:]
+    mixed_out, gate_grad_out, up_grad_out, dy_rows_out, down_grad_out, *refs = refs
+    held, refs = refs[:5], refs[5:]
+    hidden, down_w, resid, gate, up = held
+    scatter_refs, refs = refs[:10], refs[10:]
     full, *refs = refs
     gather_sems, refs = refs[:6], refs[6:]
-    tile_acc, load_sem, store_sem = refs
+    tile_acc, down_acc, down_grad, mixed, gate_grad, up_grad, dy_rows, refs = *refs[:7], refs[7:]
+    load_sem, load_sems, chunk_sems, end_sems = refs
     at = around(AXES)
     group, level, core = at
     place = 2 * level + core
@@ -697,38 +823,34 @@
     piece = chunk // ranks
     load = pltpu.make_async_copy(dy_part, full.at[:, level, core], load_sem)
     load.start()
+    loads = Moves(list(zip(ins, held)), load_sems)
+    loads.start(*range(5))
     greet(column_peers(at, sizes))
-    part = scatter_refs[0]
-    scatter = Scatter(at, sizes, count, *scatter_refs[:5], scatter_refs[5:])
+    scatter = Scatter(at, sizes, count, scatter_refs)
     gather = Gather(at, sizes, count, full, gather_sems)
+    store = Chunks(
+        [(mixed, mixed_out), (gate_grad, gate_grad_out), (up_grad, up_grad_out)], chunk, chunk_sems
+    )
+    early = Chunks(store.pairs[:1], chunk, chunk_sems.at[:1])
+    late = Chunks(store.pairs[1:], chunk, chunk_sems.at[1:])
     load.wait()
     gather.start(0)
-
-    def stores(k):
-        return [
-            pltpu.make_async_copy(
-                full.at[k, q, c],
-                dy_out.at[span(k, chunk), (2 * q + c) * width : (2 * q + c + 1) * width],
-                store_sem.at[2 * q + c, k],
-            )
-            for q in range(levels)
-            for c in range(2)
-        ]
+    loads.wait(0, 1, 2)
+    down_acc[...] = jnp.zeros(down_acc.shape, jnp.float32)
 
     def first(k):
+        scatter.free(k)
         rows = hidden[span(k, chunk), :]
         mine = span(place, piece)
         for rank in range(ranks):
             columns = slice(rank * width, (rank + 1) * width)
             tile_acc[...] = matmul(rows, down_w[:, columns])
             tile_acc[mine, :] += resid[span(k, piece), columns]
-            part[k, rank // 2, rank % 2] = lowered(tile_acc[...])
+            scatter.part[lax.rem(k, 2), rank // 2, rank % 2] = lowered(tile_acc[...])
         scatter.start(k)
 
     def last(k):
         gather.ready(k)
-        for copy in stores(k):
-            copy.start()
         where = span(k, chunk)
         rows = jnp.concatenate([full[k, q, c] for q in range(levels) for c in range(2)], axis=1)
         back = inner_rows(rows, down_w[...])
@@ -743,6 +865,10 @@
         slope = curve + 0.5 * g * (1.0 - bend * bend) * root * (1.0 + 0.134145 * g * g)
         gate_grad[where, :] = lowered(back * u * slope)
         up_grad[where, :] = lowered(back * g * curve)
+        late.start(k)
+        for rank in range(ranks):
+            columns = slice(rank * width, (rank + 1) * width)
+            down_acc[:, columns] += inner_cols(hidden[where, :], full[k, rank // 2, rank % 2])
 
     lag = levels - 1
 
@@ -770,47 +896,60 @@
         @pl.when(within(number - lag, count))
         def _():
             scatter.finish(number - lag)
-            mixed_out[span(number - lag, chunk), :] = lowered(scatter.total[...])
+            mixed[span(number - lag, chunk), :] = lowered(scatter.total[...])
+            early.start(number - lag)
+
+        @pl.when(number == levels)
+        def _():
+            loads.wait(3, 4)
 
         @pl.when(within(number - levels, count))
         def _():
             last(number - levels)
 
     in_order(count + levels, wave)
+    down_grad[...] = lowered(down_acc[...])
+    ends = Moves([(down_grad, down_grad_out), (dy_rows, dy_rows_out)], end_sems)
+    ends.start(0, 1)
     scatter.drain()
     gather.drain()
-
-    def stored(k):
-        for copy in stores(k):
-            copy.wait()
-
-    in_order(count, stored)
-
-
-def back_kernel(sizes, gate_grad, up_grad, gate_w, up_w, resid, dy_rows, gain, out_w, retained, swish, *refs):
-    sources, refs = refs[:4], refs[4:]
-    branch_out, swish_grad, retained_grad, gain_out, *refs = refs
-    targets, refs = refs[:4], refs[4:]
-    scatter_refs, refs = refs[:11], refs[11:]
+    store.wait(count)
+    ends.wait(0, 1)
+
+
+def back_kernel(sizes, bounds, rate, gain, *refs):
+    ins, refs = refs[:13], refs[13:]
+    mixed_src, down_src, *refs = refs
+    branch_out, swish_out, query_out, key_out, value_out, gain_out, *refs = refs
+    mixed_dst, down_dst, gate_dst, up_dst, *refs = refs
+    held, refs = refs[:13], refs[13:]
+    gate_grad, up_grad, gate_w, up_w, resid, dy_rows, normed_mid, out_w, retained, swish, *held_qkv = held
+    query, keys, values = held_qkv
+    scatter_refs, refs = refs[:10], refs[10:]
     full, *refs = refs
     gather_sems, refs = refs[:6], refs[6:]
     spread_sems, refs = refs[:3], refs[3:]
     swap_sems, refs = refs[:3], refs[3:]
-    (store_sem,) = refs
+    gate_total, up_total, swish_grad, delta, query_acc, key_acc, value_acc, refs = *refs[:7], refs[7:]
+    load_sems, chunk_sems, store_sems, end_sems = refs
     at = around(AXES)
     group, level, core = at
     count, levels, _, piece, width = full.shape
     chunk = 2 * levels * piece
+    loads = Moves(list(zip(ins, held)), load_sems)
+    loads.start(*range(13))
     greet(plane_peers(at, sizes) + column_peers(at, sizes))
-    spread = Spread(at, sizes, [(sources[0], targets[0], 0)], spread_sems)
-    swap = Swap(at, sizes, list(zip(sources[1:], targets[1:], (1, 0, 0))), swap_sems)
+    spread = Spread(at, sizes, [(mixed_src, mixed_dst, 0)], spread_sems)
+    swap = Swap(at, sizes, [(down_src, down_dst, 1), (gate_total, gate_dst, 0), (up_total, up_dst, 0)], swap_sems)
     spread.start(0)
-    for number in range(3):
-        swap.start(number)
-    part = scatter_refs[0]
-    scatter = Scatter(at, sizes, count, *scatter_refs[:5], scatter_refs[5:])
+    swap.start(0)
+    scatter = Scatter(at, sizes, count, scatter_refs)
     gather = Gather(at, sizes, count, full, gather_sems)
+    store = Chunks([(swish_grad, swish_out), (query, query_out)], chunk, chunk_sems)
     gain_out[...] = jnp.zeros(gain_out.shape, jnp.float32)
+    key_acc[...] = jnp.zeros(key_acc.shape, jnp.float32)
+    value_acc[...] = jnp.zeros(value_acc.shape, jnp.float32)
+    loads.wait(0, 1, 2, 3)
     tile = 512
 
     def stores(k):
@@ -819,18 +958,25 @@
             for c in range(2):
                 rows = pl.ds(pl.multiple_of(k * chunk + (2 * q + c) * piece, piece), piece)
                 copies.append(
-                    pltpu.make_async_copy(full.at[k, q, c], branch_out.at[rows], store_sem.at[2 * q + c, k])
+                    pltpu.make_async_copy(full.at[k, q, c], branch_out.at[rows], store_sems.at[2 * q + c, k])
                 )
         return copies
 
     def first(k):
+        scatter.free(k)
         where = span(k, chunk)
         for column in range(0, width, tile):
             columns = slice(column, column + tile)
             value = inner_rows(gate_grad[where, :], gate_w[columns, :])
             value += inner_rows(up_grad[where, :], up_w[columns, :])
-            part[k, :, :, :, columns] = lowered(value).reshape(levels, 2, piece, tile)
+            scatter.part[lax.rem(k, 2), :, :, :, columns] = lowered(value).reshape(levels, 2, piece, tile)
         scatter.start(k)
+
+    def weigh(k):
+        columns = span(k, chunk)
+        rows = normed_mid[:, columns]
+        gate_total[columns, :] = lowered(inner_cols(rows, gate_grad[...]))
+        up_total[columns, :] = lowered(inner_cols(rows, up_grad[...]))
 
     def norm(k):
         scatter.finish(k)
@@ -839,10 +985,10 @@
             sub = span(number, 16)
             where = pl.ds(pl.multiple_of(k * piece + number * 16, 16), 16)
             unit, scale = layer_norm(resid[where, :], EPSILON)
-            delta = scatter.total[sub, :]
-            outer = delta * unit
+            grad = scatter.total[sub, :]
+            outer = grad * unit
             gain_out[...] += outer[:8] + outer[8:]
-            value = wide(dy_rows[where, :]) + norm_back(delta * gain[...], unit, scale)
+            value = wide(dy_rows[where, :]) + norm_back(grad * gain[...], unit, scale)
             full[k, level, core, sub, :] = lowered(value)
             return carry
 
@@ -855,14 +1001,30 @@
             copy.start()
         rows = full[k].reshape(chunk, width)
         where = span(k, chunk)
-        delta = inner_rows(rows, out_w[...])
+        grad = inner_rows(rows, out_w[...])
         normed, scale = layer_norm(retained[where, :], GROUP_EPS)
         value = swish[where, :]
         gated = jax.nn.sigmoid(value)
-        swish_grad[where, :] = lowered(delta * normed * gated * (1.0 + value * (1.0 - gated)))
-        retained_grad[where, :] = lowered(norm_back(delta * value * gated, normed, scale))
+        swish_grad[where, :] = lowered(grad * normed * gated * (1.0 + value * (1.0 - gated)))
+        delta[...] = lowered(norm_back(grad * value * gated, normed, scale))
+        query_acc[...] = jnp.zeros(query_acc.shape, jnp.float32)
+
+        def block(j, carry):
+            there = span(j, chunk)
+            decay = decay_tile(k, j, chunk, bounds, rate)
+            weight = lowered(inner_rows(query[where, :], keys[there, :]) * decay)
+            score = lowered(inner_rows(delta[...], values[there, :]) * decay)
+            query_acc[...] += matmul(score, keys[there, :])
+            key_acc[there, :] += inner_cols(score, query[where, :])
+            value_acc[there, :] += inner_cols(weight, delta[...])
+            return carry
+
+        lax.fori_loop(0, k + 1, block, 0)
+        query[where, :] = lowered(query_acc[...])
+        store.start(k)
 
     lag = levels - 1
+    tiles = width // chunk
 
     def wave(number):
         @pl.when(number < count)
@@ -875,6 +1037,10 @@
             def _():
                 gather.hop(number - lag - hop, hop)
 
+        @pl.when(number == 2 * lag + 1)
+        def _():
+            loads.wait(7, 8, 9, 10, 11, 12)
+
         @pl.when(within(number - 2 * lag - 1, count))
         def _():
             last(number - 2 * lag - 1)
@@ -885,17 +1051,40 @@
 
         scatter.steps(number)
 
+        @pl.when(number == lag)
+        def _():
+            loads.wait(4, 5)
+
         @pl.when(within(number - lag, count))
         def _():
             norm(number - lag)
 
+        @pl.when(number == 0)
+        def _():
+            loads.wait(6)
+
+        @pl.when(number < tiles)
+        def _():
+            weigh(number)
+
+        @pl.when(number == tiles)
+        def _():
+            swap.start(1)
+            swap.start(2)
+
     in_order(count + 2 * lag + 1, wave)
+    keys[...] = lowered(key_acc[...])
+    values[...] = lowered(value_acc[...])
+    ends = Moves([(keys, key_out), (values, value_out)], end_sems)
+    ends.start(0, 1)
     spread.wait(0)
     for number in range(3):
         swap.wait(number)
     spread.drain(0)
     scatter.drain()
     gather.drain()
+    store.wait(count)
+    ends.wait(0, 1)
 
     def stored(k):
         for copy in stores(k):
@@ -904,29 +1093,36 @@
     in_order(count, stored)
 
 
-def close_kernel(sizes, gain, normed_in, *refs):
-    deltas, refs = refs[:4], refs[4:]
-    weights, refs = refs[:4], refs[4:]
-    number_of = len(SWAP_AXES)
-    sources, refs = refs[:number_of], refs[number_of:]
-    delta_out, sums_out, *refs = refs
-    targets, refs = refs[:number_of], refs[number_of:]
-    scatter_refs, refs = refs[:11], refs[11:]
+def close_kernel(sizes, gain, gain_two, *refs):
+    ins, refs = refs[:13], refs[13:]
+    grad_out, gains_out, *refs = refs
+    targets, refs = refs[:5], refs[5:]
+    held, refs = refs[:13], refs[13:]
+    deltas, weights = held[:4], held[4:8]
+    normed_in, branch, mixed_in, unit, scale = held[8:]
+    grads, refs = refs[:5], refs[5:]
+    scatter_refs, refs = refs[:10], refs[10:]
     swap_sems, refs = refs[:3], refs[3:]
-    sums, sums_sent, sums_got = refs
+    sums, line_one, share, packed, gains, gains_in, refs = *refs[:6], refs[6:]
+    load_sems, sums_sent, sums_got, gain_sent, gain_got, deal_sent, deal_got, deal_own = refs
     at = around(AXES)
     group, level, core = at
     place = 2 * level + core
-    part = scatter_refs[0]
-    count, levels, _, chunk, width = part.shape
-    ranks = 2 * levels
+    groups = sizes[0]
+    scatter = Scatter(at, sizes, sums.shape[1], scatter_refs)
+    _, levels, _, chunk, width = scatter.part.shape
+    count, ranks = sums.shape[1], 2 * levels
+    rows_all = count * chunk
+    loads = Moves(list(zip(ins, held)), load_sems)
+    loads.start(*range(13))
     greet(plane_peers(at, sizes) + column_all(at, sizes))
-    swap = Swap(at, sizes, [(s, t, a) for s, t, a in zip(sources, targets, SWAP_AXES)], swap_sems)
-    for number in range(number_of):
-        swap.start(number)
-    scatter = Scatter(at, sizes, count, *scatter_refs[:5], scatter_refs[5:])
+    swap = Swap(at, sizes, list(zip(grads, targets, SWAP_AXES)) + [(gains, gains_in, 1)], swap_sems)
+    line_one[...] = jnp.zeros(line_one.shape, jnp.float32)
+    loads.wait(*range(9))
+    mine = pl.ds(pl.multiple_of(place * width, width), width)
 
     def first(k):
+        scatter.free(k)
         where = span(k, chunk)
         rows = [d[where, :] for d in deltas]
         one = jnp.zeros((chunk, width), jnp.float32)
@@ -936,7 +1132,7 @@
             value = inner_rows(rows[0], weights[0][columns, :])
             for row, weight in zip(rows[1:], weights[1:]):
                 value += inner_rows(row, weight[columns, :])
-            part[k, rank // 2, rank % 2] = lowered(value)
+            scatter.part[lax.rem(k, 2), rank // 2, rank % 2] = lowered(value)
             one += value * gain[:, columns]
             two += value * wide(normed_in[where, columns])
         scatter.start(k)
@@ -953,72 +1149,151 @@
         ]
         line = lax.broadcasted_iota(jnp.int32, (8, chunk), 0)
         sums[place, k] = jnp.where(line == 0, flat[0], flat[1])
-
-    def sums_copy(k):
-        peer = lax.rem(place + k, ranks)
+        for j in range(1, ranks):
+            sums_copy(k, j, place).start()
+
+    def sums_copy(k, j, owner):
+        peer = lax.rem(place + j, ranks)
         return pltpu.make_async_remote_copy(
-            src_ref=sums.at[place],
-            dst_ref=sums.at[place],
-            send_sem=sums_sent.at[k - 1],
-            recv_sem=sums_got.at[k - 1],
+            src_ref=sums.at[owner, k],
+            dst_ref=sums.at[owner, k],
+            send_sem=sums_sent.at[j - 1, k],
+            recv_sem=sums_got.at[j - 1, k],
             device_id=(group, peer // 2, lax.rem(peer, 2)),
             device_id_type=MESH,
         )
 
-    def sums_landed(k):
-        peer = lax.rem(place + ranks - k, ranks)
+    def pack_copy(j, owner):
+        peer = lax.rem(place + j, ranks)
         return pltpu.make_async_remote_copy(
-            src_ref=sums.at[peer],
-            dst_ref=sums.at[peer],
-            send_sem=sums_sent.at[k - 1],
-            recv_sem=sums_got.at[k - 1],
+            src_ref=packed.at[owner],
+            dst_ref=packed.at[owner],
+            send_sem=gain_sent.at[j - 1],
+            recv_sem=gain_got.at[j - 1],
             device_id=(group, peer // 2, lax.rem(peer, 2)),
             device_id_type=MESH,
         )
 
+    def sender(j):
+        return lax.rem(place + ranks - j, ranks)
+
+    def deal(k, j, owner):
+        rows = pl.ds(pl.multiple_of(owner * rows_all + k * chunk, chunk), chunk)
+        return pltpu.make_async_remote_copy(
+            src_ref=share.at[span(k, chunk)],
+            dst_ref=grad_out.at[rows],
+            send_sem=deal_sent.at[j - 1, k],
+            recv_sem=deal_got.at[j - 1, k],
+            device_id=(lax.rem(group + j, groups), level, core),
+            device_id_type=MESH,
+        )
+
+    def deal_here(k):
+        rows = pl.ds(pl.multiple_of(group * rows_all + k * chunk, chunk), chunk)
+        return pltpu.make_async_copy(share.at[span(k, chunk)], grad_out.at[rows], deal_own.at[k])
+
+    def finish(k):
+        scatter.finish(k)
+        for j in range(1, ranks):
+            sums_copy(k, j, sender(j)).wait_recv()
+        line = lax.broadcasted_iota(jnp.int32, (8, 128), 0)
+        lane = lax.broadcasted_iota(jnp.int32, (8, 128), 1)
+        means = lax.dot_general(
+            jnp.sum(sums[:, k], 0),
+            jnp.where(line == lane, 1.0 / (ranks * width), 0.0),
+            (((0,), (0,)), ((), ())),
+            precision=lax.Precision.HIGHEST,
+            preferred_element_type=jnp.float32,
+        )
+        where = span(k, chunk)
+        value, normed = scatter.total[...], unit[where, :]
+        outer = value * normed
+        line_one[...] += jnp.sum(outer.reshape(chunk // 8, 8, width), 0)
+        back = value * gain[:, mine] - means[:, :1] - normed * means[:, 1:2]
+        share[where, :] = lowered(wide(branch[where, mine]) + scale[where, :1] * back)
+        deal_here(k).start()
+        for j in range(1, groups):
+            deal(k, j, group).start()
+
+    def weigh(number):
+        if number == 4:
+
+            def part(k):
+                columns = span(k, chunk)
+                grads[4][:, columns] = lowered(inner_cols(mixed_in[...], branch[:, columns]))
+        else:
+
+            def part(k):
+                columns = span(k, chunk)
+                grads[number][columns, :] = lowered(inner_cols(normed_in[:, columns], deltas[number][...]))
+
+        in_order(ranks * width // chunk, part)
+        swap.start(number)
+
     lag = levels - 1
 
     def wave(number):
         @pl.when(number < count)
         def _():
             first(number)
+
+        @pl.when(number == 0)
+        def _():
+            weigh(3)
+
+        for step, which in ((1, 2), (2, 0), (3, 1)):
+
+            @pl.when(number == step)
+            def _():
+                weigh(which)
+
+        @pl.when(number < count)
+        def _():
             scatter.join(number)
 
         scatter.steps(number)
 
-        @pl.when(number == count - 1)
-        def _():
-            for k in range(1, ranks):
-                sums_copy(k).start()
+        @pl.when(number == lag)
+        def _():
+            loads.wait(9, 10, 11, 12)
 
         @pl.when(within(number - lag, count))
         def _():
-            scatter.finish(number - lag)
-            delta_out[span(number - lag, chunk), :] = scatter.total[...]
+            finish(number - lag)
+
+        @pl.when(number == lag + 1)
+        def _():
+            weigh(4)
 
     in_order(count + lag, wave)
-    for k in range(1, ranks):
-        sums_landed(k).wait_recv()
-    sums_out[...] = jnp.sum(sums[...], 0)
-    for k in range(1, ranks):
-        sums_copy(k).wait_send()
-    for number in range(number_of):
+    total = jnp.sum(gain_two[...], 0, keepdims=True)
+    packed[place] = jnp.concatenate([total, jnp.sum(line_one[...], 0, keepdims=True)], axis=1)
+    for j in range(1, ranks):
+        pack_copy(j, place).start()
+    for j in range(1, ranks):
+        pack_copy(j, sender(j)).wait_recv()
+    everything = ranks * width
+    line = lax.broadcasted_iota(jnp.int32, (8, everything), 0)
+    two = sum(packed[rank, :, :everything] for rank in range(ranks))
+    one = jnp.concatenate([packed[rank, :, everything:] for rank in range(ranks)], axis=1)
+    gains[...] = jnp.where(line == 0, one, two)
+    swap.start(5)
+    for number in range(6):
         swap.wait(number)
+    gains_out[...] = jnp.sum(gains_in[...], 0)
+    for j in range(1, ranks):
+        pack_copy(j, place).wait_send()
     scatter.drain()
 
-
-def spread_kernel(sizes, number_of, axes, *refs):
-    sources, refs = refs[:number_of], refs[number_of:]
-    targets, sems = refs[:number_of], refs[number_of:]
-    at = around(AXES)
-    greet(plane_peers(at, sizes))
-    spread = Spread(at, sizes, list(zip(sources, targets, axes)), sems)
-    for number in range(number_of):
-        spread.start(number)
-    for number in range(number_of):
-        spread.wait(number)
-    for number in range(number_of):
-        spread.drain(number)
+    def drain(k):
+        deal_here(k).wait()
+        for j in range(1, groups):
+            deal(k, j, lax.rem(group + groups - j, groups)).wait_recv()
+            deal(k, j, group).wait_send()
+        for j in range(1, ranks):
+            sums_copy(k, j, place).wait_send()
+
+    in_order(count, drain)
 
 
 def column_all(at, sizes):
@@ -1037,7 +1312,11 @@
 
 
 def kernel_call(body, number, ins, outs, scratch):
-    places = {True: pl.BlockSpec(memory_space=pltpu.VMEM), False: pl.BlockSpec(memory_space=pl.ANY)}
+    places = {
+        "vmem": pl.BlockSpec(memory_space=pltpu.VMEM),
+        "smem": pl.BlockSpec(memory_space=pltpu.SMEM),
+        "any": pl.BlockSpec(memory_space=pl.ANY),
+    }
     return pl.pallas_call(
         body,
         out_shape=[shape for _, shape in outs],
@@ -1062,39 +1341,16 @@
     return struct((sizes[0],) + tuple(shape), whole.dtype)
 
 
-def spread_call(number, shards, axes, sizes):
-    count = len(shards)
-    return kernel_call(
-        functools.partial(spread_kernel, sizes, count, axes),
-        number,
-        [(False, s) for s in shards],
-        [(False, spread_shape(s, a, sizes)) for s, a in zip(shards, axes)],
-        Spread.scratch(count, sizes),
-    )
-
-
-def pick_rows(targets, carry, pieces):
-    count = pieces[0].shape[0]
-    inside = ((targets >= 0) & (targets < count))[:, None]
-    position = jnp.clip(targets, 0, count - 1)
-    return tuple(
-        (
-            jnp.where(inside, jnp.take(piece, position, axis=0), held)
-            for piece, held in zip(pieces, carry)
-        )
-    )
-
-
-def decay_block(start, seq_ids, log_decay, block, factor):
-    every = jnp.arange(seq_ids.shape[0], dtype=jnp.int32)
-    near = start + jnp.arange(block, dtype=jnp.int32)
-    distance = near[:, None] - every[None, :]
-    own = lax.dynamic_slice_in_dim(seq_ids, start, block)
-    valid = (distance >= 0) & (own[:, None] == seq_ids[None, :])
-    return (
-        jnp.where(valid, jnp.exp(jnp.maximum(distance, 0).astype(jnp.float32) * log_decay), 0.0)
-        * factor
-    )
+def anywhere(items):
+    return [("any", item) for item in items]
+
+
+def held_like(arrays):
+    return [VMEM(a.shape, a.dtype) for a in arrays]
+
+
+def pick(rows, whole):
+    return whole.at[rows].get(mode="promise_in_bounds")
 
 
 def shards(
@@ -1132,23 +1388,27 @@
     sizes = (lax.axis_size("dp"), lax.axis_size("heads"))
     ranks = sizes[1] * lax.axis_size("tensor")
     chunk = ranks * PIECE
-    chunks = rows_dev // chunk
+    count = rows_dev // chunk
     width = slice_width * ranks
-    query_s, key_s, value_s, swish_s, out_s, gate_s, up_s, down_s = (
-        lowered(w) for w in (w_query, w_key, w_value, w_swish, w_out, w_gate, w_up, w_down)
-    )
+    own = rows_dev // ranks
+    qk_dim, v_dim, ff_dim = w_query.shape[1], w_value.shape[1], w_gate.shape[1]
+    f32 = jnp.float32
+    masters = (w_query, w_key, w_value, w_swish, w_out, w_gate, w_up, w_down)
+    axes = (0, 0, 0, 0, 1, 0, 0, 1)
     gain_rows = jnp.pad(jnp.stack([gain_attn, gain_mlp]), ((0, 6), (0, 0)))
-    x_all, gains_all = spread_call(0, (tokens, gain_rows), (0, 0), sizes)
+    rounded = [struct(w.shape) for w in masters]
+    x_all, gains_all, *low = kernel_call(
+        functools.partial(deal_kernel, sizes),
+        0,
+        anywhere((tokens, gain_rows) + masters),
+        anywhere([spread_shape(tokens, 0, sizes), spread_shape(gain_rows, 0, sizes)] + rounded),
+        Spread.scratch(2, sizes) + held_like(masters) + held_like(rounded) + [DMA((8,)), DMA((8,))],
+    )
+    full_w = [spread_shape(w, a, sizes) for w, a in zip(low, axes)]
     gains_all = wide(lowered(gains_all.reshape(sizes[0], 8, -1)))
     wide_one = gains_all[:, 0].reshape(1, width)
     wide_two = gains_all[:, 1].reshape(1, width)
-    empty = jnp.zeros(tokens.shape, jnp.bfloat16)
-    (x_part,) = pick_rows(source, (empty,), (x_all,))
-    qk_dim, v_dim = w_query.shape[1], w_value.shape[1]
-    own = rows_dev // ranks
-    first_shards = (query_s, key_s, value_s, swish_s, out_s)
-    first_axes = (0, 0, 0, 0, 1)
-    full_shapes = [spread_shape(s, a, sizes) for s, a in zip(first_shards, first_axes)]
+    x_part = pick(source, x_all)
     (
         normed_in,
         query,
@@ -1166,197 +1426,212 @@
     ) = kernel_call(
         functools.partial(open_kernel, sizes),
         1,
-        [(False, x_part.reshape(chunks, chunk, slice_width)), (True, wide_one)]
-        + [(False, s) for s in first_shards],
-        [
-            (False, struct((rows_dev, width))),
-            (False, struct((rows_dev, qk_dim))),
-            (False, struct((rows_dev, qk_dim))),
-            (False, struct((rows_dev, v_dim))),
-            (False, struct((rows_dev, v_dim), jnp.float32)),
-        ]
-        + [(False, s) for s in full_shapes]
+        [("any", x_part.reshape(count, chunk, slice_width)), ("vmem", wide_one)] + anywhere(low[:5]),
+        anywhere(
+            [
+                struct((rows_dev, width)),
+                struct((rows_dev, qk_dim)),
+                struct((rows_dev, qk_dim)),
+                struct((rows_dev, v_dim)),
+                struct((rows_dev, v_dim), f32),
+            ]
+            + full_w[:5]
+        )
         + [
-            (True, struct((own, width))),
-            (True, struct((rows_dev, slice_width), jnp.float32)),
-            (True, struct((rows_dev, 128), jnp.float32)),
+            ("vmem", struct((own, width))),
+            ("vmem", struct((rows_dev, slice_width), f32)),
+            ("vmem", struct((rows_dev, 128), f32)),
         ],
-        Gather.scratch(chunks, sizes, (chunk, slice_width))
+        Gather.scratch(count, sizes, (chunk, slice_width))
         + Spread.scratch(5, sizes)
-        + [VMEM(s.shape, s.dtype) for s in full_shapes[:4]]
+        + held_like(full_w[:4])
         + [
             VMEM((rows_dev, width), jnp.bfloat16),
             VMEM((rows_dev, qk_dim), jnp.bfloat16),
             VMEM((rows_dev, qk_dim), jnp.bfloat16),
             VMEM((rows_dev, v_dim), jnp.bfloat16),
-            VMEM((rows_dev, v_dim), jnp.float32),
+            VMEM((rows_dev, v_dim), f32),
             DMA,
             DMA((4,)),
             DMA((4,)),
-            DMA((chunks,)),
+            DMA((count,)),
         ],
     )
-    log_decay = jnp.log1p(-jnp.exp2(-5.0 - place.astype(jnp.float32)))
-    score_factor = QK_DIM ** (-0.5)
-    blocks = rows_dev // QBLOCK
-
-    def forward_block(number):
-        start = number * QBLOCK
-        decay = decay_block(start, seq_ids, log_decay, QBLOCK, score_factor)
-        weight = (inner_rows(lax.dynamic_slice_in_dim(query, start, QBLOCK), keys) * decay).astype(
-            jnp.bfloat16
-        )
-        return product(weight, values)
-
-    retained = lax.map(forward_block, jnp.arange(blocks, dtype=jnp.int32)).reshape(
-        rows_dev, values.shape[1]
-    )
-    normed, _ = layer_norm(retained, GROUP_EPS)
-    mixed_in = (swish_in * jax.nn.sigmoid(swish_in) * normed).astype(jnp.bfloat16)
-    ff_dim = w_gate.shape[1]
-    middle_shards = (gate_s, up_s, down_s, cotangent)
-    middle_axes = (0, 0, 1, 0)
-    middle_shapes = [spread_shape(s, a, sizes) for s, a in zip(middle_shards, middle_axes)]
-    normed_mid, gate, up_proj, hidden, resid, gate_w, up_w, down_w, dy_all = kernel_call(
+    rate = jnp.log1p(-jnp.exp2(-5.0 - place.astype(f32))).reshape(1)
+    middle_ins = (query, keys, values, swish_in, out_w, x_rows)
+    normed_mid, gate, up_proj, hidden, resid, retained, mixed_in, gate_w, up_w, down_w, dy_all = kernel_call(
         functools.partial(middle_kernel, sizes),
         2,
-        [(True, mixed_in), (True, out_w), (True, x_rows), (True, wide_two)]
-        + [(False, s) for s in middle_shards],
-        [
-            (False, struct((rows_dev, width))),
-            (False, struct((rows_dev, ff_dim), jnp.float32)),
-            (False, struct((rows_dev, ff_dim), jnp.float32)),
-            (True, struct((rows_dev, ff_dim))),
-            (True, struct((own, width), jnp.float32)),
-        ]
-        + [(False, s) for s in middle_shapes],
-        Scatter.scratch(chunks, sizes, (PIECE, width))
-        + Gather.scratch(chunks, sizes, (PIECE, width))
+        [("smem", dealt_start), ("smem", rate), ("vmem", wide_two)]
+        + anywhere(middle_ins)
+        + anywhere(low[5:] + [cotangent]),
+        anywhere(
+            [
+                struct((rows_dev, width)),
+                struct((rows_dev, ff_dim), f32),
+                struct((rows_dev, ff_dim), f32),
+                struct((rows_dev, ff_dim)),
+                struct((own, width), f32),
+                struct((rows_dev, v_dim), f32),
+                struct((rows_dev, v_dim)),
+            ]
+            + full_w[5:]
+            + [spread_shape(cotangent, 0, sizes)]
+        ),
+        held_like(middle_ins)
+        + Scatter.scratch(count, sizes, (PIECE, width))
+        + Gather.scratch(count, sizes, (PIECE, width))
         + Spread.scratch(4, sizes)
+        + held_like(full_w[5:7])
         + [
-            VMEM(middle_shapes[0].shape, jnp.bfloat16),
-            VMEM(middle_shapes[1].shape, jnp.bfloat16),
-            VMEM((rows_dev, ff_dim), jnp.float32),
-            VMEM((rows_dev, ff_dim), jnp.float32),
-            DMA((2 + ranks, chunks)),
+            VMEM((rows_dev, ff_dim), f32),
+            VMEM((rows_dev, ff_dim), f32),
+            VMEM((rows_dev, ff_dim), jnp.bfloat16),
+            VMEM((own, width), f32),
+            VMEM((rows_dev, v_dim), f32),
+            VMEM((rows_dev, v_dim), jnp.bfloat16),
+            DMA((6,)),
+            DMA((5, count)),
+            DMA((ranks, count)),
+            DMA((2,)),
+            DMA,
+        ],
+    )
+    dy_part = pick(source, dy_all)
+    feed_ins = (hidden, down_w, resid, gate, up_proj)
+    mixed_share, delta_gate, delta_up, dy_rows, grad_down = kernel_call(
+        functools.partial(feed_kernel, sizes),
+        3,
+        anywhere((dy_part.reshape(count, chunk, slice_width),) + feed_ins),
+        anywhere(
+            [
+                struct((rows_dev, slice_width)),
+                struct((rows_dev, ff_dim)),
+                struct((rows_dev, ff_dim)),
+                struct((own, width)),
+                struct((ff_dim, width)),
+            ]
+        ),
+        held_like(feed_ins)
+        + Scatter.scratch(count, sizes, (chunk, slice_width))
+        + Gather.scratch(count, sizes, (chunk, slice_width))
+        + [
+            VMEM((chunk, slice_width), f32),
+            VMEM((ff_dim, width), f32),
+            VMEM((ff_dim, width), jnp.bfloat16),
+            VMEM((rows_dev, slice_width), jnp.bfloat16),
+            VMEM((rows_dev, ff_dim), jnp.bfloat16),
+            VMEM((rows_dev, ff_dim), jnp.bfloat16),
+            VMEM((own, width), jnp.bfloat16),
+            DMA,
+            DMA((5,)),
+            DMA((3, count)),
             DMA((2,)),
         ],
     )
-    (dy_part,) = pick_rows(source, (empty,), (dy_all,))
-    mixed_share, dy_full, delta_gate, delta_up, dy_rows = kernel_call(
-        functools.partial(feed_kernel, sizes),
-        3,
-        [
-            (False, dy_part.reshape(chunks, chunk, slice_width)),
-            (True, hidden),
-            (True, gate),
-            (True, up_proj),
-            (True, down_w),
-            (True, resid),
-        ],
-        [
-            (True, struct((rows_dev, slice_width))),
-            (False, struct((rows_dev, width))),
-            (True, struct((rows_dev, ff_dim))),
-            (True, struct((rows_dev, ff_dim))),
-            (True, struct((own, width))),
-        ],
-        Scatter.scratch(chunks, sizes, (chunk, slice_width))
-        + Gather.scratch(chunks, sizes, (chunk, slice_width))
-        + [VMEM((chunk, slice_width), jnp.float32), DMA, DMA((ranks, chunks))],
-    )
-    grad_down = lowered(inner_cols(hidden, dy_full))
-    grad_gate = lowered(inner_cols(normed_mid, delta_gate))
-    grad_up = lowered(inner_cols(normed_mid, delta_up))
-    back_swaps = ((grad_down, 1), (grad_gate, 0), (grad_up, 0))
-    delta_branch, delta_swish, delta_retained, gain_two_part, mixed_all, *ff_grads = kernel_call(
-        functools.partial(back_kernel, sizes),
-        4,
-        [
-            (True, delta_gate),
-            (True, delta_up),
-            (True, gate_w),
-            (True, up_w),
-            (True, resid),
-            (True, dy_rows),
-            (True, wide_two),
-            (True, out_w),
-            (True, retained),
-            (True, swish_in),
-            (False, mixed_share),
-        ]
-        + [(False, g) for g, _ in back_swaps],
-        [
-            (False, struct((rows_dev, width))),
-            (True, struct((rows_dev, v_dim))),
-            (True, struct((rows_dev, v_dim))),
-            (True, struct((8, width), jnp.float32)),
-            (False, spread_shape(mixed_share, 0, sizes)),
-        ]
-        + [(False, swap_shape(g, a, sizes)) for g, a in back_swaps],
-        Scatter.scratch(chunks, sizes, (PIECE, width))
-        + Gather.scratch(chunks, sizes, (PIECE, width))
-        + Spread.scratch(1, sizes)
-        + Swap.scratch(3, sizes)
-        + [DMA((ranks, chunks))],
-    )
-    grad_out = lowered(inner_cols(mixed_in, delta_branch))
-
-    def backward_block(carry, number):
-        delta_keys, delta_values = carry
-        start = number * QBLOCK
-        decay = decay_block(start, seq_ids, log_decay, QBLOCK, score_factor)
-        query_block = lax.dynamic_slice_in_dim(query, start, QBLOCK)
-        grad_block = lax.dynamic_slice_in_dim(delta_retained, start, QBLOCK)
-        weight = (inner_rows(query_block, keys) * decay).astype(jnp.bfloat16)
-        delta_score = (inner_rows(grad_block, values) * decay).astype(jnp.bfloat16)
-        delta_keys = delta_keys + inner_cols(delta_score, query_block)
-        delta_values = delta_values + inner_cols(weight, grad_block)
-        return ((delta_keys, delta_values), product(delta_score, keys))
-
-    start_carry = (jnp.zeros(keys.shape, jnp.float32), jnp.zeros(values.shape, jnp.float32))
-    (delta_keys, delta_values), delta_query = lax.scan(
-        backward_block, start_carry, jnp.arange(blocks, dtype=jnp.int32)
-    )
-    delta_query = delta_query.reshape(rows_dev, query.shape[1]).astype(jnp.bfloat16)
-    delta_keys = delta_keys.astype(jnp.bfloat16)
-    delta_values = delta_values.astype(jnp.bfloat16)
-    grad_query = lowered(inner_cols(normed_in, delta_query))
-    grad_key = lowered(inner_cols(normed_in, delta_keys))
-    grad_value = lowered(inner_cols(normed_in, delta_values))
-    grad_swish = lowered(inner_cols(normed_in, delta_swish))
-    close_swaps = tuple(zip((grad_query, grad_key, grad_value, grad_swish, grad_out), SWAP_AXES))
-    delta_in, sums, *attn_grads = kernel_call(
+    back_ins = (
+        delta_gate,
+        delta_up,
+        gate_w,
+        up_w,
+        resid,
+        dy_rows,
+        normed_mid,
+        out_w,
+        retained,
+        swish_in,
+        query,
+        keys,
+        values,
+    )
+    delta_branch, delta_swish, delta_query, delta_keys, delta_values, gain_two_part, mixed_all, *ff_grads = (
+        kernel_call(
+            functools.partial(back_kernel, sizes),
+            4,
+            [("smem", dealt_start), ("smem", rate), ("vmem", wide_two)]
+            + anywhere(back_ins)
+            + anywhere((mixed_share, grad_down)),
+            anywhere(
+                [
+                    struct((rows_dev, width)),
+                    struct((rows_dev, v_dim)),
+                    struct((rows_dev, qk_dim)),
+                    struct((rows_dev, qk_dim)),
+                    struct((rows_dev, v_dim)),
+                ]
+            )
+            + [("vmem", struct((8, width), f32))]
+            + anywhere(
+                [
+                    spread_shape(mixed_share, 0, sizes),
+                    swap_shape(full_w[7], 1, sizes),
+                    swap_shape(full_w[5], 0, sizes),
+                    swap_shape(full_w[6], 0, sizes),
+                ]
+            ),
+            held_like(back_ins)
+            + Scatter.scratch(count, sizes, (PIECE, width))
+            + Gather.scratch(count, sizes, (PIECE, width))
+            + Spread.scratch(1, sizes)
+            + Swap.scratch(3, sizes)
+            + held_like(full_w[5:7])
+            + [
+                VMEM((rows_dev, v_dim), jnp.bfloat16),
+                VMEM((chunk, v_dim), jnp.bfloat16),
+                VMEM((chunk, qk_dim), f32),
+                VMEM((rows_dev, qk_dim), f32),
+                VMEM((rows_dev, v_dim), f32),
+                DMA((13,)),
+                DMA((2, count)),
+                DMA((ranks, count)),
+                DMA((2,)),
+            ],
+        )
+    )
+    close_ins = (
+        delta_query,
+        delta_keys,
+        delta_values,
+        delta_swish,
+        query_w,
+        key_w,
+        value_w,
+        swish_w,
+        normed_in,
+        delta_branch,
+        mixed_in,
+        unit_share,
+        scale_one,
+    )
+    swaps = len(SWAP_AXES)
+    grad_all, gains, *attn_grads = kernel_call(
         functools.partial(close_kernel, sizes),
         5,
-        [(True, wide_one), (True, normed_in)]
-        + [(True, d) for d in (delta_query, delta_keys, delta_values, delta_swish)]
-        + [(True, w) for w in (query_w, key_w, value_w, swish_w)]
-        + [(False, g) for g, _ in close_swaps],
-        [
-            (True, struct((rows_dev, slice_width), jnp.float32)),
-            (True, struct((chunks, 8, chunk), jnp.float32)),
-        ]
-        + [(False, swap_shape(g, a, sizes)) for g, a in close_swaps],
-        Scatter.scratch(chunks, sizes, (chunk, slice_width))
-        + Swap.scratch(len(SWAP_AXES), sizes)
-        + [VMEM((ranks, chunks, 8, chunk), jnp.float32), DMA((ranks - 1,)), DMA((ranks - 1,))],
-    )
-    col_start = place * slice_width
-    mean_one = sums[:, 0].reshape(rows_dev, 1) / width
-    mean_two = sums[:, 1].reshape(rows_dev, 1) / width
-    gain_share = lax.dynamic_slice_in_dim(wide_one, col_start, slice_width, 1)
-    resid_share = wide(lax.dynamic_slice_in_dim(delta_branch, col_start, slice_width, 1))
-    grad_share = lowered(
-        resid_share + scale_one[:, :1] * (delta_in * gain_share - mean_one - unit_share * mean_two)
-    )
-    gain_one_part = lax.dynamic_update_slice_in_dim(
-        jnp.zeros((width,), jnp.float32), jnp.sum(delta_in * unit_share, 0), col_start, 0
-    )
-    gains = lax.psum(jnp.stack([gain_one_part, jnp.sum(gain_two_part, 0)]), AXES)
-    gain_width = gain_attn.shape[0]
-    gains = lax.dynamic_slice_in_dim(gains, group * gain_width, gain_width, 1)
-    (grad_all,) = spread_call(6, (grad_share,), (0,), sizes)
+        [("vmem", wide_one), ("vmem", gain_two_part)] + anywhere(close_ins),
+        anywhere([struct((sizes[0] * rows_dev, slice_width))])
+        + [("vmem", struct((8, gain_attn.shape[0]), f32))]
+        + anywhere([swap_shape(w, a, sizes) for w, a in zip(full_w[:5], SWAP_AXES)]),
+        held_like(close_ins)
+        + held_like(full_w[:5])
+        + Scatter.scratch(count, sizes, (chunk, slice_width))
+        + Swap.scratch(swaps + 1, sizes)
+        + [
+            VMEM((ranks, count, 8, chunk), f32),
+            VMEM((8, slice_width), f32),
+            VMEM((rows_dev, slice_width), jnp.bfloat16),
+            VMEM((ranks, 1, width + slice_width), f32),
+            VMEM((8, width), f32),
+            VMEM((sizes[0], 8, gain_attn.shape[0]), f32),
+            DMA((len(close_ins),)),
+            DMA((ranks - 1, count)),
+            DMA((ranks - 1, count)),
+            DMA((ranks - 1,)),
+            DMA((ranks - 1,)),
+            DMA((sizes[0] - 1, count)),
+            DMA((sizes[0] - 1, count)),
+            DMA((count,)),
+        ],
+    )
     grads = [jnp.sum(wide(g), 0) for g in attn_grads + ff_grads[1:] + ff_grads[:1]]
     slot_match = dealing[:, None] == ident[None, :]
     slot_len = jnp.sum(jnp.where(slot_match, lengths[None, :], 0), 1)
@@ -1371,7 +1646,7 @@
         jnp.sum(jnp.where(seq_of[:, None] == ident[None, :], owner_base[None, :], 0), 1)
         + global_rows
     )
-    mixed_rows, grad_rows = pick_rows(targets, (empty, empty), (mixed_all, grad_all))
+    mixed_rows, grad_rows = pick(targets, mixed_all), pick(targets, grad_all)
     return (
         mixed_rows,
         grad_rows,

time: 837 us -> 688 us (0.82); the launches traced: 828 us -> 688 us
  matrix products: 95.4 us -> 0 us
  blocking collectives: 38.9 us -> 0 us
  Pallas kernels: 613 us -> 641 us
  other arithmetic: 39.9 us -> 17 us
    dot_general x23 -> x0, matrix products: 95.4 us -> none  [the longest x14 71.7 us: inner_cols(): lax.dot_general(left, right, (((0,), (0,)), ((), ())), preferred_element_...]
    psum x1 -> x0, blocking collectives: 38.9 us -> none  [shards(): lax.psum(jnp.stack([gain_one_part, jnp.sum(gain_two_part, 0)]), AXES)]
    pallas_call x7 -> x6, Pallas kernels: 613 us -> 641 us  [kernel_call(): pl.pallas_call(body, out_shape=[shape for _, shape in outs], in_specs=[pl...]
    convert_element_type x11 -> x0, other arithmetic: 12.6 us -> none  [the longest x8 6.62 us: lowered(): return value.astype(jnp.bfloat16)]
where the time goes in v2:
time: 688 us
  Pallas kernels  641 us (93%)
  local copies, waits for them, and re-layouts  28.9 us (4%)
  other arithmetic  17 us (2%)
    pallas_call x6, Pallas kernels, kernel_call(): pl.pallas_call(body, out_shape=[shape for _, shape in outs], in_specs=[pl...  641 us
    gather x4, local copies, waits for them, and re-layouts, pick(): return whole.at[rows].get(mode='promise_in_bounds')  26 us

profile of v2, /device:TPU:0, one launch (start us, length us, event | category | flops | bytes accessed | tf_op | source)
XLA Modules:
  0.0 687.8 jit_solution(4210653301775469775)
XLA Ops:
  0.6 0.7 dynamic_slice.3
  1.4 0.8 reduce-window.17
  2.2 0.7 bitcast_subtract_fusion
  2.9 0.9 select_reduce_fusion.5
  3.7 0.2 reduce-window.16
  3.9 0.0 copy-start.6
  3.9 0.1 convert_reduce_fusion.9
  4.0 0.1 select_reduce_fusion.1
  4.2 1.3 select_maximum_fusion.gains
  5.5 39.9 %shard_map.229 = (bf16[6144,256]{1,0:T(8,128)(2,1)}, f32[32,512]{1,0:T(8,128)}, bf16[512,256]{1,0:T(8,128)(2,1)}, bf16[512,256]{1,0:T(8,128)(2,1)}, bf16[512,512...) custom-call(bf16[1536,256]{1,0:T(8,128)(2,1)} %tokens.1, ...), custom_call_target="tpu_custom_call" | custom-call | tf_op jit(solution)/shard_map/pallas_call | solution.py:1320
  45.4 0.0 copy-done.6
  45.4 0.0 copy-start.5
  45.4 6.8 gather_fusion
  52.3 0.0 copy-done.5
  52.3 0.6 fusion.6
  52.9 100.1 %shard_map.230 = (bf16[1536,2048]{1,0:T(8,128)(2,1)}, bf16[1536,256]{1,0:T(8,128)(2,1)}, bf16[1536,256]{1,0:T(8,128)(2,1)}, bf16[1536,512]{1,0:T(8,128)(2,1)}, f...) custom-call(bf16[6,256,256]{2,1,0:T(8,128)(2,1)} %bitcast.20, ...), custom_call_target="tpu_custom_call" | custom-call | tf_op jit(solution)/shard_map/pallas_call | solution.py:1320
  153.1 119.5 %shard_map.231 = (bf16[1536,2048]{1,0:T(8,128)(2,1)}, f32[1536,512]{1,0:T(8,128)}, f32[1536,512]{1,0:T(8,128)}, bf16[1536,512]{1,0:T(8,128)(2,1)}, f32[192,2048]...) custom-call(s32[3]{0:T(128)} %copy-done.6, ...), custom_call_target="tpu_custom_call" | custom-call | tf_op jit(solution)/shard_map/pallas_call | solution.py:1320
  272.5 6.8 gather_fusion.1
  279.4 88.9 %shard_map.232 = (bf16[1536,256]{1,0:T(8,128)(2,1)}, bf16[1536,512]{1,0:T(8,128)(2,1)}, bf16[1536,512]{1,0:T(8,128)(2,1)}, bf16[192,2048]{1,0:T(8,128)(2,1)}, bf16[512,2048]{1,0:T(8,128)(2,1)}) custom-call(bf16[6,256,256]{2,1,0:T(8,128)(2,1)} %bitcast.19, bf16[1536,512]{1,0:T(8,128)(2,1)} %get-tuple-element.85.refs_0_, ...), custom_call_target="tpu_custom_call" | custom-call | tf_op jit(solution)/shard_map/pallas_call | solution.py:1320
  368.3 150.0 %shard_map.233 = (bf16[1536,2048]{1,0:T(8,128)(2,1)}, bf16[1536,512]{1,0:T(8,128)(2,1)}, bf16[1536,256]{1,0:T(8,128)(2,1)}, bf16[1536,256]{1,0:T(8,128)(2,1)}, b...) custom-call(s32[3]{0:T(128)} %copy-done.6, ...), custom_call_target="tpu_custom_call" | custom-call | tf_op jit(solution)/shard_map/pallas_call | solution.py:1320
  518.3 4.4 convert_reduce_fusion
  522.7 142.7 %shard_map.234 = (bf16[6144,256]{1,0:T(8,128)(2,1)}, f32[8,512]{1,0:T(8,128)}, bf16[4,512,256]{2,1,0:T(8,128)(2,1)}, bf16[4,512,256]{2,1,0:T(8,128)(2,1)}, bf16[...) custom-call(f32[1,2048]{1,0:T(1,128)} %bitcast.22, ...), custom_call_target="tpu_custom_call" | custom-call | tf_op jit(solution)/shard_map/pallas_call | solution.py:1320
  665.4 0.0 copy-start.1
  665.4 0.0 copy-start.2
  665.4 4.6 convert_reduce_fusion.3
  669.9 0.0 copy-done.1
  669.9 0.0 copy-done.2
  669.9 0.0 copy-start.3
  670.0 0.0 copy-start.4
  670.0 1.9 convert_reduce_fusion.2
  671.9 0.0 copy-start.7
  671.9 0.0 copy-done.3
  671.9 0.0 copy-done.4
  671.9 1.3 convert_reduce_fusion.6
  673.2 0.0 copy-done.7
  673.2 0.0 copy-done.8
  673.2 0.2 select_reduce_fusion.4
  673.3 0.1 reshape.188
  673.4 0.2 reduce_window_sum.27
  673.6 0.1 reduce_window_sum.28
  673.7 0.1 select_reduce_fusion.2
  673.8 0.1 convert_reduce_fusion.8
  674.0 0.1 select_reduce_fusion
  674.1 0.0 copy-start
  674.1 7.0 %gather_fusion.3 = bf16[1536,256]{1,0:T(8,128)(2,1)} fusion(bf16[6144,256]{1,0:T(8,128)(2,1)} %get-tuple-element.114, s32[2048]{0:T(1024)S(1)} %pad_clamp_fusion), kind=kCustom, calls=%fused_computation.3 | custom fusion | bytes 1579008 | tf_op jit(solution)/shard_map/gather | solution.py:1353
  681.1 1.4 fusion.7
  682.5 0.0 copy-done
  682.5 5.4 gather_fusion.2
  (11 shorter events, 0.1 us)
Async XLA Ops:
  3.9 41.5 %copy-start.6 = (s32[3]{0:T(128)}, s32[3]{0:T(128)S(1)}, u32[]{:S(2)}) copy-start(s32[3]{0:T(128)S(1)} %get-tuple-element.129.bounds) | copy-start | bytes 40
  45.4 6.9 copy-start.5
  665.4 4.6 copy-start.1
  665.4 4.6 copy-start.2
  669.9 1.9 copy-start.3
  670.0 1.9 copy-start.4
  671.9 1.3 copy-start.7
  671.9 1.3 copy-start.8
  674.1 8.4 %copy-start = (bf16[6144,256]{1,0:T(8,128)(2,1)S(1)}, bf16[6144,256]{1,0:T(8,128)(2,1)}, u32[]{:S(2)}) copy-start(bf16[6144,256]{1,0:T(8,128)(2,1)} %get-tuple-element.99) | copy-start | bytes 9437188

commit v3 on v2

--- a/solution.py
+++ b/solution.py
@@ -84,64 +84,116 @@
     ]
 
 
+def beside(group):
+    return group + 1 - 2 * lax.rem(group, 2), lax.rem(group + 2, 4), 3 - group
+
+
 class Spread:
-    def __init__(self, at, sizes, items, sems):
+    def __init__(self, at, sizes, items, sems, relay=True):
         self.at, self.count, self.items = at, sizes[0], items
         self.local, self.sent, self.got = sems
+        self.plane = relay and sizes[0] == 4
 
     @staticmethod
     def scratch(items, sizes):
+        ways = max(4, sizes[0] - 1)
         return [
             pltpu.SemaphoreType.DMA((items,)),
-            pltpu.SemaphoreType.DMA((items, sizes[0] - 1)),
-            pltpu.SemaphoreType.DMA((items, sizes[0] - 1)),
+            pltpu.SemaphoreType.DMA((items, ways)),
+            pltpu.SemaphoreType.DMA((items, ways)),
         ]
 
-    def place(self, number, owner):
-        source, target, axis = self.items[number]
+    def place(self, number, owner, half=None):
+        source, target, axis, *where = self.items[number]
+        rows, columns = source.shape
         size = source.shape[axis]
-        span = pl.ds(pl.multiple_of(owner * size, size), size)
-        return target.at[span] if axis == 0 else target.at[:, span]
+        step, offset = where or (size, 0)
+        start = owner * step + offset
+        if half is None:
+            begin, height = 0, rows
+        else:
+            begin, height = half * (rows // 2), rows // 2
+        if axis == 0:
+            return target.at[pl.ds(pl.multiple_of(start + begin, height), height)]
+        return target.at[pl.ds(begin, height), pl.ds(pl.multiple_of(start, size), size)]
 
     def own(self, number):
         return pltpu.make_async_copy(
             self.items[number][0], self.place(number, self.at[0]), self.local.at[number]
         )
 
+    def copy(self, number, source, place, way, peer):
+        return pltpu.make_async_remote_copy(
+            src_ref=source,
+            dst_ref=place,
+            send_sem=self.sent.at[number, way],
+            recv_sem=self.got.at[number, way],
+            device_id=(peer,) + self.at[1:],
+            device_id_type=MESH,
+        )
+
     def away(self, number, k):
-        return pltpu.make_async_remote_copy(
-            src_ref=self.items[number][0],
-            dst_ref=self.place(number, self.at[0]),
-            send_sem=self.sent.at[number, k - 1],
-            recv_sem=self.got.at[number, k - 1],
-            device_id=(lax.rem(self.at[0] + k, self.count),) + self.at[1:],
-            device_id_type=MESH,
-        )
+        peer = lax.rem(self.at[0] + k, self.count)
+        return self.copy(number, self.items[number][0], self.place(number, self.at[0]), k - 1, peer)
 
     def landed(self, number, k):
         owner = lax.rem(self.at[0] + self.count - k, self.count)
-        return pltpu.make_async_remote_copy(
-            src_ref=self.items[number][0],
-            dst_ref=self.place(number, owner),
-            send_sem=self.sent.at[number, k - 1],
-            recv_sem=self.got.at[number, k - 1],
-            device_id=(owner,) + self.at[1:],
-            device_id_type=MESH,
-        )
-
-    def start(self, number):
-        self.own(number).start()
-        for k in range(1, self.count):
-            self.away(number, k).start()
-
-    def wait(self, number):
-        self.own(number).wait()
-        for k in range(1, self.count):
-            self.landed(number, k).wait_recv()
-
-    def drain(self, number):
-        for k in range(1, self.count):
-            self.away(number, k).wait_send()
+        return self.copy(number, self.items[number][0], self.place(number, owner), k - 1, owner)
+
+    def to(self, number, way):
+        peer = beside(self.at[0])[way]
+        return self.copy(number, self.items[number][0], self.place(number, self.at[0]), way, peer)
+
+    def of(self, number, way):
+        peer = beside(self.at[0])[way]
+        return self.copy(number, self.items[number][0], self.place(number, peer), way, peer)
+
+    def on(self, number, way):
+        near = beside(self.at[0])
+        ref = self.place(number, near[way], way)
+        return self.copy(number, ref, ref, 2 + way, near[1 - way])
+
+    def last(self, number, way):
+        near = beside(self.at[0])
+        ref = self.place(number, near[2], way)
+        return self.copy(number, ref, ref, 2 + way, near[1 - way])
+
+    def start(self, *numbers):
+        for number in numbers:
+            if self.plane:
+                self.to(number, 0).start()
+                self.to(number, 1).start()
+            else:
+                for k in range(1, self.count):
+                    self.away(number, k).start()
+            self.own(number).start()
+
+    def relay(self, *numbers):
+        if self.plane:
+            for number in numbers:
+                for way in range(2):
+                    self.of(number, way).wait_recv()
+                    self.on(number, way).start()
+
+    def wait(self, *numbers):
+        for number in numbers:
+            self.own(number).wait()
+            if self.plane:
+                self.last(number, 0).wait_recv()
+                self.last(number, 1).wait_recv()
+            else:
+                for k in range(1, self.count):
+                    self.landed(number, k).wait_recv()
+
+    def drain(self, *numbers):
+        for number in numbers:
+            if self.plane:
+                for way in range(2):
+                    self.to(number, way).wait_send()
+                    self.on(number, way).wait_send()
+            else:
+                for k in range(1, self.count):
+                    self.away(number, k).wait_send()
 
 
 class Gather:
@@ -370,13 +422,17 @@
         above = wave - level
         below = wave - (self.levels - 1 - level)
 
-        @pl.when(within(above, self.count))
+        @pl.when(within(above, self.count) & (level < self.levels // 2))
         def _():
             self.step_up(above)
 
         @pl.when(within(below, self.count))
         def _():
             self.step_down(below)
+
+        @pl.when(within(above, self.count) & (level >= self.levels // 2))
+        def _():
+            self.step_up(above)
 
     def finish(self, k):
         level = self.at[1]
@@ -482,17 +538,48 @@
 
 
 class Swap:
-    def __init__(self, at, sizes, items, sems):
+    def __init__(self, at, sizes, items, sems, halves=None):
         self.at, self.count, self.items = at, sizes[0], items
         self.local, self.sent, self.got = sems
-
-    scratch = Spread.scratch
-
-    def block(self, number, owner):
+        self.halves = halves
+        self.plane = halves is not None and sizes[0] == 4
+
+    @staticmethod
+    def scratch(items, sizes):
+        ways = max(6, sizes[0] - 1)
+        return [
+            pltpu.SemaphoreType.DMA((items,)),
+            pltpu.SemaphoreType.DMA((items, ways)),
+            pltpu.SemaphoreType.DMA((items, ways)),
+        ]
+
+    def block(self, number, owner, half=None):
         source, target, axis = self.items[number]
+        rows, columns = source.shape
         size = source.shape[axis] // self.count
-        window = pl.ds(pl.multiple_of(owner * size, size), size)
-        return source.at[window] if axis == 0 else source.at[:, window]
+        height = size if axis == 0 else rows
+        begin = 0
+        if half is not None:
+            height //= 2
+            begin = half * height
+        if axis == 0:
+            return source.at[pl.ds(pl.multiple_of(owner * size + begin, height), height)]
+        return source.at[pl.ds(begin, height), pl.ds(pl.multiple_of(owner * size, size), size)]
+
+    def half(self, number, slot, half):
+        target = self.items[number][1]
+        height = target.shape[1] // 2
+        return target.at[slot, pl.ds(half * height, height)]
+
+    def copy(self, number, source, place, way, peer):
+        return pltpu.make_async_remote_copy(
+            src_ref=source,
+            dst_ref=place,
+            send_sem=self.sent.at[number, way],
+            recv_sem=self.got.at[number, way],
+            device_id=(peer,) + self.at[1:],
+            device_id_type=MESH,
+        )
 
     def own(self, number):
         return pltpu.make_async_copy(
@@ -501,24 +588,74 @@
 
     def away(self, number, k):
         peer = lax.rem(self.at[0] + k, self.count)
-        return pltpu.make_async_remote_copy(
-            src_ref=self.block(number, peer),
-            dst_ref=self.items[number][1].at[k],
-            send_sem=self.sent.at[number, k - 1],
-            recv_sem=self.got.at[number, k - 1],
-            device_id=(peer,) + self.at[1:],
-            device_id_type=MESH,
-        )
-
-    def start(self, number):
-        self.own(number).start()
-        for k in range(1, self.count):
-            self.away(number, k).start()
-
-    def wait(self, number):
-        self.own(number).wait()
-        for k in range(1, self.count):
-            self.away(number, k).wait()
+        return self.copy(number, self.block(number, peer), self.items[number][1].at[k], k - 1, peer)
+
+    def across(self, number, way):
+        near = beside(self.at[0])
+        return self.copy(
+            number, self.block(number, near[2], way), self.halves[number].at[way], way, near[way]
+        )
+
+    def direct(self, number, way):
+        near = beside(self.at[0])
+        return self.copy(
+            number, self.block(number, near[way], way), self.half(number, 1 + way, way), 2 + way, near[way]
+        )
+
+    def added(self, number, way):
+        peer = beside(self.at[0])[1 - way]
+        return self.copy(
+            number, self.block(number, peer, way), self.half(number, 2 - way, way), 4 + way, peer
+        )
+
+    def start(self, *numbers):
+        for number in numbers:
+            if self.plane:
+                for way in range(2):
+                    self.across(number, way).start()
+                for way in range(2):
+                    self.direct(number, way).start()
+            else:
+                for k in range(1, self.count):
+                    self.away(number, k).start()
+            self.own(number).start()
+
+    def relay(self, *numbers):
+        if self.plane:
+            near = beside(self.at[0])
+            for number in numbers:
+                for way in range(2):
+                    self.across(number, way).wait_recv()
+                    part = self.block(number, near[1 - way], way)
+                    part[...] = lowered(wide(part[...]) + wide(self.halves[number][way]))
+                    self.added(number, way).start()
+
+    def wait(self, *numbers):
+        for number in numbers:
+            self.own(number).wait()
+            if self.plane:
+                for way in range(2):
+                    self.across(number, way).wait_send()
+                    self.direct(number, way).wait()
+                    self.added(number, way).wait()
+            else:
+                for k in range(1, self.count):
+                    self.away(number, k).wait()
+
+
+def half_blocks(items, sizes):
+    room = []
+    for whole, axis in items:
+        shape = list(whole.shape)
+        shape[axis] //= sizes[0]
+        room.append(pltpu.VMEM((2, shape[0] // 2, shape[1]), jnp.bfloat16))
+    return room
+
+
+def quarters(source, target):
+    rows = source.shape[0]
+    run = rows // 4
+    return [(source.at[pl.ds(k * run, run)], target, 0, rows, k * run) for k in range(4)]
 
 
 def deal_kernel(sizes, tokens, gains, *refs):
@@ -526,17 +663,20 @@
     tokens_out, gains_out, *refs = refs
     rounded_out, refs = refs[:8], refs[8:]
     spread_sems, refs = refs[:3], refs[3:]
+    small_sems, refs = refs[:3], refs[3:]
     held, refs = refs[:8], refs[8:]
     rounded, refs = refs[:8], refs[8:]
-    load_sems, store_sems = refs
+    load_sems, store_sems, tokens_held, gains_held = refs
     at = around(AXES)
-    loads = Moves(list(zip(masters, held)), load_sems)
+    loads = Moves(list(zip(masters, held)) + [(tokens, tokens_held), (gains, gains_held)], load_sems)
     stores = Moves(list(zip(rounded, rounded_out)), store_sems)
-    loads.start(*range(8))
+    loads.start(8, 9, *range(8))
     greet(plane_peers(at, sizes))
-    spread = Spread(at, sizes, [(tokens, tokens_out, 0), (gains, gains_out, 0)], spread_sems)
-    spread.start(0)
-    spread.start(1)
+    loads.wait(8, 9)
+    spread = Spread(at, sizes, quarters(tokens_held, tokens_out), spread_sems)
+    small = Spread(at, sizes, [(gains_held, gains_out, 0)], small_sems, relay=False)
+    spread.start(*range(4))
+    small.start(0)
     for number in range(8):
         loads.wait(number)
 
@@ -546,11 +686,13 @@
 
         in_order(held[number].shape[0] // 32, block)
         stores.start(number)
+    for number in range(4):
+        spread.relay(number)
     stores.wait(*range(8))
-    spread.wait(0)
-    spread.wait(1)
-    spread.drain(0)
-    spread.drain(1)
+    small.wait(0)
+    spread.wait(*range(4))
+    small.drain(0)
+    spread.drain(*range(4))
 
 
 def open_kernel(sizes, shards, gain, *refs):
@@ -563,7 +705,7 @@
     gather_sems, refs = refs[:6], refs[6:]
     spread_sems, refs = refs[:3], refs[3:]
     weights, refs = refs[:4], refs[4:]
-    normed, query, keys, values, swish, load_sem, out_sem, weight_sem, normed_sem = refs
+    normed, query, keys, values, swish, load_sem, out_sem, weight_sem, normed_sem, shard = refs
     at = around(AXES)
     group, level, core = at
     place = 2 * level + core
@@ -571,14 +713,16 @@
     ranks = 2 * levels
     load = pltpu.make_async_copy(x_part, full.at[:, level, core], load_sem)
     load.start()
+    load_shard = pltpu.make_async_copy(sources[4], shard, weight_sem.at[4])
+    load_shard.start()
     greet(plane_peers(at, sizes) + column_peers(at, sizes))
-    items = [(s, t, 0) for s, t in zip(sources[:4], weights)] + [(sources[4], weight_outs[4], 1)]
+    items = [(s, t, 0) for s, t in zip(sources[:4], weights)] + [(shard, weight_outs[4], 1)]
     spread = Spread(at, sizes, items, spread_sems)
     gather = Gather(at, sizes, count, full, gather_sems)
     load.wait()
     gather.start(0)
-    for number in range(5):
-        spread.start(number)
+    load_shard.wait()
+    spread.start(0, 1, 2)
     piece = chunk // ranks
 
     def norm(k):
@@ -610,18 +754,27 @@
         def _():
             gather.start(number + 1)
 
-        for hop in range(1, levels):
+        for hop in range(levels - 1, 0, -1):
 
             @pl.when(within(number - hop, count))
             def _():
                 gather.hop(number - hop, hop)
 
+        for step, relayed, started in ((1, 0, None), (2, 1, 3), (4, 2, 4), (7, 3, None)):
+
+            @pl.when(number == step)
+            def _():
+                spread.relay(relayed)
+                if started is not None:
+                    spread.start(started)
+
         @pl.when(within(number - levels, count))
         def _():
             gather.ready(number - levels)
             norm(number - levels)
 
     in_order(count + levels, wave)
+    spread.relay(4)
     outs = [(query, query_out), (keys, key_out), (values, value_out), (swish, swish_out)]
     for number, (held, out) in enumerate(outs):
         spread.wait(number)
@@ -637,8 +790,7 @@
     for number, (held, out) in enumerate(outs):
         pltpu.make_async_copy(held, out, out_sem.at[number]).wait()
         pltpu.make_async_copy(weights[number], weight_outs[number], weight_sem.at[number]).wait()
-    for number in range(5):
-        spread.drain(number)
+    spread.drain(*range(5))
     gather.drain()
 
     def stored(k):
@@ -661,13 +813,13 @@
     gather_sems, refs = refs[:6], refs[6:]
     spread_sems, refs = refs[:3], refs[3:]
     gate_w, up_w, gate, up, hidden, resid, retained, mixed_in, refs = *refs[:8], refs[8:]
-    load_sems, chunk_sems, normed_sems, weight_sems, resid_sem = refs
+    load_sems, chunk_sems, normed_sems, weight_sems, resid_sem, down_shard, dy_shard = refs
     at = around(AXES)
     group, level, core = at
     count, levels, _, piece, width = full.shape
     chunk = 2 * levels * piece
-    loads = Moves(list(zip(ins, held)), load_sems)
-    loads.start(*range(6))
+    loads = Moves(list(zip(ins, held)) + [(sources[2], down_shard), (sources[3], dy_shard)], load_sems)
+    loads.start(6, 7, *range(6))
     greet(plane_peers(at, sizes) + column_peers(at, sizes))
     spread = Spread(
         at,
@@ -675,13 +827,13 @@
         [
             (sources[0], gate_w, 0),
             (sources[1], up_w, 0),
-            (sources[2], down_w_out, 1),
-            (sources[3], dy_out, 0),
-        ],
+            (down_shard, down_w_out, 1),
+        ]
+        + quarters(dy_shard, dy_out),
         spread_sems,
     )
-    for number in range(4):
-        spread.start(number)
+    loads.wait(6, 7)
+    spread.start(0, 1)
     scatter = Scatter(at, sizes, count, scatter_refs)
     gather = Gather(at, sizes, count, full, gather_sems)
     weights = Moves([(gate_w, gate_w_out), (up_w, up_w_out)], weight_sems)
@@ -751,46 +903,58 @@
         hidden[where, :] = lowered(jax.nn.gelu(gate[where, :]) * up[where, :])
         late.start(k)
 
-    lag = levels - 1
+    lag = levels
 
     def wave(number):
         @pl.when(number < count)
         def _():
             first(number)
 
-        for hop in range(1, levels):
+        for hop in range(levels - 1, 0, -1):
 
             @pl.when(within(number - lag - hop, count))
             def _():
                 gather.hop(number - lag - hop, hop)
 
-        @pl.when(number == 2 * lag + 1)
-        def _():
-            spread.wait(0)
-            spread.wait(1)
+        @pl.when(within(number - lag, count))
+        def _():
+            norm(number - lag)
+
+        @pl.when(within(number - 1, count))
+        def _():
+            scatter.join(number - 1)
+
+        scatter.steps(number - 1)
+
+        for step, relayed, started in (
+            (2, (0,), (2,)),
+            (4, (1,), (3, 4)),
+            (6, (2,), (5, 6)),
+            (8, (3,), ()),
+            (9, (4,), ()),
+            (11, (5,), ()),
+        ):
+
+            @pl.when(number == step)
+            def _():
+                spread.relay(*relayed)
+                spread.start(*started)
+
+        @pl.when(number == 2 * lag - 1)
+        def _():
+            spread.wait(0, 1)
             weights.start(0, 1)
 
-        @pl.when(within(number - 2 * lag - 1, count))
-        def _():
-            last(number - 2 * lag - 1)
-
-        @pl.when(number < count)
-        def _():
-            scatter.join(number)
-
-        scatter.steps(number)
-
-        @pl.when(within(number - lag, count))
-        def _():
-            norm(number - lag)
-
-    in_order(count + 2 * lag + 1, wave)
+        @pl.when(within(number - 2 * lag + 1, count))
+        def _():
+            last(number - 2 * lag + 1)
+
+    in_order(count + 2 * lag - 1, wave)
     store_resid = pltpu.make_async_copy(resid, resid_out, resid_sem)
     store_resid.start()
-    spread.wait(2)
-    spread.wait(3)
-    for number in range(4):
-        spread.drain(number)
+    spread.relay(6)
+    spread.wait(2, 3, 4, 5, 6)
+    spread.drain(*range(7))
     scatter.drain()
     gather.drain()
     weights.wait(0, 1)
@@ -881,7 +1045,7 @@
         def _():
             first(number)
 
-        for hop in range(1, levels):
+        for hop in range(levels - 1, 0, -1):
 
             @pl.when(within(number - hop, count))
             def _():
@@ -931,18 +1095,18 @@
     spread_sems, refs = refs[:3], refs[3:]
     swap_sems, refs = refs[:3], refs[3:]
     gate_total, up_total, swish_grad, delta, query_acc, key_acc, value_acc, refs = *refs[:7], refs[7:]
-    load_sems, chunk_sems, store_sems, end_sems = refs
+    load_sems, chunk_sems, store_sems, end_sems, mixed_held, down_held, *halves = refs
     at = around(AXES)
     group, level, core = at
     count, levels, _, piece, width = full.shape
     chunk = 2 * levels * piece
-    loads = Moves(list(zip(ins, held)), load_sems)
-    loads.start(*range(13))
+    loads = Moves(list(zip(ins, held)) + [(mixed_src, mixed_held), (down_src, down_held)], load_sems)
+    loads.start(13, 14, *range(13))
     greet(plane_peers(at, sizes) + column_peers(at, sizes))
-    spread = Spread(at, sizes, [(mixed_src, mixed_dst, 0)], spread_sems)
-    swap = Swap(at, sizes, [(down_src, down_dst, 1), (gate_total, gate_dst, 0), (up_total, up_dst, 0)], swap_sems)
-    spread.start(0)
-    swap.start(0)
+    loads.wait(13, 14)
+    spread = Spread(at, sizes, quarters(mixed_held, mixed_dst), spread_sems)
+    swap = Swap(at, sizes, [(down_held, down_dst, 1), (gate_total, gate_dst, 0), (up_total, up_dst, 0)], swap_sems, halves)
+    spread.start(*range(4))
     scatter = Scatter(at, sizes, count, scatter_refs)
     gather = Gather(at, sizes, count, full, gather_sems)
     store = Chunks([(swish_grad, swish_out), (query, query_out)], chunk, chunk_sems)
@@ -1023,7 +1187,7 @@
         query[where, :] = lowered(query_acc[...])
         store.start(k)
 
-    lag = levels - 1
+    lag = levels
     tiles = width // chunk
 
     def wave(number):
@@ -1031,56 +1195,71 @@
         def _():
             first(number)
 
-        for hop in range(1, levels):
+        for hop in range(levels - 1, 0, -1):
 
             @pl.when(within(number - lag - hop, count))
             def _():
                 gather.hop(number - lag - hop, hop)
 
-        @pl.when(number == 2 * lag + 1)
+        @pl.when(number == lag)
+        def _():
+            loads.wait(4, 5)
+
+        @pl.when(within(number - lag, count))
+        def _():
+            norm(number - lag)
+
+        @pl.when(within(number - 1, count))
+        def _():
+            scatter.join(number - 1)
+
+        scatter.steps(number - 1)
+
+        @pl.when(number == 2 * lag - 1)
         def _():
             loads.wait(7, 8, 9, 10, 11, 12)
 
-        @pl.when(within(number - 2 * lag - 1, count))
-        def _():
-            last(number - 2 * lag - 1)
-
-        @pl.when(number < count)
-        def _():
-            scatter.join(number)
-
-        scatter.steps(number)
-
-        @pl.when(number == lag)
-        def _():
-            loads.wait(4, 5)
-
-        @pl.when(within(number - lag, count))
-        def _():
-            norm(number - lag)
+        @pl.when(within(number - 2 * lag + 1, count))
+        def _():
+            last(number - 2 * lag + 1)
 
         @pl.when(number == 0)
         def _():
             loads.wait(6)
 
-        @pl.when(number < tiles)
-        def _():
-            weigh(number)
-
-        @pl.when(number == tiles)
-        def _():
-            swap.start(1)
-            swap.start(2)
-
-    in_order(count + 2 * lag + 1, wave)
+        @pl.when(number < tiles // 2)
+        def _():
+            weigh(2 * number)
+            weigh(2 * number + 1)
+
+        for step, relayed in ((1, 0), (2, 1), (3, 2), (4, 3)):
+
+            @pl.when(number == step)
+            def _():
+                spread.relay(relayed)
+
+        @pl.when(number == 1)
+        def _():
+            swap.start(0)
+
+        @pl.when(number == tiles // 2)
+        def _():
+            swap.start(1, 2)
+
+        for step, relayed in ((5, 0), (7, 1), (9, 2)):
+
+            @pl.when(number == step)
+            def _():
+                swap.relay(relayed)
+
+    in_order(count + 2 * lag - 1, wave)
     keys[...] = lowered(key_acc[...])
     values[...] = lowered(value_acc[...])
     ends = Moves([(keys, key_out), (values, value_out)], end_sems)
     ends.start(0, 1)
-    spread.wait(0)
-    for number in range(3):
-        swap.wait(number)
-    spread.drain(0)
+    spread.wait(*range(4))
+    swap.wait(0, 1, 2)
+    spread.drain(*range(4))
     scatter.drain()
     gather.drain()
     store.wait(count)
@@ -1104,7 +1283,9 @@
     scatter_refs, refs = refs[:10], refs[10:]
     swap_sems, refs = refs[:3], refs[3:]
     sums, line_one, share, packed, gains, gains_in, refs = *refs[:6], refs[6:]
-    load_sems, sums_sent, sums_got, gain_sent, gain_got, deal_sent, deal_got, deal_own = refs
+    load_sems, sums_sent, sums_got, gain_sent, gain_got, refs = *refs[:5], refs[5:]
+    spread_sems, refs = refs[:3], refs[3:]
+    small_sems, halves = refs[:3], refs[3:]
     at = around(AXES)
     group, level, core = at
     place = 2 * level + core
@@ -1116,7 +1297,14 @@
     loads = Moves(list(zip(ins, held)), load_sems)
     loads.start(*range(13))
     greet(plane_peers(at, sizes) + column_all(at, sizes))
-    swap = Swap(at, sizes, list(zip(grads, targets, SWAP_AXES)) + [(gains, gains_in, 1)], swap_sems)
+    swap = Swap(at, sizes, list(zip(grads, targets, SWAP_AXES)), swap_sems, halves)
+    small = Swap(at, sizes, [(gains, gains_in, 1)], small_sems)
+    spread = Spread(
+        at,
+        sizes,
+        [(share.at[pl.ds(k * chunk, chunk)], grad_out, 0, rows_all, k * chunk) for k in range(count)],
+        spread_sems,
+    )
     line_one[...] = jnp.zeros(line_one.shape, jnp.float32)
     loads.wait(*range(9))
     mine = pl.ds(pl.multiple_of(place * width, width), width)
@@ -1177,21 +1365,6 @@
     def sender(j):
         return lax.rem(place + ranks - j, ranks)
 
-    def deal(k, j, owner):
-        rows = pl.ds(pl.multiple_of(owner * rows_all + k * chunk, chunk), chunk)
-        return pltpu.make_async_remote_copy(
-            src_ref=share.at[span(k, chunk)],
-            dst_ref=grad_out.at[rows],
-            send_sem=deal_sent.at[j - 1, k],
-            recv_sem=deal_got.at[j - 1, k],
-            device_id=(lax.rem(group + j, groups), level, core),
-            device_id_type=MESH,
-        )
-
-    def deal_here(k):
-        rows = pl.ds(pl.multiple_of(group * rows_all + k * chunk, chunk), chunk)
-        return pltpu.make_async_copy(share.at[span(k, chunk)], grad_out.at[rows], deal_own.at[k])
-
     def finish(k):
         scatter.finish(k)
         for j in range(1, ranks):
@@ -1211,9 +1384,6 @@
         line_one[...] += jnp.sum(outer.reshape(chunk // 8, 8, width), 0)
         back = value * gain[:, mine] - means[:, :1] - normed * means[:, 1:2]
         share[where, :] = lowered(wide(branch[where, mine]) + scale[where, :1] * back)
-        deal_here(k).start()
-        for j in range(1, groups):
-            deal(k, j, group).start()
 
     def weigh(number):
         if number == 4:
@@ -1261,11 +1431,29 @@
         def _():
             finish(number - lag)
 
+        for k in range(count):
+
+            @pl.when(number == lag + k)
+            def _():
+                spread.start(k)
+
+            @pl.when(number == lag + k + 2)
+            def _():
+                spread.relay(k)
+
         @pl.when(number == lag + 1)
         def _():
             weigh(4)
 
+        for step, relayed in ((2, 3), (4, 2), (5, 0), (6, 1), (8, 4)):
+
+            @pl.when(number == step)
+            def _():
+                swap.relay(relayed)
+
     in_order(count + lag, wave)
+    for k in (count - 2, count - 1):
+        spread.relay(k)
     total = jnp.sum(gain_two[...], 0, keepdims=True)
     packed[place] = jnp.concatenate([total, jnp.sum(line_one[...], 0, keepdims=True)], axis=1)
     for j in range(1, ranks):
@@ -1277,19 +1465,17 @@
     two = sum(packed[rank, :, :everything] for rank in range(ranks))
     one = jnp.concatenate([packed[rank, :, everything:] for rank in range(ranks)], axis=1)
     gains[...] = jnp.where(line == 0, one, two)
-    swap.start(5)
-    for number in range(6):
-        swap.wait(number)
+    small.start(0)
+    small.wait(0)
+    swap.wait(*range(5))
+    spread.wait(*range(count))
+    spread.drain(*range(count))
     gains_out[...] = jnp.sum(gains_in[...], 0)
     for j in range(1, ranks):
         pack_copy(j, place).wait_send()
     scatter.drain()
 
     def drain(k):
-        deal_here(k).wait()
-        for j in range(1, groups):
-            deal(k, j, lax.rem(group + groups - j, groups)).wait_recv()
-            deal(k, j, group).wait_send()
         for j in range(1, ranks):
             sums_copy(k, j, place).wait_send()
 
@@ -1338,7 +1524,7 @@
 def swap_shape(whole, axis, sizes):
     shape = list(whole.shape)
     shape[axis] //= sizes[0]
-    return struct((sizes[0],) + tuple(shape), whole.dtype)
+    return struct((3 if sizes[0] == 4 else sizes[0],) + tuple(shape), whole.dtype)
 
 
 def anywhere(items):
@@ -1402,7 +1588,7 @@
         0,
         anywhere((tokens, gain_rows) + masters),
         anywhere([spread_shape(tokens, 0, sizes), spread_shape(gain_rows, 0, sizes)] + rounded),
-        Spread.scratch(2, sizes) + held_like(masters) + held_like(rounded) + [DMA((8,)), DMA((8,))],
+        Spread.scratch(4, sizes) + Spread.scratch(1, sizes) + held_like(masters) + held_like(rounded) + [DMA((10,)), DMA((8,))] + held_like((tokens, gain_rows)),
     )
     full_w = [spread_shape(w, a, sizes) for w, a in zip(low, axes)]
     gains_all = wide(lowered(gains_all.reshape(sizes[0], 8, -1)))
@@ -1453,8 +1639,9 @@
             VMEM((rows_dev, v_dim), f32),
             DMA,
             DMA((4,)),
-            DMA((4,)),
+            DMA((5,)),
             DMA((count,)),
+            VMEM(w_out.shape, jnp.bfloat16),
         ],
     )
     rate = jnp.log1p(-jnp.exp2(-5.0 - place.astype(f32))).reshape(1)
@@ -1481,7 +1668,7 @@
         held_like(middle_ins)
         + Scatter.scratch(count, sizes, (PIECE, width))
         + Gather.scratch(count, sizes, (PIECE, width))
-        + Spread.scratch(4, sizes)
+        + Spread.scratch(7, sizes)
         + held_like(full_w[5:7])
         + [
             VMEM((rows_dev, ff_dim), f32),
@@ -1490,12 +1677,13 @@
             VMEM((own, width), f32),
             VMEM((rows_dev, v_dim), f32),
             VMEM((rows_dev, v_dim), jnp.bfloat16),
-            DMA((6,)),
+            DMA((8,)),
             DMA((5, count)),
             DMA((ranks, count)),
             DMA((2,)),
             DMA,
-        ],
+        ]
+        + held_like((low[7], cotangent)),
     )
     dy_part = pick(source, dy_all)
     feed_ins = (hidden, down_w, resid, gate, up_proj)
@@ -1572,7 +1760,7 @@
             held_like(back_ins)
             + Scatter.scratch(count, sizes, (PIECE, width))
             + Gather.scratch(count, sizes, (PIECE, width))
-            + Spread.scratch(1, sizes)
+            + Spread.scratch(4, sizes)
             + Swap.scratch(3, sizes)
             + held_like(full_w[5:7])
             + [
@@ -1581,11 +1769,13 @@
                 VMEM((chunk, qk_dim), f32),
                 VMEM((rows_dev, qk_dim), f32),
                 VMEM((rows_dev, v_dim), f32),
-                DMA((13,)),
+                DMA((15,)),
                 DMA((2, count)),
                 DMA((ranks, count)),
                 DMA((2,)),
-            ],
+            ]
+            + held_like((mixed_share, grad_down))
+            + half_blocks([(full_w[7], 1), (full_w[5], 0), (full_w[6], 0)], sizes),
         )
     )
     close_ins = (
@@ -1614,7 +1804,7 @@
         held_like(close_ins)
         + held_like(full_w[:5])
         + Scatter.scratch(count, sizes, (chunk, slice_width))
-        + Swap.scratch(swaps + 1, sizes)
+        + Swap.scratch(swaps, sizes)
         + [
             VMEM((ranks, count, 8, chunk), f32),
             VMEM((8, slice_width), f32),
@@ -1627,10 +1817,10 @@
             DMA((ranks - 1, count)),
             DMA((ranks - 1,)),
             DMA((ranks - 1,)),
-            DMA((sizes[0] - 1, count)),
-            DMA((sizes[0] - 1, count)),
-            DMA((count,)),
-        ],
+        ]
+        + Spread.scratch(count, sizes)
+        + Swap.scratch(1, sizes)
+        + half_blocks(list(zip(full_w[:5], SWAP_AXES)), sizes),
     )
     grads = [jnp.sum(wide(g), 0) for g in attn_grads + ff_grads[1:] + ff_grads[:1]]
     slot_match = dealing[:, None] == ident[None, :]

time: 688 us -> 590 us (0.86)
  Pallas kernels: 641 us -> 543 us
    pallas_call x6, Pallas kernels: 641 us -> 543 us  [kernel_call(): pl.pallas_call(body, out_shape=[shape for _, shape in outs], in_specs=[pl...]
where the time goes in v3:
time: 590 us; the launch traced here: 589 us
  Pallas kernels  543 us (92%)
  local copies, waits for them, and re-layouts  28.9 us (5%)
  other arithmetic  15.8 us (3%)
    pallas_call x6, Pallas kernels, kernel_call(): pl.pallas_call(body, out_shape=[shape for _, shape in outs], in_specs=[pl...  543 us
    gather x4, local copies, waits for them, and re-layouts, pick(): return whole.at[rows].get(mode='promise_in_bounds')  26 us

profile of v3, /device:TPU:0, one launch (start us, length us, event | category | flops | bytes accessed | tf_op | source)
XLA Modules:
  0.0 589.1 jit_solution(18153116251871475472)
XLA Ops:
  0.6 0.7 dynamic_slice.3
  1.4 0.8 reduce-window.17
  2.2 0.7 bitcast_subtract_fusion
  2.9 0.9 select_reduce_fusion.5
  3.7 0.2 reduce-window.16
  3.9 0.0 copy-start.6
  3.9 0.1 convert_reduce_fusion.9
  4.0 0.1 select_reduce_fusion.1
  4.2 1.3 select_maximum_fusion.gains
  5.5 31.6 %shard_map.229 = (bf16[6144,256]{1,0:T(8,128)(2,1)}, f32[32,512]{1,0:T(8,128)}, bf16[512,256]{1,0:T(8,128)(2,1)}, bf16[512,256]{1,0:T(8,128)(2,1)}, bf16[512,512...) custom-call(bf16[1536,256]{1,0:T(8,128)(2,1)} %tokens.1, ...), custom_call_target="tpu_custom_call" | custom-call | tf_op jit(solution)/shard_map/pallas_call | solution.py:1506
  37.1 0.0 copy-done.6
  37.1 0.0 copy-start.5
  37.1 6.8 %gather_fusion = bf16[1536,256]{1,0:T(8,128)(2,1)} fusion(bf16[6144,256]{1,0:T(8,128)(2,1)} %get-tuple-element.69, s32[2048]{0:T(1024)S(1)} %pad_clamp_fusion.1), kind=kCustom, calls=%fused_computation | custom fusion | bytes 1579008 | tf_op jit(solution)/shard_map/gather | solution.py:1539
  43.9 0.0 copy-done.5
  43.9 0.6 fusion.6
  44.5 83.3 %shard_map.230 = (bf16[1536,2048]{1,0:T(8,128)(2,1)}, bf16[1536,256]{1,0:T(8,128)(2,1)}, bf16[1536,256]{1,0:T(8,128)(2,1)}, bf16[1536,512]{1,0:T(8,128)(2,1)}, f...) custom-call(bf16[6,256,256]{2,1,0:T(8,128)(2,1)} %bitcast.20, ...), custom_call_target="tpu_custom_call" | custom-call | tf_op jit(solution)/shard_map/pallas_call | solution.py:1506
  128.0 109.4 %shard_map.231 = (bf16[1536,2048]{1,0:T(8,128)(2,1)}, f32[1536,512]{1,0:T(8,128)}, f32[1536,512]{1,0:T(8,128)}, bf16[1536,512]{1,0:T(8,128)(2,1)}, f32[192,2048]...) custom-call(s32[3]{0:T(128)} %copy-done.6, ...), custom_call_target="tpu_custom_call" | custom-call | tf_op jit(solution)/shard_map/pallas_call | solution.py:1506
  237.4 6.8 %gather_fusion.1 = bf16[1536,256]{1,0:T(8,128)(2,1)} fusion(bf16[6144,256]{1,0:T(8,128)(2,1)} %get-tuple-element.84, s32[2048]{0:T(1024)S(1)} %pad_clamp_fusion.1), kind=kCustom, calls=%fused_computation.1 | custom fusion | bytes 1579008 | tf_op jit(solution)/shard_map/gather | solution.py:1539
  244.2 89.1 %shard_map.232 = (bf16[1536,256]{1,0:T(8,128)(2,1)}, bf16[1536,512]{1,0:T(8,128)(2,1)}, bf16[1536,512]{1,0:T(8,128)(2,1)}, bf16[192,2048]{1,0:T(8,128)(2,1)}, bf16[512,2048]{1,0:T(8,128)(2,1)}) custom-call(bf16[6,256,256]{2,1,0:T(8,128)(2,1)} %bitcast.19, bf16[1536,512]{1,0:T(8,128)(2,1)} %get-tuple-element.85.refs_0_, ...), custom_call_target="tpu_custom_call" | custom-call | tf_op jit(solution)/shard_map/pallas_call | solution.py:1506
  333.4 115.6 %shard_map.233 = (bf16[1536,2048]{1,0:T(8,128)(2,1)}, bf16[1536,512]{1,0:T(8,128)(2,1)}, bf16[1536,256]{1,0:T(8,128)(2,1)}, bf16[1536,256]{1,0:T(8,128)(2,1)}, b...) custom-call(s32[3]{0:T(128)} %copy-done.6, ...), custom_call_target="tpu_custom_call" | custom-call | tf_op jit(solution)/shard_map/pallas_call | solution.py:1506
  449.0 3.9 convert_reduce_fusion
  452.9 114.4 %shard_map.234 = (bf16[6144,256]{1,0:T(8,128)(2,1)}, f32[8,512]{1,0:T(8,128)}, bf16[3,512,256]{2,1,0:T(8,128)(2,1)}, bf16[3,512,256]{2,1,0:T(8,128)(2,1)}, bf16[...) custom-call(f32[1,2048]{1,0:T(1,128)} %bitcast.22, ...), custom_call_target="tpu_custom_call" | custom-call | tf_op jit(solution)/shard_map/pallas_call | solution.py:1506
  567.3 0.0 copy-start.1
  567.3 0.0 copy-start.2
  567.4 4.1 convert_reduce_fusion.3
  571.4 0.0 copy-done.1
  571.4 0.0 copy-done.2
  571.4 0.0 copy-start.3
  571.4 0.0 copy-start.4
  571.4 1.8 convert_reduce_fusion.2
  573.2 0.0 copy-start.7
  573.2 0.0 copy-done.3
  573.2 0.0 copy-done.4
  573.3 1.2 convert_reduce_fusion.6
  574.4 0.0 copy-done.7
  574.4 0.0 copy-done.8
  574.5 0.2 select_reduce_fusion.4
  574.6 0.1 reshape.188
  574.7 0.2 reduce_window_sum.27
  574.9 0.1 reduce_window_sum.28
  575.0 0.1 select_reduce_fusion.2
  575.1 0.1 convert_reduce_fusion.8
  575.2 0.1 select_reduce_fusion
  575.4 0.0 copy-start
  575.4 7.0 %gather_fusion.3 = bf16[1536,256]{1,0:T(8,128)(2,1)} fusion(bf16[6144,256]{1,0:T(8,128)(2,1)} %get-tuple-element.114, s32[2048]{0:T(1024)S(1)} %pad_clamp_fusion), kind=kCustom, calls=%fused_computation.3 | custom fusion | bytes 1579008 | tf_op jit(solution)/shard_map/gather | solution.py:1539
  582.4 1.4 fusion.7
  583.8 0.0 copy-done
  583.8 5.4 gather_fusion.2
  (11 shorter events, 0.1 us)
Async XLA Ops:
  3.9 33.1 %copy-start.6 = (s32[3]{0:T(128)}, s32[3]{0:T(128)S(1)}, u32[]{:S(2)}) copy-start(s32[3]{0:T(128)S(1)} %get-tuple-element.129.bounds) | copy-start | bytes 40
  37.1 6.9 %copy-start.5 = (f32[32,512]{1,0:T(8,128)S(1)}, f32[32,512]{1,0:T(8,128)}, u32[]{:S(2)}) copy-start(f32[32,512]{1,0:T(8,128)} %get-tuple-element.68) | copy-start | bytes 196612
  567.3 4.1 copy-start.1
  567.3 4.1 copy-start.2
  571.4 1.8 copy-start.3
  571.4 1.8 copy-start.4
  573.2 1.2 copy-start.7
  573.2 1.2 copy-start.8
  575.4 8.4 %copy-start = (bf16[6144,256]{1,0:T(8,128)(2,1)S(1)}, bf16[6144,256]{1,0:T(8,128)(2,1)}, u32[]{:S(2)}) copy-start(bf16[6144,256]{1,0:T(8,128)(2,1)} %get-tuple-element.99) | copy-start | bytes 9437188

commit v4 on v3

--- a/solution.py
+++ b/solution.py
@@ -328,19 +328,23 @@
         self.sent_core, self.got_core, self.sent_up, self.got_up, self.sent_down, self.got_down = refs[4:]
 
     @staticmethod
+    def rooms(count, sizes, piece):
+        levels = sizes[1]
+        return [
+            pltpu.VMEM((2, levels, 2) + piece, jnp.bfloat16),
+            pltpu.VMEM((count, levels) + piece, jnp.bfloat16),
+            pltpu.VMEM((count, levels + 1) + piece, jnp.bfloat16),
+            pltpu.VMEM(piece, jnp.float32),
+        ]
+
+    @staticmethod
+    def sems(count, sizes):
+        dma = pltpu.SemaphoreType.DMA
+        return [dma((count,)) for _ in range(2)] + [dma((sizes[1], count)) for _ in range(4)]
+
+    @staticmethod
     def scratch(count, sizes, piece):
-        levels = sizes[1]
-        dma = pltpu.SemaphoreType.DMA
-        return (
-            [
-                pltpu.VMEM((2, levels, 2) + piece, jnp.bfloat16),
-                pltpu.VMEM((count, levels) + piece, jnp.bfloat16),
-                pltpu.VMEM((count, levels + 1) + piece, jnp.bfloat16),
-                pltpu.VMEM(piece, jnp.float32),
-            ]
-            + [dma((count,)) for _ in range(2)]
-            + [dma((levels, count)) for _ in range(4)]
-        )
+        return Scatter.rooms(count, sizes, piece) + Scatter.sems(count, sizes)
 
     def across(self, k):
         group, level, core = self.at
@@ -375,10 +379,16 @@
             device_id_type=MESH,
         )
 
-    def free(self, k):
+    def free(self, k, before=None):
         @pl.when(k >= 2)
         def _():
             self.across(k - 2).wait_send()
+
+        if before is not None:
+
+            @pl.when(k < 2)
+            def _():
+                before.across(self.count - 2 + k).wait_send()
 
     def start(self, k):
         self.across(k).start()
@@ -448,27 +458,22 @@
             self.down(k, level).wait_recv()
             self.total[...] += wide(self.inbox[k, level])
 
+    def sent(self, k):
+        level = self.at[1]
+        for owner in range(self.levels):
+
+            @pl.when(level < owner)
+            def _():
+                self.up(k, owner).wait_send()
+
+            @pl.when(level > owner)
+            def _():
+                self.down(k, owner).wait_send()
+
     def drain(self):
-        level = self.at[1]
-
-        def one(k, _):
-            @pl.when(k >= self.count - 2)
-            def _():
-                self.across(k).wait_send()
-
-            for owner in range(self.levels):
-
-                @pl.when(level < owner)
-                def _():
-                    self.up(k, owner).wait_send()
-
-                @pl.when(level > owner)
-                def _():
-                    self.down(k, owner).wait_send()
-
-            return 0
-
-        lax.fori_loop(0, self.count, one, 0)
+        self.across(self.count - 2).wait_send()
+        self.across(self.count - 1).wait_send()
+        in_order(self.count, self.sent)
 
 
 def in_order(count, step):
@@ -699,7 +704,7 @@
     x_part, gain, *refs = (shards, gain) + refs
     sources, refs = refs[:5], refs[5:]
     normed_out, query_out, key_out, value_out, swish_out, *refs = refs
-    weight_outs, refs = refs[:5], refs[5:]
+    weight_outs, dy_out, refs = refs[:4], refs[4], refs[5:]
     rows_out, unit_out, scale_out, *refs = refs
     full, *refs = refs
     gather_sems, refs = refs[:6], refs[6:]
@@ -716,7 +721,7 @@
     load_shard = pltpu.make_async_copy(sources[4], shard, weight_sem.at[4])
     load_shard.start()
     greet(plane_peers(at, sizes) + column_peers(at, sizes))
-    items = [(s, t, 0) for s, t in zip(sources[:4], weights)] + [(shard, weight_outs[4], 1)]
+    items = [(s, t, 0) for s, t in zip(sources[:4], weights)] + quarters(shard, dy_out)
     spread = Spread(at, sizes, items, spread_sems)
     gather = Gather(at, sizes, count, full, gather_sems)
     load.wait()
@@ -760,13 +765,19 @@
             def _():
                 gather.hop(number - hop, hop)
 
-        for step, relayed, started in ((1, 0, None), (2, 1, 3), (4, 2, 4), (7, 3, None)):
+        for step, relayed, started in (
+            (1, (0,), ()),
+            (2, (1,), (3,)),
+            (4, (2,), (4, 5)),
+            (6, (3,), (6, 7)),
+            (8, (4,), ()),
+            (9, (5,), ()),
+        ):
 
             @pl.when(number == step)
             def _():
-                spread.relay(relayed)
-                if started is not None:
-                    spread.start(started)
+                spread.relay(*relayed)
+                spread.start(*started)
 
         @pl.when(within(number - levels, count))
         def _():
@@ -774,7 +785,7 @@
             norm(number - levels)
 
     in_order(count + levels, wave)
-    spread.relay(4)
+    spread.relay(6)
     outs = [(query, query_out), (keys, key_out), (values, value_out), (swish, swish_out)]
     for number, (held, out) in enumerate(outs):
         spread.wait(number)
@@ -786,11 +797,12 @@
 
         in_order(count, rows)
         pltpu.make_async_copy(held, out, out_sem.at[number]).start()
-    spread.wait(4)
+    spread.relay(7)
+    spread.wait(4, 5, 6, 7)
     for number, (held, out) in enumerate(outs):
         pltpu.make_async_copy(held, out, out_sem.at[number]).wait()
         pltpu.make_async_copy(weights[number], weight_outs[number], weight_sem.at[number]).wait()
-    spread.drain(*range(5))
+    spread.drain(*range(8))
     gather.drain()
 
     def stored(k):
@@ -801,376 +813,240 @@
     in_order(count, stored)
 
 
-def middle_kernel(sizes, bounds, rate, gain, *refs):
-    ins, refs = refs[:6], refs[6:]
-    sources, refs = refs[:4], refs[4:]
-    normed_out, gate_out, up_out, hidden_out, resid_out, retained_out, mixed_out, *refs = refs
-    gate_w_out, up_w_out, down_w_out, dy_out, *refs = refs
-    held, refs = refs[:6], refs[6:]
-    query, keys, values, swish, out_w, x_rows = held
-    scatter_refs, refs = refs[:10], refs[10:]
-    full, *refs = refs
-    gather_sems, refs = refs[:6], refs[6:]
+class Ring:
+    def __init__(self, slots, whole, size, sems):
+        self.slots, self.whole, self.size, self.sems = slots, whole, size, sems
+
+    def load(self, k):
+        return pltpu.make_async_copy(
+            self.whole.at[span(k, self.size)], self.slots.at[lax.rem(k, 2)], self.sems.at[k]
+        )
+
+    def store(self, k):
+        return pltpu.make_async_copy(
+            self.slots.at[lax.rem(k, 2)], self.whole.at[span(k, self.size)], self.sems.at[k]
+        )
+
+    def free(self, k):
+        @pl.when(k >= 2)
+        def _():
+            self.store(k - 2).wait()
+
+
+def core_kernel(sizes, bounds, rate, gain, *refs):
+    query_src, key_src, value_src, rows_src, dy_src, swish_src, *refs = refs
+    shards, refs = refs[:4], refs[4:]
+    mixed_in_out, retained_out, branch_out, swish_out, query_out, key_out, value_out, *refs = refs
+    gain_out, mixed_dst, down_dst, gate_dst, up_dst, *refs = refs
+    query, keys, values, x_rows, out_w, gate_w, up_w, down_w, *refs = refs
+    rooms, refs = refs[:4], refs[4:]
+    (other_part,), refs = refs[:1], refs[1:]
+    sems_one, sems_two, sems_three, refs = refs[:6], refs[6:12], refs[12:18], refs[18:]
+    normed_mid, refs = refs[0], refs[1:]
+    normed_sems, refs = refs[:6], refs[6:]
+    dy, refs = refs[0], refs[1:]
+    dy_sems, refs = refs[:6], refs[6:]
+    branch, refs = refs[0], refs[1:]
+    branch_sems, refs = refs[:6], refs[6:]
     spread_sems, refs = refs[:3], refs[3:]
-    gate_w, up_w, gate, up, hidden, resid, retained, mixed_in, refs = *refs[:8], refs[8:]
-    load_sems, chunk_sems, normed_sems, weight_sems, resid_sem, down_shard, dy_shard = refs
+    deal_sems, refs = refs[:3], refs[3:]
+    swap_sems, refs = refs[:3], refs[3:]
+    hidden, gate_grad, up_grad, resid, swish_slots, retained_slots, mixed_in_slots, grad_slots, *refs = refs
+    key_acc, value_acc, query_acc, delta, down_grad, mixed, *refs = refs
+    load_sems, ring_sems, branch_store, query_store, end_sems, *halves = refs
     at = around(AXES)
     group, level, core = at
-    count, levels, _, piece, width = full.shape
-    chunk = 2 * levels * piece
-    loads = Moves(list(zip(ins, held)) + [(sources[2], down_shard), (sources[3], dy_shard)], load_sems)
-    loads.start(6, 7, *range(6))
+    place = 2 * level + core
+    count, levels, _, piece, width = normed_mid.shape
+    ranks = 2 * levels
+    chunk = ranks * piece
+    part_width = width // ranks
+    loads = Moves(
+        [
+            (dy_src, dy.at[:, level, core]),
+            (query_src, query),
+            (key_src, keys),
+            (value_src, values),
+            (rows_src, x_rows),
+        ],
+        load_sems,
+    )
+    loads.start(*range(5))
+    swish_one = Ring(swish_slots, swish_src, chunk, ring_sems.at[0])
+    swish_two = Ring(swish_slots, swish_src, chunk, ring_sems.at[1])
+    retained_one = Ring(retained_slots, retained_out, chunk, ring_sems.at[2])
+    retained_two = Ring(retained_slots, retained_out, chunk, ring_sems.at[3])
+    mixed_in_ring = Ring(mixed_in_slots, mixed_in_out, chunk, ring_sems.at[4])
+    grad_ring = Ring(grad_slots, swish_out, chunk, ring_sems.at[5])
+    query_ends = Chunks([(query, query_out)], chunk, query_store)
+    swish_one.load(0).start()
+    swish_one.load(1).start()
     greet(plane_peers(at, sizes) + column_peers(at, sizes))
     spread = Spread(
         at,
         sizes,
-        [
-            (sources[0], gate_w, 0),
-            (sources[1], up_w, 0),
-            (down_shard, down_w_out, 1),
-        ]
-        + quarters(dy_shard, dy_out),
+        [(shards[0], out_w, 1), (shards[1], gate_w, 0), (shards[2], up_w, 0), (shards[3], down_w, 1)],
         spread_sems,
     )
-    loads.wait(6, 7)
+    deal = Spread(
+        at,
+        sizes,
+        [
+            (mixed.at[pl.ds(k * chunk, chunk)], mixed_dst, 0, count * chunk, k * chunk)
+            for k in range(count)
+        ],
+        deal_sems,
+    )
+    swap = Swap(
+        at, sizes, [(down_grad, down_dst, 1), (gate_w, gate_dst, 0), (up_w, up_dst, 0)], swap_sems, halves
+    )
     spread.start(0, 1)
-    scatter = Scatter(at, sizes, count, scatter_refs)
-    gather = Gather(at, sizes, count, full, gather_sems)
-    weights = Moves([(gate_w, gate_w_out), (up_w, up_w_out)], weight_sems)
-    early = Chunks([(retained, retained_out), (mixed_in, mixed_out)], chunk, chunk_sems.at[:2])
-    late = Chunks([(gate, gate_out), (up, up_out), (hidden, hidden_out)], chunk, chunk_sems.at[2:])
-    loads.wait(*range(6))
+    one = Scatter(at, sizes, count, list(rooms) + list(sems_one))
+    two = Scatter(at, sizes, count, [other_part] + list(rooms[1:]) + list(sems_two))
+    three = Scatter(at, sizes, count, list(rooms) + list(sems_three))
+    total = rooms[3]
+    mid_gather = Gather(at, sizes, count, normed_mid, normed_sems)
+    dy_gather = Gather(at, sizes, count, dy, dy_sems)
+    branch_gather = Gather(at, sizes, count, branch, branch_sems)
+    gain_out[...] = jnp.zeros(gain_out.shape, jnp.float32)
+    key_acc[...] = jnp.zeros(key_acc.shape, jnp.float32)
+    value_acc[...] = jnp.zeros(value_acc.shape, jnp.float32)
+    loads.wait(0)
+    dy_gather.start(0)
+    loads.wait(1, 2, 3, 4)
     tile = 512
 
-    def stores(k):
+    def branch_stores(k):
         copies = []
         for q in range(levels):
             for c in range(2):
                 rows = pl.ds(pl.multiple_of(k * chunk + (2 * q + c) * piece, piece), piece)
                 copies.append(
-                    pltpu.make_async_copy(full.at[k, q, c], normed_out.at[rows], normed_sems.at[2 * q + c, k])
+                    pltpu.make_async_copy(branch.at[k, q, c], branch_out.at[rows], branch_store.at[2 * q + c, k])
                 )
         return copies
 
     def first(k):
         where = span(k, chunk)
-        retained[where, :] = jnp.zeros((chunk, retained.shape[1]), jnp.float32)
+        slot = lax.rem(k, 2)
+        retained_one.free(k)
+        retained_slots[slot] = jnp.zeros((chunk, values.shape[1]), jnp.float32)
 
         def block(j, carry):
             there = span(j, chunk)
             decay = decay_tile(k, j, chunk, bounds, rate)
             weight = lowered(inner_rows(query[where, :], keys[there, :]) * decay)
-            retained[where, :] += matmul(weight, values[there, :])
+            retained_slots[slot] += matmul(weight, values[there, :])
             return carry
 
         lax.fori_loop(0, k + 1, block, 0)
-        normed, _ = layer_norm(retained[where, :], GROUP_EPS)
-        value = swish[where, :]
-        mixed_in[where, :] = lowered(value * jax.nn.sigmoid(value) * normed)
-        early.start(k)
-        scatter.free(k)
-        rows = mixed_in[where, :]
+        retained_one.store(k).start()
+        normed, _ = layer_norm(retained_slots[slot], GROUP_EPS)
+        swish_one.load(k).wait()
+        value = swish_slots[slot]
+        mixed_in_ring.free(k)
+        mixed_in_slots[slot] = lowered(value * jax.nn.sigmoid(value) * normed)
+        mixed_in_ring.store(k).start()
+
+        @pl.when(k + 2 < count)
+        def _():
+            swish_one.load(k + 2).start()
+
+        @pl.when(k == 0)
+        def _():
+            spread.wait(0)
+
+        one.free(k)
+        rows = mixed_in_slots[slot]
         for column in range(0, width, tile):
             value = matmul(rows, out_w[:, column : column + tile])
-            scatter.part[lax.rem(k, 2), :, :, :, column : column + tile] = lowered(value).reshape(
-                levels, 2, piece, tile
-            )
-        scatter.start(k)
-
-    def norm(k):
-        scatter.finish(k)
+            one.part[slot, :, :, :, column : column + tile] = lowered(value).reshape(levels, 2, piece, tile)
+        one.start(k)
+
+    def mid_norm(k):
+        one.finish(k)
 
         def block(number, carry):
             sub = span(number, 16)
             where = pl.ds(pl.multiple_of(k * piece + number * 16, 16), 16)
-            value = wide(x_rows[where, :]) + scatter.total[sub, :]
+            value = wide(x_rows[where, :]) + total[sub, :]
             resid[where, :] = value
             unit, _ = layer_norm(value, EPSILON)
-            full[k, level, core, sub, :] = lowered(unit * gain[...])
+            normed_mid[k, level, core, sub, :] = lowered(unit * gain[...])
             return carry
 
         lax.fori_loop(0, piece // 16, block, 0)
-        gather.start(k)
-
-    def last(k):
-        gather.ready(k)
-        for copy in stores(k):
-            copy.start()
-        rows = full[k].reshape(chunk, width)
+        mid_gather.start(k)
+
+    def turn(k):
+        mid_gather.ready(k)
+        rows = normed_mid[k].reshape(chunk, width)
         where = span(k, chunk)
-        gate[where, :] = matmul(rows, gate_w[...])
-        up[where, :] = matmul(rows, up_w[...])
-        hidden[where, :] = lowered(jax.nn.gelu(gate[where, :]) * up[where, :])
-        late.start(k)
-
-    lag = levels
-
-    def wave(number):
-        @pl.when(number < count)
-        def _():
-            first(number)
-
-        for hop in range(levels - 1, 0, -1):
-
-            @pl.when(within(number - lag - hop, count))
-            def _():
-                gather.hop(number - lag - hop, hop)
-
-        @pl.when(within(number - lag, count))
-        def _():
-            norm(number - lag)
-
-        @pl.when(within(number - 1, count))
-        def _():
-            scatter.join(number - 1)
-
-        scatter.steps(number - 1)
-
-        for step, relayed, started in (
-            (2, (0,), (2,)),
-            (4, (1,), (3, 4)),
-            (6, (2,), (5, 6)),
-            (8, (3,), ()),
-            (9, (4,), ()),
-            (11, (5,), ()),
-        ):
-
-            @pl.when(number == step)
-            def _():
-                spread.relay(*relayed)
-                spread.start(*started)
-
-        @pl.when(number == 2 * lag - 1)
-        def _():
-            spread.wait(0, 1)
-            weights.start(0, 1)
-
-        @pl.when(within(number - 2 * lag + 1, count))
-        def _():
-            last(number - 2 * lag + 1)
-
-    in_order(count + 2 * lag - 1, wave)
-    store_resid = pltpu.make_async_copy(resid, resid_out, resid_sem)
-    store_resid.start()
-    spread.relay(6)
-    spread.wait(2, 3, 4, 5, 6)
-    spread.drain(*range(7))
-    scatter.drain()
-    gather.drain()
-    weights.wait(0, 1)
-    store_resid.wait()
-    early.wait(count)
-    late.wait(count)
-
-    def stored(k):
-        for copy in stores(k):
-            copy.wait()
-
-    in_order(count, stored)
-
-
-def feed_kernel(sizes, dy_part, *refs):
-    ins, refs = refs[:5], refs[5:]
-    mixed_out, gate_grad_out, up_grad_out, dy_rows_out, down_grad_out, *refs = refs
-    held, refs = refs[:5], refs[5:]
-    hidden, down_w, resid, gate, up = held
-    scatter_refs, refs = refs[:10], refs[10:]
-    full, *refs = refs
-    gather_sems, refs = refs[:6], refs[6:]
-    tile_acc, down_acc, down_grad, mixed, gate_grad, up_grad, dy_rows, refs = *refs[:7], refs[7:]
-    load_sem, load_sems, chunk_sems, end_sems = refs
-    at = around(AXES)
-    group, level, core = at
-    place = 2 * level + core
-    count, levels, _, chunk, width = full.shape
-    ranks = 2 * levels
-    piece = chunk // ranks
-    load = pltpu.make_async_copy(dy_part, full.at[:, level, core], load_sem)
-    load.start()
-    loads = Moves(list(zip(ins, held)), load_sems)
-    loads.start(*range(5))
-    greet(column_peers(at, sizes))
-    scatter = Scatter(at, sizes, count, scatter_refs)
-    gather = Gather(at, sizes, count, full, gather_sems)
-    store = Chunks(
-        [(mixed, mixed_out), (gate_grad, gate_grad_out), (up_grad, up_grad_out)], chunk, chunk_sems
-    )
-    early = Chunks(store.pairs[:1], chunk, chunk_sems.at[:1])
-    late = Chunks(store.pairs[1:], chunk, chunk_sems.at[1:])
-    load.wait()
-    gather.start(0)
-    loads.wait(0, 1, 2)
-    down_acc[...] = jnp.zeros(down_acc.shape, jnp.float32)
-
-    def first(k):
-        scatter.free(k)
-        rows = hidden[span(k, chunk), :]
-        mine = span(place, piece)
-        for rank in range(ranks):
-            columns = slice(rank * width, (rank + 1) * width)
-            tile_acc[...] = matmul(rows, down_w[:, columns])
-            tile_acc[mine, :] += resid[span(k, piece), columns]
-            scatter.part[lax.rem(k, 2), rank // 2, rank % 2] = lowered(tile_acc[...])
-        scatter.start(k)
-
-    def last(k):
-        gather.ready(k)
-        where = span(k, chunk)
-        rows = jnp.concatenate([full[k, q, c] for q in range(levels) for c in range(2)], axis=1)
-        back = inner_rows(rows, down_w[...])
-        mine = span(place, piece)
-        dy_rows[span(k, piece), :] = jnp.concatenate(
-            [full[k, q, c, mine, :] for q in range(levels) for c in range(2)], axis=1
-        )
-        g, u = gate[where, :], up[where, :]
+        g = matmul(rows, gate_w[...])
+        u = matmul(rows, up_w[...])
         root = 0.7978845608028654
         bend = jnp.tanh(root * (g + 0.044715 * g * g * g))
         curve = 0.5 * (1.0 + bend)
+        active = g * curve
+        hidden[where, :] = lowered(active * u)
         slope = curve + 0.5 * g * (1.0 - bend * bend) * root * (1.0 + 0.134145 * g * g)
+        dy_gather.ready(k)
+        rows = jnp.concatenate([dy[k, q, c] for q in range(levels) for c in range(2)], axis=1)
+        back = inner_rows(rows, down_w[...])
         gate_grad[where, :] = lowered(back * u * slope)
-        up_grad[where, :] = lowered(back * g * curve)
-        late.start(k)
-        for rank in range(ranks):
-            columns = slice(rank * width, (rank + 1) * width)
-            down_acc[:, columns] += inner_cols(hidden[where, :], full[k, rank // 2, rank % 2])
-
-    lag = levels - 1
-
-    def wave(number):
-        @pl.when(number + 1 < count)
-        def _():
-            gather.start(number + 1)
-
-        @pl.when(number < count)
-        def _():
-            first(number)
-
-        for hop in range(levels - 1, 0, -1):
-
-            @pl.when(within(number - hop, count))
-            def _():
-                gather.hop(number - hop, hop)
-
-        @pl.when(number < count)
-        def _():
-            scatter.join(number)
-
-        scatter.steps(number)
-
-        @pl.when(within(number - lag, count))
-        def _():
-            scatter.finish(number - lag)
-            mixed[span(number - lag, chunk), :] = lowered(scatter.total[...])
-            early.start(number - lag)
-
-        @pl.when(number == levels)
-        def _():
-            loads.wait(3, 4)
-
-        @pl.when(within(number - levels, count))
-        def _():
-            last(number - levels)
-
-    in_order(count + levels, wave)
-    down_grad[...] = lowered(down_acc[...])
-    ends = Moves([(down_grad, down_grad_out), (dy_rows, dy_rows_out)], end_sems)
-    ends.start(0, 1)
-    scatter.drain()
-    gather.drain()
-    store.wait(count)
-    ends.wait(0, 1)
-
-
-def back_kernel(sizes, bounds, rate, gain, *refs):
-    ins, refs = refs[:13], refs[13:]
-    mixed_src, down_src, *refs = refs
-    branch_out, swish_out, query_out, key_out, value_out, gain_out, *refs = refs
-    mixed_dst, down_dst, gate_dst, up_dst, *refs = refs
-    held, refs = refs[:13], refs[13:]
-    gate_grad, up_grad, gate_w, up_w, resid, dy_rows, normed_mid, out_w, retained, swish, *held_qkv = held
-    query, keys, values = held_qkv
-    scatter_refs, refs = refs[:10], refs[10:]
-    full, *refs = refs
-    gather_sems, refs = refs[:6], refs[6:]
-    spread_sems, refs = refs[:3], refs[3:]
-    swap_sems, refs = refs[:3], refs[3:]
-    gate_total, up_total, swish_grad, delta, query_acc, key_acc, value_acc, refs = *refs[:7], refs[7:]
-    load_sems, chunk_sems, store_sems, end_sems, mixed_held, down_held, *halves = refs
-    at = around(AXES)
-    group, level, core = at
-    count, levels, _, piece, width = full.shape
-    chunk = 2 * levels * piece
-    loads = Moves(list(zip(ins, held)) + [(mixed_src, mixed_held), (down_src, down_held)], load_sems)
-    loads.start(13, 14, *range(13))
-    greet(plane_peers(at, sizes) + column_peers(at, sizes))
-    loads.wait(13, 14)
-    spread = Spread(at, sizes, quarters(mixed_held, mixed_dst), spread_sems)
-    swap = Swap(at, sizes, [(down_held, down_dst, 1), (gate_total, gate_dst, 0), (up_total, up_dst, 0)], swap_sems, halves)
-    spread.start(*range(4))
-    scatter = Scatter(at, sizes, count, scatter_refs)
-    gather = Gather(at, sizes, count, full, gather_sems)
-    store = Chunks([(swish_grad, swish_out), (query, query_out)], chunk, chunk_sems)
-    gain_out[...] = jnp.zeros(gain_out.shape, jnp.float32)
-    key_acc[...] = jnp.zeros(key_acc.shape, jnp.float32)
-    value_acc[...] = jnp.zeros(value_acc.shape, jnp.float32)
-    loads.wait(0, 1, 2, 3)
-    tile = 512
-
-    def stores(k):
-        copies = []
-        for q in range(levels):
-            for c in range(2):
-                rows = pl.ds(pl.multiple_of(k * chunk + (2 * q + c) * piece, piece), piece)
-                copies.append(
-                    pltpu.make_async_copy(full.at[k, q, c], branch_out.at[rows], store_sems.at[2 * q + c, k])
-                )
-        return copies
-
-    def first(k):
-        scatter.free(k)
-        where = span(k, chunk)
+        up_grad[where, :] = lowered(back * active)
+        two.free(k)
         for column in range(0, width, tile):
             columns = slice(column, column + tile)
             value = inner_rows(gate_grad[where, :], gate_w[columns, :])
             value += inner_rows(up_grad[where, :], up_w[columns, :])
-            scatter.part[lax.rem(k, 2), :, :, :, columns] = lowered(value).reshape(levels, 2, piece, tile)
-        scatter.start(k)
-
-    def weigh(k):
-        columns = span(k, chunk)
-        rows = normed_mid[:, columns]
-        gate_total[columns, :] = lowered(inner_cols(rows, gate_grad[...]))
-        up_total[columns, :] = lowered(inner_cols(rows, up_grad[...]))
-
-    def norm(k):
-        scatter.finish(k)
+            two.part[lax.rem(k, 2), :, :, :, columns] = lowered(value).reshape(levels, 2, piece, tile)
+        two.start(k)
+
+    def branch_norm(k):
+        two.finish(k)
 
         def block(number, carry):
             sub = span(number, 16)
             where = pl.ds(pl.multiple_of(k * piece + number * 16, 16), 16)
             unit, scale = layer_norm(resid[where, :], EPSILON)
-            grad = scatter.total[sub, :]
+            grad = total[sub, :]
             outer = grad * unit
             gain_out[...] += outer[:8] + outer[8:]
-            value = wide(dy_rows[where, :]) + norm_back(grad * gain[...], unit, scale)
-            full[k, level, core, sub, :] = lowered(value)
+            mine = pl.ds(pl.multiple_of(place * piece + number * 16, 16), 16)
+            upstream = jnp.concatenate(
+                [dy[k, q, c, mine, :] for q in range(levels) for c in range(2)], axis=1
+            )
+            value = wide(upstream) + norm_back(grad * gain[...], unit, scale)
+            branch[k, level, core, sub, :] = lowered(value)
             return carry
 
         lax.fori_loop(0, piece // 16, block, 0)
-        gather.start(k)
+        branch_gather.start(k)
 
     def last(k):
-        gather.ready(k)
-        for copy in stores(k):
+        branch_gather.ready(k)
+        for copy in branch_stores(k):
             copy.start()
-        rows = full[k].reshape(chunk, width)
+        rows = branch[k].reshape(chunk, width)
         where = span(k, chunk)
+        slot = lax.rem(k, 2)
         grad = inner_rows(rows, out_w[...])
-        normed, scale = layer_norm(retained[where, :], GROUP_EPS)
-        value = swish[where, :]
+        retained_two.load(k).wait()
+        swish_two.load(k).wait()
+        normed, scale = layer_norm(retained_slots[slot], GROUP_EPS)
+        value = swish_slots[slot]
         gated = jax.nn.sigmoid(value)
-        swish_grad[where, :] = lowered(grad * normed * gated * (1.0 + value * (1.0 - gated)))
+        grad_ring.free(k)
+        grad_slots[slot] = lowered(grad * normed * gated * (1.0 + value * (1.0 - gated)))
+        grad_ring.store(k).start()
         delta[...] = lowered(norm_back(grad * value * gated, normed, scale))
+
+        @pl.when(k + 2 < count)
+        def _():
+            retained_two.load(k + 2).start()
+            swish_two.load(k + 2).start()
+
         query_acc[...] = jnp.zeros(query_acc.shape, jnp.float32)
 
         def block(j, carry):
@@ -1185,88 +1061,161 @@
 
         lax.fori_loop(0, k + 1, block, 0)
         query[where, :] = lowered(query_acc[...])
-        store.start(k)
-
-    lag = levels
-    tiles = width // chunk
+        query_ends.start(k)
+
+    def out_part(k):
+        three.free(k, one)
+        rows = hidden[span(k, chunk), :]
+        mine = pl.ds(pl.multiple_of(k * piece, piece), piece)
+        for rank in range(ranks):
+            columns = slice(rank * part_width, (rank + 1) * part_width)
+            value = matmul(rows, down_w[:, columns])
+            for run in range(ranks):
+                held = jnp.where(place == run, resid[mine, columns], 0.0)
+                three.part[
+                    lax.rem(k, 2), rank // 2, rank % 2, :, run * part_width : (run + 1) * part_width
+                ] = lowered(value[run * piece : (run + 1) * piece, :] + held)
+        three.start(k)
+
+    def out_finish(k):
+        three.finish(k)
+        for run in range(ranks):
+            where = pl.ds(pl.multiple_of(k * chunk + run * piece, piece), piece)
+            mixed[where, :] = lowered(total[:, run * part_width : (run + 1) * part_width])
+
+    def weigh(which):
+        def part(k):
+            columns = span(k, chunk)
+            if which == 0:
+                down = jnp.zeros((hidden.shape[1], part_width), jnp.float32)
+                for j in range(count):
+                    down += inner_cols(hidden[j * chunk : (j + 1) * chunk, :], dy[j, k // 2, lax.rem(k, 2)])
+                there = pl.ds(pl.multiple_of(k * part_width, part_width), part_width)
+                down_grad[:, there] = lowered(down)
+            else:
+                target, source = ((gate_w, gate_grad), (up_w, up_grad))[which - 1]
+                rows = jnp.concatenate(
+                    [
+                        normed_mid[j, q, c, :, columns]
+                        for j in range(count)
+                        for q in range(levels)
+                        for c in range(2)
+                    ],
+                    axis=0,
+                )
+                target[columns, :] = lowered(inner_cols(rows, source[...]))
+
+        in_order(width // chunk, part)
+        swap.start(which)
+
+    lead = 2
+    mid_lag = lead + levels
+    turn_lag = mid_lag + levels - 1
+    branch_lag = turn_lag + levels
+    last_lag = branch_lag + levels - 1
+
+    def at_wave(number, lag, step):
+        @pl.when(within(number - lag, count))
+        def _():
+            step(number - lag)
 
     def wave(number):
-        @pl.when(number < count)
-        def _():
-            first(number)
-
+        at_wave(number, lead, first)
+        for gather, lag, scatter in ((branch_gather, branch_lag, two), (mid_gather, mid_lag, one)):
+            at_wave(number, lag + 1, scatter.sent)
+            for hop in range(levels - 1, 0, -1):
+                at_wave(number, lag + hop, functools.partial(hop_on, gather, hop))
+        at_wave(number, branch_lag, branch_norm)
+        at_wave(number, mid_lag, mid_norm)
+        at_wave(number, -1, next_dy)
         for hop in range(levels - 1, 0, -1):
-
-            @pl.when(within(number - lag - hop, count))
-            def _():
-                gather.hop(number - lag - hop, hop)
-
-        @pl.when(number == lag)
-        def _():
-            loads.wait(4, 5)
-
-        @pl.when(within(number - lag, count))
-        def _():
-            norm(number - lag)
-
-        @pl.when(within(number - 1, count))
-        def _():
-            scatter.join(number - 1)
-
-        scatter.steps(number - 1)
-
-        @pl.when(number == 2 * lag - 1)
-        def _():
-            loads.wait(7, 8, 9, 10, 11, 12)
-
-        @pl.when(within(number - 2 * lag + 1, count))
-        def _():
-            last(number - 2 * lag + 1)
-
-        @pl.when(number == 0)
-        def _():
-            loads.wait(6)
-
-        @pl.when(number < tiles // 2)
-        def _():
-            weigh(2 * number)
-            weigh(2 * number + 1)
-
-        for step, relayed in ((1, 0), (2, 1), (3, 2), (4, 3)):
+            at_wave(number, hop, functools.partial(hop_on, dy_gather, hop))
+        for scatter, lag in ((two, turn_lag), (one, lead)):
+            at_wave(number, lag + 1, scatter.join)
+            scatter.steps(number - lag - 1)
+        for step, relayed, started in ((1, (0,), (2,)), (3, (1,), (3,)), (5, (2,), ()), (7, (3,), ())):
 
             @pl.when(number == step)
             def _():
-                spread.relay(relayed)
-
-        @pl.when(number == 1)
-        def _():
-            swap.start(0)
-
-        @pl.when(number == tiles // 2)
-        def _():
-            swap.start(1, 2)
-
-        for step, relayed in ((5, 0), (7, 1), (9, 2)):
-
-            @pl.when(number == step)
+                spread.relay(*relayed)
+                spread.start(*started)
+
+        @pl.when(number == turn_lag)
+        def _():
+            spread.wait(1, 2, 3)
+
+        at_wave(number, turn_lag, turn)
+
+        @pl.when(number == turn_lag + 1)
+        def _():
+            retained_one.store(count - 2).wait()
+            retained_one.store(count - 1).wait()
+            for k in range(2):
+                retained_two.load(k).start()
+                swish_two.load(k).start()
+
+        @pl.when(number == turn_lag + count)
+        def _():
+            spread.drain(*range(4))
+
+        for step, which in ((0, 1), (1, 2), (2, 0)):
+
+            @pl.when(number == turn_lag + count + step)
             def _():
-                swap.relay(relayed)
-
-    in_order(count + 2 * lag - 1, wave)
+                weigh(which)
+
+        for step, which in ((2, 1), (4, 2), (6, 0)):
+
+            @pl.when(number == turn_lag + count + step)
+            def _():
+                swap.relay(which)
+
+        at_wave(number, last_lag, last)
+        at_wave(number, last_lag, out_part)
+        at_wave(number, last_lag + 1, three.join)
+        three.steps(number - last_lag - 1)
+        at_wave(number, last_lag + levels, out_finish)
+        for k in range(count):
+
+            @pl.when(number == last_lag + levels + k)
+            def _():
+                deal.start(k)
+
+            @pl.when(number == last_lag + levels + k + 2)
+            def _():
+                deal.relay(k)
+
+    def hop_on(gather, hop, k):
+        gather.hop(k, hop)
+
+    def next_dy(k):
+        @pl.when(k > 0)
+        def _():
+            dy_gather.start(k)
+
+    in_order(count + last_lag + levels, wave)
+    deal.relay(count - 2, count - 1)
     keys[...] = lowered(key_acc[...])
     values[...] = lowered(value_acc[...])
     ends = Moves([(keys, key_out), (values, value_out)], end_sems)
     ends.start(0, 1)
-    spread.wait(*range(4))
     swap.wait(0, 1, 2)
-    spread.drain(*range(4))
-    scatter.drain()
-    gather.drain()
-    store.wait(count)
+    deal.wait(*range(count))
+    deal.drain(*range(count))
+    two.across(count - 2).wait_send()
+    two.across(count - 1).wait_send()
+    three.drain()
+    mid_gather.drain()
+    dy_gather.drain()
+    branch_gather.drain()
     ends.wait(0, 1)
+    query_ends.wait(count)
+    for k in (count - 2, count - 1):
+        mixed_in_ring.store(k).wait()
+        grad_ring.store(k).wait()
 
     def stored(k):
-        for copy in stores(k):
+        for copy in branch_stores(k):
             copy.wait()
 
     in_order(count, stored)
@@ -1510,7 +1459,7 @@
         out_specs=[places[inside] for inside, _ in outs],
         scratch_shapes=scratch,
         compiler_params=pltpu.CompilerParams(
-            collective_id=number, has_side_effects=True, vmem_limit_bytes=60 * 2**20
+            collective_id=number, has_side_effects=True, vmem_limit_bytes=63 * 2**20
         ),
     )(*[array for _, array in ins])
 
@@ -1605,14 +1554,14 @@
         key_w,
         value_w,
         swish_w,
-        out_w,
+        dy_all,
         x_rows,
         unit_share,
         scale_one,
     ) = kernel_call(
         functools.partial(open_kernel, sizes),
         1,
-        [("any", x_part.reshape(count, chunk, slice_width)), ("vmem", wide_one)] + anywhere(low[:5]),
+        [("any", x_part.reshape(count, chunk, slice_width)), ("vmem", wide_one)] + anywhere(low[:4] + [cotangent]),
         anywhere(
             [
                 struct((rows_dev, width)),
@@ -1621,7 +1570,8 @@
                 struct((rows_dev, v_dim)),
                 struct((rows_dev, v_dim), f32),
             ]
-            + full_w[:5]
+            + full_w[:4]
+            + [spread_shape(cotangent, 0, sizes)]
         )
         + [
             ("vmem", struct((own, width))),
@@ -1629,7 +1579,7 @@
             ("vmem", struct((rows_dev, 128), f32)),
         ],
         Gather.scratch(count, sizes, (chunk, slice_width))
-        + Spread.scratch(5, sizes)
+        + Spread.scratch(8, sizes)
         + held_like(full_w[:4])
         + [
             VMEM((rows_dev, width), jnp.bfloat16),
@@ -1641,142 +1591,83 @@
             DMA((4,)),
             DMA((5,)),
             DMA((count,)),
-            VMEM(w_out.shape, jnp.bfloat16),
+            VMEM(cotangent.shape, jnp.bfloat16),
         ],
     )
     rate = jnp.log1p(-jnp.exp2(-5.0 - place.astype(f32))).reshape(1)
-    middle_ins = (query, keys, values, swish_in, out_w, x_rows)
-    normed_mid, gate, up_proj, hidden, resid, retained, mixed_in, gate_w, up_w, down_w, dy_all = kernel_call(
-        functools.partial(middle_kernel, sizes),
+    dy_part = pick(source, dy_all)
+    by_rows = (PIECE, width)
+    bf16 = jnp.bfloat16
+    (
+        mixed_in,
+        _,
+        delta_branch,
+        delta_swish,
+        delta_query,
+        delta_keys,
+        delta_values,
+        gain_two_part,
+        mixed_all,
+        *ff_grads,
+    ) = kernel_call(
+        functools.partial(core_kernel, sizes),
         2,
         [("smem", dealt_start), ("smem", rate), ("vmem", wide_two)]
-        + anywhere(middle_ins)
-        + anywhere(low[5:] + [cotangent]),
+        + anywhere((query, keys, values, x_rows, dy_part.reshape(count, chunk, slice_width), swish_in))
+        + anywhere(low[4:]),
         anywhere(
             [
+                struct((rows_dev, v_dim)),
+                struct((rows_dev, v_dim), f32),
                 struct((rows_dev, width)),
-                struct((rows_dev, ff_dim), f32),
-                struct((rows_dev, ff_dim), f32),
-                struct((rows_dev, ff_dim)),
-                struct((own, width), f32),
-                struct((rows_dev, v_dim), f32),
+                struct((rows_dev, v_dim)),
+                struct((rows_dev, qk_dim)),
+                struct((rows_dev, qk_dim)),
                 struct((rows_dev, v_dim)),
             ]
-            + full_w[5:]
-            + [spread_shape(cotangent, 0, sizes)]
-        ),
-        held_like(middle_ins)
-        + Scatter.scratch(count, sizes, (PIECE, width))
-        + Gather.scratch(count, sizes, (PIECE, width))
-        + Spread.scratch(7, sizes)
-        + held_like(full_w[5:7])
-        + [
-            VMEM((rows_dev, ff_dim), f32),
-            VMEM((rows_dev, ff_dim), f32),
-            VMEM((rows_dev, ff_dim), jnp.bfloat16),
-            VMEM((own, width), f32),
-            VMEM((rows_dev, v_dim), f32),
-            VMEM((rows_dev, v_dim), jnp.bfloat16),
-            DMA((8,)),
-            DMA((5, count)),
-            DMA((ranks, count)),
-            DMA((2,)),
-            DMA,
-        ]
-        + held_like((low[7], cotangent)),
-    )
-    dy_part = pick(source, dy_all)
-    feed_ins = (hidden, down_w, resid, gate, up_proj)
-    mixed_share, delta_gate, delta_up, dy_rows, grad_down = kernel_call(
-        functools.partial(feed_kernel, sizes),
-        3,
-        anywhere((dy_part.reshape(count, chunk, slice_width),) + feed_ins),
-        anywhere(
+        )
+        + [("vmem", struct((8, width), f32))]
+        + anywhere(
             [
-                struct((rows_dev, slice_width)),
-                struct((rows_dev, ff_dim)),
-                struct((rows_dev, ff_dim)),
-                struct((own, width)),
-                struct((ff_dim, width)),
+                struct((sizes[0] * rows_dev, slice_width)),
+                swap_shape(full_w[7], 1, sizes),
+                swap_shape(full_w[5], 0, sizes),
+                swap_shape(full_w[6], 0, sizes),
             ]
         ),
-        held_like(feed_ins)
-        + Scatter.scratch(count, sizes, (chunk, slice_width))
+        held_like((query, keys, values, x_rows))
+        + held_like(full_w[4:])
+        + Scatter.rooms(count, sizes, by_rows)
+        + Scatter.rooms(count, sizes, by_rows)[:1]
+        + Scatter.sems(count, sizes) * 3
+        + Gather.scratch(count, sizes, by_rows)
         + Gather.scratch(count, sizes, (chunk, slice_width))
+        + Gather.scratch(count, sizes, by_rows)
+        + Spread.scratch(4, sizes)
+        + Spread.scratch(count, sizes)
+        + Swap.scratch(3, sizes)
         + [
-            VMEM((chunk, slice_width), f32),
-            VMEM((ff_dim, width), f32),
-            VMEM((ff_dim, width), jnp.bfloat16),
-            VMEM((rows_dev, slice_width), jnp.bfloat16),
-            VMEM((rows_dev, ff_dim), jnp.bfloat16),
-            VMEM((rows_dev, ff_dim), jnp.bfloat16),
-            VMEM((own, width), jnp.bfloat16),
-            DMA,
+            VMEM((rows_dev, ff_dim), bf16),
+            VMEM((rows_dev, ff_dim), bf16),
+            VMEM((rows_dev, ff_dim), bf16),
+            VMEM((own, width), f32),
+            VMEM((2, chunk, v_dim), f32),
+            VMEM((2, chunk, v_dim), f32),
+            VMEM((2, chunk, v_dim), bf16),
+            VMEM((2, chunk, v_dim), bf16),
+            VMEM((rows_dev, qk_dim), f32),
+            VMEM((rows_dev, v_dim), f32),
+            VMEM((chunk, qk_dim), f32),
+            VMEM((chunk, v_dim), bf16),
+            VMEM((ff_dim, width), bf16),
+            VMEM((rows_dev, slice_width), bf16),
             DMA((5,)),
-            DMA((3, count)),
+            DMA((6, count)),
+            DMA((ranks, count)),
+            DMA((1, count)),
             DMA((2,)),
-        ],
-    )
-    back_ins = (
-        delta_gate,
-        delta_up,
-        gate_w,
-        up_w,
-        resid,
-        dy_rows,
-        normed_mid,
-        out_w,
-        retained,
-        swish_in,
-        query,
-        keys,
-        values,
-    )
-    delta_branch, delta_swish, delta_query, delta_keys, delta_values, gain_two_part, mixed_all, *ff_grads = (
-        kernel_call(
-            functools.partial(back_kernel, sizes),
-            4,
-            [("smem", dealt_start), ("smem", rate), ("vmem", wide_two)]
-            + anywhere(back_ins)
-            + anywhere((mixed_share, grad_down)),
-            anywhere(
-                [
-                    struct((rows_dev, width)),
-                    struct((rows_dev, v_dim)),
-                    struct((rows_dev, qk_dim)),
-                    struct((rows_dev, qk_dim)),
-                    struct((rows_dev, v_dim)),
-                ]
-            )
-            + [("vmem", struct((8, width), f32))]
-            + anywhere(
-                [
-                    spread_shape(mixed_share, 0, sizes),
-                    swap_shape(full_w[7], 1, sizes),
-                    swap_shape(full_w[5], 0, sizes),
-                    swap_shape(full_w[6], 0, sizes),
-                ]
-            ),
-            held_like(back_ins)
-            + Scatter.scratch(count, sizes, (PIECE, width))
-            + Gather.scratch(count, sizes, (PIECE, width))
-            + Spread.scratch(4, sizes)
-            + Swap.scratch(3, sizes)
-            + held_like(full_w[5:7])
-            + [
-                VMEM((rows_dev, v_dim), jnp.bfloat16),
-                VMEM((chunk, v_dim), jnp.bfloat16),
-                VMEM((chunk, qk_dim), f32),
-                VMEM((rows_dev, qk_dim), f32),
-                VMEM((rows_dev, v_dim), f32),
-                DMA((15,)),
-                DMA((2, count)),
-                DMA((ranks, count)),
-                DMA((2,)),
-            ]
-            + held_like((mixed_share, grad_down))
-            + half_blocks([(full_w[7], 1), (full_w[5], 0), (full_w[6], 0)], sizes),
-        )
+        ]
+        + half_blocks([(full_w[7], 1), (full_w[5], 0), (full_w[6], 0)], sizes),
     )
     close_ins = (
         delta_query,
@@ -1796,7 +1687,7 @@
     swaps = len(SWAP_AXES)
     grad_all, gains, *attn_grads = kernel_call(
         functools.partial(close_kernel, sizes),
-        5,
+        3,
         [("vmem", wide_one), ("vmem", gain_two_part)] + anywhere(close_ins),
         anywhere([struct((sizes[0] * rows_dev, slice_width))])
         + [("vmem", struct((8, gain_attn.shape[0]), f32))]

time: 590 us -> 555 us (0.941)
  Pallas kernels: 543 us -> 509 us
    pallas_call x6 -> x4, Pallas kernels: 543 us -> 509 us  [kernel_call(): pl.pallas_call(body, out_shape=[shape for _, shape in outs], in_specs=[pl...]
where the time goes in v4:
time: 555 us; the launch traced here: 554 us
  Pallas kernels  509 us (92%)
  local copies, waits for them, and re-layouts  28.9 us (5%)
  other arithmetic  15.8 us (3%)
    pallas_call x4, Pallas kernels, kernel_call(): pl.pallas_call(body, out_shape=[shape for _, shape in outs], in_specs=[pl...  509 us
    gather x4, local copies, waits for them, and re-layouts, pick(): return whole.at[rows].get(mode='promise_in_bounds')  26 us

profile of v4, /device:TPU:0, one launch (start us, length us, event | category | flops | bytes accessed | tf_op | source)
XLA Modules:
  0.0 554.1 jit_solution(89705635782812506)
XLA Ops:
  0.6 0.7 dynamic_slice.3
  1.4 0.8 reduce-window.17
  2.2 0.7 bitcast_subtract_fusion
  2.9 0.9 select_reduce_fusion.5
  3.7 0.2 reduce-window.16
  3.9 0.0 copy-start.6
  3.9 0.1 convert_reduce_fusion.9
  4.0 0.1 select_reduce_fusion.1
  4.2 1.3 select_maximum_fusion.gains
  5.5 31.6 %shard_map.229 = (bf16[6144,256]{1,0:T(8,128)(2,1)}, f32[32,512]{1,0:T(8,128)}, bf16[512,256]{1,0:T(8,128)(2,1)}, bf16[512,256]{1,0:T(8,128)(2,1)}, bf16[512,512...) custom-call(bf16[1536,256]{1,0:T(8,128)(2,1)} %tokens.1, ...), custom_call_target="tpu_custom_call" | custom-call | tf_op jit(solution)/shard_map/pallas_call | solution.py:1455
  37.1 0.0 copy-done.6
  37.1 0.0 copy-start.5
  37.1 6.8 %gather_fusion = bf16[1536,256]{1,0:T(8,128)(2,1)} fusion(bf16[6144,256]{1,0:T(8,128)(2,1)} %get-tuple-element.54, s32[2048]{0:T(1024)S(1)} %pad_clamp_fusion.1), kind=kCustom, calls=%fused_computation | custom fusion | bytes 1579008 | tf_op jit(solution)/shard_map/gather | solution.py:1488
  43.9 0.0 copy-done.5
  43.9 0.6 fusion.6
  44.5 92.3 %shard_map.230 = (bf16[1536,2048]{1,0:T(8,128)(2,1)}, bf16[1536,256]{1,0:T(8,128)(2,1)}, bf16[1536,256]{1,0:T(8,128)(2,1)}, bf16[1536,512]{1,0:T(8,128)(2,1)}, f...) custom-call(bf16[6,256,256]{2,1,0:T(8,128)(2,1)} %bitcast.20, ...), custom_call_target="tpu_custom_call" | custom-call | tf_op jit(solution)/shard_map/pallas_call | solution.py:1455
  136.8 6.8 %gather_fusion.1 = bf16[1536,256]{1,0:T(8,128)(2,1)} fusion(bf16[6144,256]{1,0:T(8,128)(2,1)} %get-tuple-element.63, s32[2048]{0:T(1024)S(1)} %pad_clamp_fusion.1), kind=kCustom, calls=%fused_computation.1 | custom fusion | bytes 1579008 | tf_op jit(solution)/shard_map/gather | solution.py:1488
  143.7 274.1 %shard_map.231 = (bf16[1536,512]{1,0:T(8,128)(2,1)}, f32[1536,512]{1,0:T(8,128)}, bf16[1536,2048]{1,0:T(8,128)(2,1)}, bf16[1536,512]{1,0:T(8,128)(2,1)}, bf16[15...) custom-call(s32[3]{0:T(128)} %copy-done.6, ...), custom_call_target="tpu_custom_call" | custom-call | tf_op jit(solution)/shard_map/pallas_call | solution.py:1455
  417.9 3.9 convert_reduce_fusion
  421.8 110.5 %shard_map.232 = (bf16[6144,256]{1,0:T(8,128)(2,1)}, f32[8,512]{1,0:T(8,128)}, bf16[3,512,256]{2,1,0:T(8,128)(2,1)}, bf16[3,512,256]{2,1,0:T(8,128)(2,1)}, bf16[...) custom-call(f32[1,2048]{1,0:T(1,128)} %bitcast.22, ...), custom_call_target="tpu_custom_call" | custom-call | tf_op jit(solution)/shard_map/pallas_call | solution.py:1455
  532.4 0.0 copy-start.1
  532.4 0.0 copy-start.2
  532.4 4.1 convert_reduce_fusion.3
  536.4 0.0 copy-done.1
  536.4 0.0 copy-done.2
  536.4 0.0 copy-start.3
  536.4 0.0 copy-start.4
  536.4 1.8 convert_reduce_fusion.2
  538.3 0.0 copy-start.7
  538.3 0.0 copy-start.8
  538.3 0.0 copy-done.3
  538.3 0.0 copy-done.4
  538.3 1.2 convert_reduce_fusion.6
  539.5 0.0 copy-done.7
  539.5 0.0 copy-done.8
  539.5 0.2 select_reduce_fusion.4
  539.6 0.1 reshape.188
  539.7 0.2 reduce_window_sum.27
  539.9 0.1 reduce_window_sum.28
  540.0 0.1 select_reduce_fusion.2
  540.1 0.1 convert_reduce_fusion.8
  540.3 0.1 select_reduce_fusion
  540.4 0.0 copy-start
  540.4 7.0 %gather_fusion.3 = bf16[1536,256]{1,0:T(8,128)(2,1)} fusion(bf16[6144,256]{1,0:T(8,128)(2,1)} %get-tuple-element.84, s32[2048]{0:T(1024)S(1)} %pad_clamp_fusion), kind=kCustom, calls=%fused_computation.3 | custom fusion | bytes 1579008 | tf_op jit(solution)/shard_map/gather | solution.py:1488
  547.4 1.4 fusion.7
  548.8 0.0 copy-done
  548.8 5.4 gather_fusion.2
  (10 shorter events, 0.1 us)
Async XLA Ops:
  3.9 33.1 %copy-start.6 = (s32[3]{0:T(128)}, s32[3]{0:T(128)S(1)}, u32[]{:S(2)}) copy-start(s32[3]{0:T(128)S(1)} %get-tuple-element.99.bounds) | copy-start | bytes 40
  37.1 6.9 %copy-start.5 = (f32[32,512]{1,0:T(8,128)S(1)}, f32[32,512]{1,0:T(8,128)}, u32[]{:S(2)}) copy-start(f32[32,512]{1,0:T(8,128)} %get-tuple-element.53) | copy-start | bytes 196612
  532.4 4.1 copy-start.1
  532.4 4.1 copy-start.2
  536.4 1.8 copy-start.3
  536.4 1.8 copy-start.4
  538.3 1.2 copy-start.7
  538.3 1.2 copy-start.8
  540.4 8.4 %copy-start = (bf16[6144,256]{1,0:T(8,128)(2,1)S(1)}, bf16[6144,256]{1,0:T(8,128)(2,1)}, u32[]{:S(2)}) copy-start(bf16[6144,256]{1,0:T(8,128)(2,1)} %get-tuple-element.69) | copy-start | bytes 9437188

commit v5 on v4

--- a/solution.py
+++ b/solution.py
@@ -105,7 +105,7 @@
 
     def place(self, number, owner, half=None):
         source, target, axis, *where = self.items[number]
-        rows, columns = source.shape
+        rows = source.shape[0]
         size = source.shape[axis]
         step, offset = where or (size, 0)
         start = owner * step + offset
@@ -663,72 +663,97 @@
     return [(source.at[pl.ds(k * run, run)], target, 0, rows, k * run) for k in range(4)]
 
 
-def deal_kernel(sizes, tokens, gains, *refs):
+def pick_rows(whole, number, first, rows, bounds, shifts, begins):
+    window = 2 * rows
+    lane = lax.broadcasted_iota(jnp.int32, (rows, window), 1)
+    slot = jnp.zeros((rows, 1), jnp.int32)
+    own = first + lax.broadcasted_iota(jnp.int32, (rows, 1), 0)
+    for item in range(1, SEQ_DEV):
+        slot += (own >= bounds[item]).astype(jnp.int32)
+    chosen, windows = [], []
+    for item in range(SEQ_DEV):
+        start = begins[number * SEQ_DEV + item]
+        wanted = jnp.where(slot == item, own + shifts[item] - 16 * start, -1)
+        chosen.append(jnp.where(lane == wanted, 1.0, 0.0).astype(jnp.bfloat16))
+        windows += [whole[start + k] for k in range(window // 16)]
+    return lowered(matmul(jnp.concatenate(chosen, axis=1), jnp.concatenate(windows, axis=0)))
+
+
+def front_kernel(sizes, bounds, shifts, begins, tokens, cotangent, gain_rows, *refs):
     masters, refs = refs[:8], refs[8:]
-    tokens_out, gains_out, *refs = refs
-    rounded_out, refs = refs[:8], refs[8:]
-    spread_sems, refs = refs[:3], refs[3:]
-    small_sems, refs = refs[:3], refs[3:]
-    held, refs = refs[:8], refs[8:]
-    rounded, refs = refs[:8], refs[8:]
-    load_sems, store_sems, tokens_held, gains_held = refs
-    at = around(AXES)
-    loads = Moves(list(zip(masters, held)) + [(tokens, tokens_held), (gains, gains_held)], load_sems)
-    stores = Moves(list(zip(rounded, rounded_out)), store_sems)
-    loads.start(8, 9, *range(8))
-    greet(plane_peers(at, sizes))
-    loads.wait(8, 9)
-    spread = Spread(at, sizes, quarters(tokens_held, tokens_out), spread_sems)
-    small = Spread(at, sizes, [(gains_held, gains_out, 0)], small_sems, relay=False)
-    spread.start(*range(4))
-    small.start(0)
-    for number in range(8):
-        loads.wait(number)
-
-        def block(k):
-            rows = span(k, 32)
-            rounded[number][rows, :] = lowered(held[number][rows, :])
-
-        in_order(held[number].shape[0] // 32, block)
-        stores.start(number)
-    for number in range(4):
-        spread.relay(number)
-    stores.wait(*range(8))
-    small.wait(0)
-    spread.wait(*range(4))
-    small.drain(0)
-    spread.drain(*range(4))
-
-
-def open_kernel(sizes, shards, gain, *refs):
-    x_part, gain, *refs = (shards, gain) + refs
-    sources, refs = refs[:5], refs[5:]
-    normed_out, query_out, key_out, value_out, swish_out, *refs = refs
-    weight_outs, dy_out, refs = refs[:4], refs[4], refs[5:]
-    rows_out, unit_out, scale_out, *refs = refs
+    normed_out, query_out, key_out, value_out, swish_out, dy_out, *refs = refs
+    weight_outs, rounded_outs, refs = refs[:4], refs[4:8], refs[8:]
+    gain_one, gain_two, rows_out, unit_out, scale_out, *refs = refs
     full, *refs = refs
     gather_sems, refs = refs[:6], refs[6:]
-    spread_sems, refs = refs[:3], refs[3:]
-    weights, refs = refs[:4], refs[4:]
-    normed, query, keys, values, swish, load_sem, out_sem, weight_sem, normed_sem, shard = refs
+    spread_sems, small_sems, refs = refs[:3], refs[3:6], refs[6:]
+    held, rounded, weights, refs = refs[:8], refs[8:16], refs[16:20], refs[20:]
+    tokens_held, dy_held, gains_held, tokens_all, dy_all, gains_all, dy_part, *refs = refs
+    normed, query, keys, values, swish, load_sems, store_sems, out_sems, normed_sem = refs
     at = around(AXES)
     group, level, core = at
     place = 2 * level + core
     count, levels, _, chunk, width = full.shape
     ranks = 2 * levels
-    load = pltpu.make_async_copy(x_part, full.at[:, level, core], load_sem)
-    load.start()
-    load_shard = pltpu.make_async_copy(sources[4], shard, weight_sem.at[4])
-    load_shard.start()
+    piece = chunk // ranks
+    loads = Moves(
+        list(zip(masters, held)) + [(tokens, tokens_held), (gain_rows, gains_held), (cotangent, dy_held)], load_sems
+    )
+    loads.start(8, 9, 2, 3, 1, 0, 10, 4, 5, 6, 7)
     greet(plane_peers(at, sizes) + column_peers(at, sizes))
-    items = [(s, t, 0) for s, t in zip(sources[:4], weights)] + quarters(shard, dy_out)
-    spread = Spread(at, sizes, items, spread_sems)
+    loads.wait(8, 9)
+    spread = Spread(
+        at,
+        sizes,
+        quarters(tokens_held, tokens_all)
+        + [(rounded[2], weights[2], 0), (rounded[3], weights[3], 0)]
+        + quarters(dy_held, dy_all)
+        + [(rounded[1], weights[1], 0), (rounded[0], weights[0], 0)],
+        spread_sems,
+    )
+    small = Spread(at, sizes, [(gains_held, gains_all, 0)], small_sems, relay=False)
+    spread.start(*range(4))
+    small.start(0)
     gather = Gather(at, sizes, count, full, gather_sems)
-    load.wait()
-    gather.start(0)
-    load_shard.wait()
-    spread.start(0, 1, 2)
-    piece = chunk // ranks
+
+    def cast(number):
+        loads.wait(number)
+        rows = min(32, held[number].shape[0])
+
+        def block(k):
+            held_rows = span(k, rows)
+            rounded[number][held_rows, :] = lowered(held[number][held_rows, :])
+
+        in_order(held[number].shape[0] // rows, block)
+
+    stores = Moves(list(zip(rounded[4:], rounded_outs)), store_sems)
+    cast(2)
+    spread.start(4)
+    for number in (3, 1, 0, 4, 5, 6, 7):
+        cast(number)
+    loads.wait(10)
+    stores.start(*range(4))
+    for number in range(4):
+        spread.relay(number)
+    spread.start(5, 6, 7)
+    small.wait(0)
+    own = gains_held.shape[0]
+    for row, gain in enumerate((gain_one, gain_two)):
+        gain[...] = wide(
+            lowered(
+                jnp.concatenate([gains_all[own * k + row : own * k + row + 1, :] for k in range(sizes[0])], axis=1)
+            )
+        )
+    spread.wait(*range(4))
+    run = chunk // 2
+
+    def pick_chunk(whole, k, half):
+        return pick_rows(whole, 2 * k + half, k * chunk + half * run, run, bounds, shifts, begins)
+
+    def begin(k):
+        for half in range(2):
+            full[k, level, core, half * run : (half + 1) * run, :] = pick_chunk(tokens_all, k, half)
+        gather.start(k)
 
     def norm(k):
         def block(number, carry):
@@ -738,7 +763,7 @@
             )
             unit, scale = layer_norm(value, EPSILON)
             where = pl.ds(pl.multiple_of(k * chunk + number * 16, 16), 16)
-            normed[where, :] = lowered(unit * gain[...])
+            normed[where, :] = lowered(unit * gain_one[...])
             mine = wide(full[k, level, core, rows, :])
             mean = jnp.mean(value, -1, keepdims=True)
             unit_out[where, :] = (mine - mean) * scale
@@ -754,10 +779,19 @@
             normed.at[span(k, chunk)], normed_out.at[span(k, chunk)], normed_sem.at[k]
         ).start()
 
+    begin(0)
+    outs = [(query, query_out), (keys, key_out), (values, value_out), (swish, swish_out)]
+    ends = Moves(outs + list(zip(weights, weight_outs)) + [(dy_part, dy_out)], out_sems)
+
+    def project_rows(number, k):
+        where = span(k, chunk)
+        target = outs[number][0]
+        target[where, :] = matmul(normed[where, :], weights[number][...]).astype(target.dtype)
+
     def wave(number):
         @pl.when(number + 1 < count)
         def _():
-            gather.start(number + 1)
+            begin(number + 1)
 
         for hop in range(levels - 1, 0, -1):
 
@@ -766,12 +800,11 @@
                 gather.hop(number - hop, hop)
 
         for step, relayed, started in (
-            (1, (0,), ()),
-            (2, (1,), (3,)),
-            (4, (2,), (4, 5)),
-            (6, (3,), (6, 7)),
-            (8, (4,), ()),
-            (9, (5,), ()),
+            (1, (4,), (8, 9)),
+            (3, (5,), (10, 11)),
+            (5, (6, 7), ()),
+            (6, (8, 9), ()),
+            (8, (10,), ()),
         ):
 
             @pl.when(number == step)
@@ -784,26 +817,44 @@
             gather.ready(number - levels)
             norm(number - levels)
 
+        @pl.when(number == levels + 3)
+        def _():
+            spread.wait(4)
+            ends.start(6)
+            for k in range(3):
+                project_rows(2, k)
+
+        @pl.when(number >= levels + 3)
+        def _():
+            project_rows(2, number - levels)
+
     in_order(count + levels, wave)
-    spread.relay(6)
-    outs = [(query, query_out), (keys, key_out), (values, value_out), (swish, swish_out)]
-    for number, (held, out) in enumerate(outs):
-        spread.wait(number)
-        pltpu.make_async_copy(weights[number], weight_outs[number], weight_sem.at[number]).start()
-
-        def rows(k):
-            where = span(k, chunk)
-            held[where, :] = matmul(normed[where, :], weights[number][...]).astype(held.dtype)
-
-        in_order(count, rows)
-        pltpu.make_async_copy(held, out, out_sem.at[number]).start()
-    spread.relay(7)
-    spread.wait(4, 5, 6, 7)
-    for number, (held, out) in enumerate(outs):
-        pltpu.make_async_copy(held, out, out_sem.at[number]).wait()
-        pltpu.make_async_copy(weights[number], weight_outs[number], weight_sem.at[number]).wait()
-    spread.drain(*range(8))
+
+    def project(number, item):
+        if item is not None:
+            spread.wait(item)
+            ends.start(4 + number)
+            in_order(count, functools.partial(project_rows, number))
+        ends.start(number)
+
+    spread.relay(11)
+    project(2, None)
+    project(3, 5)
+    spread.wait(*range(6, 10))
+
+    def dy_chunk(k):
+        for half in range(2):
+            dy_part[k, half * run : (half + 1) * run, :] = pick_chunk(dy_all, k, half)
+
+    in_order(count, dy_chunk)
+    ends.start(8)
+    project(1, 10)
+    project(0, 11)
+    small.drain(0)
+    spread.drain(*range(12))
     gather.drain()
+    stores.wait(*range(4))
+    ends.wait(*range(9))
 
     def stored(k):
         pltpu.make_async_copy(
@@ -900,7 +951,7 @@
     swap = Swap(
         at, sizes, [(down_grad, down_dst, 1), (gate_w, gate_dst, 0), (up_w, up_dst, 0)], swap_sems, halves
     )
-    spread.start(0, 1)
+    spread.start(0)
     one = Scatter(at, sizes, count, list(rooms) + list(sems_one))
     two = Scatter(at, sizes, count, [other_part] + list(rooms[1:]) + list(sems_two))
     three = Scatter(at, sizes, count, list(rooms) + list(sems_three))
@@ -1108,7 +1159,7 @@
         in_order(width // chunk, part)
         swap.start(which)
 
-    lead = 2
+    lead = 3
     mid_lag = lead + levels
     turn_lag = mid_lag + levels - 1
     branch_lag = turn_lag + levels
@@ -1133,7 +1184,7 @@
         for scatter, lag in ((two, turn_lag), (one, lead)):
             at_wave(number, lag + 1, scatter.join)
             scatter.steps(number - lag - 1)
-        for step, relayed, started in ((1, (0,), (2,)), (3, (1,), (3,)), (5, (2,), ()), (7, (3,), ())):
+        for step, relayed, started in ((1, (0,), (1, 2)), (4, (1,), (3,)), (6, (2,), ()), (8, (3,), ())):
 
             @pl.when(number == step)
             def _():
@@ -1244,7 +1295,7 @@
     count, ranks = sums.shape[1], 2 * levels
     rows_all = count * chunk
     loads = Moves(list(zip(ins, held)), load_sems)
-    loads.start(*range(13))
+    loads.start(8, 3, 4, 5, 6, 7, 0, 1, 2, 9, 10, 11, 12)
     greet(plane_peers(at, sizes) + column_all(at, sizes))
     swap = Swap(at, sizes, list(zip(grads, targets, SWAP_AXES)), swap_sems, halves)
     small = Swap(at, sizes, [(gains, gains_in, 1)], small_sems)
@@ -1255,7 +1306,6 @@
         spread_sems,
     )
     line_one[...] = jnp.zeros(line_one.shape, jnp.float32)
-    loads.wait(*range(9))
     mine = pl.ds(pl.multiple_of(place * width, width), width)
 
     def first(k):
@@ -1356,10 +1406,6 @@
         def _():
             first(number)
 
-        @pl.when(number == 0)
-        def _():
-            weigh(3)
-
         for step, which in ((1, 2), (2, 0), (3, 1)):
 
             @pl.when(number == step)
@@ -1400,6 +1446,9 @@
             def _():
                 swap.relay(relayed)
 
+    loads.wait(3, 8)
+    weigh(3)
+    loads.wait(0, 1, 2, 4, 5, 6, 7)
     in_order(count + lag, wave)
     for k in (count - 2, count - 1):
         spread.relay(k)
@@ -1518,8 +1567,6 @@
     dealt_start = jnp.cumsum(dealt_len) - dealt_len
     rows = jnp.arange(rows_dev, dtype=jnp.int32)
     seq_ids = jnp.sum((rows[:, None] >= dealt_start[None, :]).astype(jnp.int32), 1) - 1
-    member = seq_ids[:, None] == jnp.arange(SEQ_DEV, dtype=jnp.int32)[None, :]
-    source = jnp.sum(jnp.where(member, (home_start - dealt_start)[None, :], 0), 1) + rows
     sizes = (lax.axis_size("dp"), lax.axis_size("heads"))
     ranks = sizes[1] * lax.axis_size("tensor")
     chunk = ranks * PIECE
@@ -1531,37 +1578,37 @@
     masters = (w_query, w_key, w_value, w_swish, w_out, w_gate, w_up, w_down)
     axes = (0, 0, 0, 0, 1, 0, 0, 1)
     gain_rows = jnp.pad(jnp.stack([gain_attn, gain_mlp]), ((0, 6), (0, 0)))
+    shifts = home_start - dealt_start
+    firsts = jnp.arange(2 * count, dtype=jnp.int32) * (chunk // 2)
+    begins = jnp.clip(firsts[:, None] + shifts[None, :], 0, sizes[0] * rows_dev - chunk) // 16
+    bf16 = jnp.bfloat16
     rounded = [struct(w.shape) for w in masters]
-    x_all, gains_all, *low = kernel_call(
-        functools.partial(deal_kernel, sizes),
-        0,
-        anywhere((tokens, gain_rows) + masters),
-        anywhere([spread_shape(tokens, 0, sizes), spread_shape(gain_rows, 0, sizes)] + rounded),
-        Spread.scratch(4, sizes) + Spread.scratch(1, sizes) + held_like(masters) + held_like(rounded) + [DMA((10,)), DMA((8,))] + held_like((tokens, gain_rows)),
-    )
-    full_w = [spread_shape(w, a, sizes) for w, a in zip(low, axes)]
-    gains_all = wide(lowered(gains_all.reshape(sizes[0], 8, -1)))
-    wide_one = gains_all[:, 0].reshape(1, width)
-    wide_two = gains_all[:, 1].reshape(1, width)
-    x_part = pick(source, x_all)
+    full_w = [spread_shape(w, a, sizes) for w, a in zip(rounded, axes)]
+    by_runs = struct((rows_dev // 16, 16, slice_width))
+    every = spread_shape(by_runs, 0, sizes)
+    gains_all = struct((sizes[0] * 8, gain_rows.shape[1]), f32)
     (
         normed_in,
         query,
         keys,
         values,
         swish_in,
+        dy_part,
         query_w,
         key_w,
         value_w,
         swish_w,
-        dy_all,
+        *low,
+        wide_one,
+        wide_two,
         x_rows,
         unit_share,
         scale_one,
     ) = kernel_call(
-        functools.partial(open_kernel, sizes),
-        1,
-        [("any", x_part.reshape(count, chunk, slice_width)), ("vmem", wide_one)] + anywhere(low[:4] + [cotangent]),
+        functools.partial(front_kernel, sizes),
+        0,
+        [("smem", dealt_start), ("smem", shifts), ("smem", begins.reshape(-1))]
+        + anywhere((tokens.reshape(by_runs.shape), cotangent.reshape(by_runs.shape), gain_rows) + masters),
         anywhere(
             [
                 struct((rows_dev, width)),
@@ -1569,35 +1616,40 @@
                 struct((rows_dev, qk_dim)),
                 struct((rows_dev, v_dim)),
                 struct((rows_dev, v_dim), f32),
+                struct((count, chunk, slice_width)),
             ]
             + full_w[:4]
-            + [spread_shape(cotangent, 0, sizes)]
+            + rounded[4:]
         )
         + [
+            ("vmem", struct((1, width), f32)),
+            ("vmem", struct((1, width), f32)),
             ("vmem", struct((own, width))),
             ("vmem", struct((rows_dev, slice_width), f32)),
             ("vmem", struct((rows_dev, 128), f32)),
         ],
         Gather.scratch(count, sizes, (chunk, slice_width))
-        + Spread.scratch(8, sizes)
+        + Spread.scratch(12, sizes)
+        + Spread.scratch(1, sizes)
+        + held_like(masters)
+        + held_like(rounded)
         + held_like(full_w[:4])
+        + held_like((by_runs, by_runs, gain_rows, every, every, gains_all))
         + [
-            VMEM((rows_dev, width), jnp.bfloat16),
-            VMEM((rows_dev, qk_dim), jnp.bfloat16),
-            VMEM((rows_dev, qk_dim), jnp.bfloat16),
-            VMEM((rows_dev, v_dim), jnp.bfloat16),
+            VMEM((count, chunk, slice_width), bf16),
+            VMEM((rows_dev, width), bf16),
+            VMEM((rows_dev, qk_dim), bf16),
+            VMEM((rows_dev, qk_dim), bf16),
+            VMEM((rows_dev, v_dim), bf16),
             VMEM((rows_dev, v_dim), f32),
-            DMA,
+            DMA((11,)),
             DMA((4,)),
-            DMA((5,)),
+            DMA((9,)),
             DMA((count,)),
-            VMEM(cotangent.shape, jnp.bfloat16),
         ],
     )
     rate = jnp.log1p(-jnp.exp2(-5.0 - place.astype(f32))).reshape(1)
-    dy_part = pick(source, dy_all)
     by_rows = (PIECE, width)
-    bf16 = jnp.bfloat16
     (
         mixed_in,
         _,
@@ -1611,10 +1663,10 @@
         *ff_grads,
     ) = kernel_call(
         functools.partial(core_kernel, sizes),
-        2,
+        1,
         [("smem", dealt_start), ("smem", rate), ("vmem", wide_two)]
-        + anywhere((query, keys, values, x_rows, dy_part.reshape(count, chunk, slice_width), swish_in))
-        + anywhere(low[4:]),
+        + anywhere((query, keys, values, x_rows, dy_part, swish_in))
+        + anywhere(low),
         anywhere(
             [
                 struct((rows_dev, v_dim)),
@@ -1687,7 +1739,7 @@
     swaps = len(SWAP_AXES)
     grad_all, gains, *attn_grads = kernel_call(
         functools.partial(close_kernel, sizes),
-        3,
+        2,
         [("vmem", wide_one), ("vmem", gain_two_part)] + anywhere(close_ins),
         anywhere([struct((sizes[0] * rows_dev, slice_width))])
         + [("vmem", struct((8, gain_attn.shape[0]), f32))]

time: 555 us -> 522 us (0.941)
  Pallas kernels: 509 us -> 489 us
  local copies, waits for them, and re-layouts: 28.9 us -> 14.7 us
    pallas_call x4 -> x3, Pallas kernels: 509 us -> 489 us  [kernel_call(): pl.pallas_call(body, out_shape=[shape for _, shape in outs], in_specs=[pl...]
    gather x4 -> x2, local copies, waits for them, and re-layouts: 26 us -> 12.3 us  [pick(): return whole.at[rows].get(mode='promise_in_bounds')]
where the time goes in v5:
time: 522 us; the launch traced here: 521 us
  Pallas kernels  489 us (94%)
  other arithmetic  16.7 us (3%)
  local copies, waits for them, and re-layouts  14.7 us (3%)
    pallas_call x3, Pallas kernels, kernel_call(): pl.pallas_call(body, out_shape=[shape for _, shape in outs], in_specs=[pl...  489 us
    gather x2, local copies, waits for them, and re-layouts, pick(): return whole.at[rows].get(mode='promise_in_bounds')  12.3 us
    reduce_sum x4, other arithmetic, shards(): jnp.sum(wide(g), 0)  11 us

profile of v5, /device:TPU:0, one launch (start us, length us, event | category | flops | bytes accessed | tf_op | source)
XLA Modules:
  0.0 520.9 jit_solution(10515114772431400823)
XLA Ops:
  0.6 0.7 dynamic_slice.3
  1.4 0.8 reduce-window.17
  2.2 0.7 bitcast_subtract_fusion
  2.9 0.9 select_reduce_fusion.4
  3.7 0.2 reduce-window.16
  3.9 0.5 fusion.4
  4.4 0.0 copy-start.5
  4.4 0.1 add_clamp_fusion
  4.5 0.1 min.12
  4.6 0.5 and_select_fusion.1.begins
  5.1 1.3 select_maximum_fusion.gain_rows
  6.4 0.0 copy-done.5
  6.5 125.9 %shard_map.229 = (bf16[1536,2048]{1,0:T(8,128)(2,1)}, bf16[1536,256]{1,0:T(8,128)(2,1)}, bf16[1536,256]{1,0:T(8,128)(2,1)}, bf16[1536,512]{1,0:T(8,128)(2,1)}, f...) custom-call(s32[3]{0:T(128)} %get-tuple-element.91.bounds, ...), custom_call_target="tpu_custom_call" | custom-call | tf_op jit(solution)/shard_map/pallas_call | solution.py:1504
  132.4 255.5 %shard_map.230 = (bf16[1536,512]{1,0:T(8,128)(2,1)}, f32[1536,512]{1,0:T(8,128)}, bf16[1536,2048]{1,0:T(8,128)(2,1)}, bf16[1536,512]{1,0:T(8,128)(2,1)}, bf16[15...) custom-call(s32[3]{0:T(128)} %get-tuple-element.91.bounds, ...), custom_call_target="tpu_custom_call" | custom-call | tf_op jit(solution)/shard_map/pallas_call | solution.py:1504
  387.9 3.9 convert_reduce_fusion
  391.8 107.4 %shard_map.231 = (bf16[6144,256]{1,0:T(8,128)(2,1)}, f32[8,512]{1,0:T(8,128)}, bf16[3,512,256]{2,1,0:T(8,128)(2,1)}, bf16[3,512,256]{2,1,0:T(8,128)(2,1)}, bf16[...) custom-call(f32[1,2048]{1,0:T(1,128)} %get-tuple-element.61.gain, ...), custom_call_target="tpu_custom_call" | custom-call | tf_op jit(solution)/shard_map/pallas_call | solution.py:1504
  499.2 0.0 copy-start.1
  499.2 0.0 copy-start.2
  499.2 4.1 convert_reduce_fusion.3
  503.2 0.0 copy-done.1
  503.2 0.0 copy-done.2
  503.2 0.0 copy-start.3
  503.2 0.0 copy-start.4
  503.3 1.8 convert_reduce_fusion.2
  505.1 0.0 copy-start.6
  505.1 0.0 copy-start.7
  505.1 0.0 copy-done.3
  505.1 0.0 copy-done.4
  505.1 1.2 convert_reduce_fusion.6
  506.3 0.0 copy-done.6
  506.3 0.0 copy-done.7
  506.3 0.2 select_reduce_fusion.3
  506.5 0.1 reshape.167
  506.5 0.2 reduce_window_sum.27
  506.7 0.1 reduce_window_sum.28
  506.8 0.1 select_reduce_fusion.1
  506.9 0.1 convert_reduce_fusion.8
  507.1 0.1 select_reduce_fusion
  507.2 0.0 copy-start
  507.2 7.0 %gather_fusion.1 = bf16[1536,256]{1,0:T(8,128)(2,1)} fusion(bf16[6144,256]{1,0:T(8,128)(2,1)} %get-tuple-element.76, s32[2048]{0:T(1024)S(1)} %pad_clamp_fusion), kind=kCustom, calls=%fused_computation.1 | custom fusion | bytes 1579008 | tf_op jit(solution)/shard_map/gather | solution.py:1537
  514.2 1.4 fusion.5
  515.6 0.0 copy-done
  515.6 5.4 %gather_fusion = bf16[1536,256]{1,0:T(8,128)(2,1)} fusion(bf16[6144,256]{1,0:T(8,128)(2,1)S(1)} %copy-done, s32[2048]{0:T(1024)S(1)} %pad_clamp_fusion), kind=kCustom, calls=%fused_computation | custom fusion | bytes 1579008 | tf_op jit(solution)/shard_map/gather | solution.py:1537
  (6 shorter events, 0.1 us)
Async XLA Ops:
  4.4 2.0 copy-start.5
  499.2 4.1 copy-start.1
  499.2 4.1 copy-start.2
  503.2 1.8 copy-start.3
  503.2 1.8 copy-start.4
  505.1 1.2 copy-start.6
  505.1 1.2 copy-start.7
  507.2 8.4 %copy-start = (bf16[6144,256]{1,0:T(8,128)(2,1)S(1)}, bf16[6144,256]{1,0:T(8,128)(2,1)}, u32[]{:S(2)}) copy-start(bf16[6144,256]{1,0:T(8,128)(2,1)} %get-tuple-element.60) | copy-start | bytes 9437188

commit v6 on v5

--- a/solution.py
+++ b/solution.py
@@ -11,7 +11,6 @@
 SEQ_DEV = 3
 PIECE = 32
 AXES = ("dp", "heads", "tensor")
-SWAP_AXES = (0, 0, 0, 0, 1)
 MESH = pl.DeviceIdType.MESH
 
 
@@ -560,7 +559,7 @@
 
     def block(self, number, owner, half=None):
         source, target, axis = self.items[number]
-        rows, columns = source.shape
+        rows = source.shape[0]
         size = source.shape[axis] // self.count
         height = size if axis == 0 else rows
         begin = 0
@@ -633,6 +632,7 @@
                     self.across(number, way).wait_recv()
                     part = self.block(number, near[1 - way], way)
                     part[...] = lowered(wide(part[...]) + wide(self.halves[number][way]))
+                for way in range(2):
                     self.added(number, way).start()
 
     def wait(self, *numbers):
@@ -885,14 +885,18 @@
 
 
 def core_kernel(sizes, bounds, rate, gain, *refs):
+    gain_first, *refs = refs
     query_src, key_src, value_src, rows_src, dy_src, swish_src, *refs = refs
+    normed_src, unit_src, scale_src, *refs = refs
+    project_src, refs = refs[:4], refs[4:]
     shards, refs = refs[:4], refs[4:]
-    mixed_in_out, retained_out, branch_out, swish_out, query_out, key_out, value_out, *refs = refs
-    gain_out, mixed_dst, down_dst, gate_dst, up_dst, *refs = refs
+    mixed_in_out, retained_out, gains_out, *refs = refs
+    mixed_dst, grad_dst, down_dst, gate_dst, up_dst, *refs = refs
+    late_dst, refs = refs[:5], refs[5:]
     query, keys, values, x_rows, out_w, gate_w, up_w, down_w, *refs = refs
     rooms, refs = refs[:4], refs[4:]
     (other_part,), refs = refs[:1], refs[1:]
-    sems_one, sems_two, sems_three, refs = refs[:6], refs[6:12], refs[12:18], refs[18:]
+    sems_one, sems_two, sems_three, sems_four, refs = refs[:6], refs[6:12], refs[12:18], refs[18:24], refs[24:]
     normed_mid, refs = refs[0], refs[1:]
     normed_sems, refs = refs[:6], refs[6:]
     dy, refs = refs[0], refs[1:]
@@ -901,10 +905,12 @@
     branch_sems, refs = refs[:6], refs[6:]
     spread_sems, refs = refs[:3], refs[3:]
     deal_sems, refs = refs[:3], refs[3:]
-    swap_sems, refs = refs[:3], refs[3:]
-    hidden, gate_grad, up_grad, resid, swish_slots, retained_slots, mixed_in_slots, grad_slots, *refs = refs
-    key_acc, value_acc, query_acc, delta, down_grad, mixed, *refs = refs
-    load_sems, ring_sems, branch_store, query_store, end_sems, *halves = refs
+    swap_sems, late_sems, small_sems, refs = refs[:3], refs[3:6], refs[6:9], refs[9:]
+    give_sems, refs = refs[:3], refs[3:]
+    hidden, gate_grad, up_grad, resid, swish_slots, retained_slots, mixed_in_slots, *refs = refs
+    key_acc, value_acc, query_acc, delta, down_grad, mixed, gain_acc, *refs = refs
+    sums, line_one, packed, gains, gains_in, *refs = refs
+    load_sems, ring_sems, late_load, unit_sems, room, sums_sent, sums_got, gain_sent, gain_got, *halves = refs
     at = around(AXES)
     group, level, core = at
     place = 2 * level + core
@@ -928,11 +934,18 @@
     retained_one = Ring(retained_slots, retained_out, chunk, ring_sems.at[2])
     retained_two = Ring(retained_slots, retained_out, chunk, ring_sems.at[3])
     mixed_in_ring = Ring(mixed_in_slots, mixed_in_out, chunk, ring_sems.at[4])
-    grad_ring = Ring(grad_slots, swish_out, chunk, ring_sems.at[5])
-    query_ends = Chunks([(query, query_out)], chunk, query_store)
+    groups, v_dim = sizes[0], values.shape[1]
+    late_loads = Moves(
+        [(normed_src, normed_mid), (mixed_in_out, up_grad), (project_src[0], dy.at[0]), (project_src[1], dy.at[1])]
+        + [
+            (project_src[2 + n // 2].at[:, :, :, pl.ds(n % 2 * part_width, part_width)], dy.at[2 + n])
+            for n in range(4)
+        ],
+        late_load,
+    )
     swish_one.load(0).start()
     swish_one.load(1).start()
-    greet(plane_peers(at, sizes) + column_peers(at, sizes))
+    greet(plane_peers(at, sizes) + column_all(at, sizes))
     spread = Spread(
         at,
         sizes,
@@ -949,33 +962,49 @@
         deal_sems,
     )
     swap = Swap(
-        at, sizes, [(down_grad, down_dst, 1), (gate_w, gate_dst, 0), (up_w, up_dst, 0)], swap_sems, halves
+        at, sizes, [(down_grad, down_dst, 1), (gate_w, gate_dst, 0), (up_w, up_dst, 0)], swap_sems, halves[:3]
+    )
+    qk_dim = query.shape[1]
+    late = Swap(
+        at,
+        sizes,
+        [
+            (gate_w, late_dst[0], 0),
+            (out_w, late_dst[1], 1),
+            (up_w, late_dst[2], 0),
+            (down_grad.at[pl.ds(0, qk_dim)], late_dst[3], 1),
+            (down_grad.at[pl.ds(qk_dim, qk_dim)], late_dst[4], 1),
+        ],
+        late_sems,
+        [halves[1], halves[0], halves[2], halves[3], halves[4]],
+    )
+    small = Swap(at, sizes, [(gains, gains_in, 1)], small_sems)
+    give = Spread(
+        at,
+        sizes,
+        [
+            (hidden.at[pl.ds(k * chunk, chunk), pl.ds(0, part_width)], grad_dst, 0, count * chunk, k * chunk)
+            for k in range(count)
+        ],
+        give_sems,
     )
     spread.start(0)
     one = Scatter(at, sizes, count, list(rooms) + list(sems_one))
     two = Scatter(at, sizes, count, [other_part] + list(rooms[1:]) + list(sems_two))
     three = Scatter(at, sizes, count, list(rooms) + list(sems_three))
+    four = Scatter(at, sizes, count, [other_part] + list(rooms[1:]) + list(sems_four))
     total = rooms[3]
     mid_gather = Gather(at, sizes, count, normed_mid, normed_sems)
     dy_gather = Gather(at, sizes, count, dy, dy_sems)
     branch_gather = Gather(at, sizes, count, branch, branch_sems)
-    gain_out[...] = jnp.zeros(gain_out.shape, jnp.float32)
+    gain_acc[...] = jnp.zeros(gain_acc.shape, jnp.float32)
+    line_one[...] = jnp.zeros(line_one.shape, jnp.float32)
     key_acc[...] = jnp.zeros(key_acc.shape, jnp.float32)
     value_acc[...] = jnp.zeros(value_acc.shape, jnp.float32)
     loads.wait(0)
     dy_gather.start(0)
     loads.wait(1, 2, 3, 4)
     tile = 512
-
-    def branch_stores(k):
-        copies = []
-        for q in range(levels):
-            for c in range(2):
-                rows = pl.ds(pl.multiple_of(k * chunk + (2 * q + c) * piece, piece), piece)
-                copies.append(
-                    pltpu.make_async_copy(branch.at[k, q, c], branch_out.at[rows], branch_store.at[2 * q + c, k])
-                )
-        return copies
 
     def first(k):
         where = span(k, chunk)
@@ -1063,7 +1092,7 @@
             unit, scale = layer_norm(resid[where, :], EPSILON)
             grad = total[sub, :]
             outer = grad * unit
-            gain_out[...] += outer[:8] + outer[8:]
+            gain_acc[...] += outer[:8] + outer[8:]
             mine = pl.ds(pl.multiple_of(place * piece + number * 16, 16), 16)
             upstream = jnp.concatenate(
                 [dy[k, q, c, mine, :] for q in range(levels) for c in range(2)], axis=1
@@ -1077,8 +1106,6 @@
 
     def last(k):
         branch_gather.ready(k)
-        for copy in branch_stores(k):
-            copy.start()
         rows = branch[k].reshape(chunk, width)
         where = span(k, chunk)
         slot = lax.rem(k, 2)
@@ -1088,9 +1115,7 @@
         normed, scale = layer_norm(retained_slots[slot], GROUP_EPS)
         value = swish_slots[slot]
         gated = jax.nn.sigmoid(value)
-        grad_ring.free(k)
-        grad_slots[slot] = lowered(grad * normed * gated * (1.0 + value * (1.0 - gated)))
-        grad_ring.store(k).start()
+        gate_grad[where, :] = lowered(grad * normed * gated * (1.0 + value * (1.0 - gated)))
         delta[...] = lowered(norm_back(grad * value * gated, normed, scale))
 
         @pl.when(k + 2 < count)
@@ -1112,7 +1137,6 @@
 
         lax.fori_loop(0, k + 1, block, 0)
         query[where, :] = lowered(query_acc[...])
-        query_ends.start(k)
 
     def out_part(k):
         three.free(k, one)
@@ -1134,6 +1158,11 @@
             where = pl.ds(pl.multiple_of(k * chunk + run * piece, piece), piece)
             mixed[where, :] = lowered(total[:, run * part_width : (run + 1) * part_width])
 
+    def runs_of(ref, columns):
+        return jnp.concatenate(
+            [ref[j, q, c, :, columns] for j in range(count) for q in range(levels) for c in range(2)], axis=0
+        )
+
     def weigh(which):
         def part(k):
             columns = span(k, chunk)
@@ -1145,25 +1174,164 @@
                 down_grad[:, there] = lowered(down)
             else:
                 target, source = ((gate_w, gate_grad), (up_w, up_grad))[which - 1]
-                rows = jnp.concatenate(
-                    [
-                        normed_mid[j, q, c, :, columns]
-                        for j in range(count)
-                        for q in range(levels)
-                        for c in range(2)
-                    ],
-                    axis=0,
-                )
-                target[columns, :] = lowered(inner_cols(rows, source[...]))
+                target[columns, :] = lowered(inner_cols(runs_of(normed_mid, columns), source[...]))
 
         in_order(width // chunk, part)
         swap.start(which)
+
+    def weigh_late(which):
+        def part(k):
+            columns = span(k, chunk)
+            if which == 0:
+                gate_w[columns, :] = lowered(inner_cols(runs_of(normed_mid, columns), gate_grad[...]))
+            elif which == 1:
+                out_w[:, columns] = lowered(inner_cols(up_grad[...], runs_of(branch, columns)))
+            elif which == 2:
+                up_w[columns, :] = lowered(inner_cols(runs_of(normed_mid, columns), values[...]))
+            else:
+                rows = runs_of(normed_mid, columns)
+                down_grad[:qk_dim, columns] = lowered(inner_cols(query[...], rows))
+                down_grad[qk_dim:, columns] = lowered(inner_cols(keys[...], rows))
+
+        in_order(width // chunk, part)
+        late.start(*((which,) if which < 3 else (3, 4)))
+
+    def units(k):
+        slot = lax.rem(k, 2)
+        return [
+            pltpu.make_async_copy(
+                unit_src.at[span(k, chunk)], swish_slots.at[slot, :, pl.ds(0, part_width)], unit_sems.at[0, k]
+            ),
+            pltpu.make_async_copy(
+                scale_src.at[span(k, chunk)], retained_slots.at[slot, :, pl.ds(0, 128)], unit_sems.at[1, k]
+            ),
+        ]
+
+    def peer_of(j):
+        peer = lax.rem(place + j, ranks)
+        return (group, peer // 2, lax.rem(peer, 2))
+
+    def sender(j):
+        return lax.rem(place + ranks - j, ranks)
+
+    def sums_copy(k, j, owner):
+        return pltpu.make_async_remote_copy(
+            src_ref=sums.at[owner, k],
+            dst_ref=sums.at[owner, k],
+            send_sem=sums_sent.at[j - 1, k],
+            recv_sem=sums_got.at[j - 1, k],
+            device_id=peer_of(j),
+            device_id_type=MESH,
+        )
+
+    def pack_copy(j, owner):
+        return pltpu.make_async_remote_copy(
+            src_ref=packed.at[owner],
+            dst_ref=packed.at[owner],
+            send_sem=gain_sent.at[j - 1],
+            recv_sem=gain_got.at[j - 1],
+            device_id=peer_of(j),
+            device_id_type=MESH,
+        )
+
+    def make_room(k):
+        three.sent(k)
+        pl.semaphore_signal(room.at[0], inc=1, device_id=(group, level, 1 - core), device_id_type=MESH)
+
+        @pl.when(level > 0)
+        def _():
+            pl.semaphore_signal(room.at[1], inc=1, device_id=(group, level - 1, core), device_id_type=MESH)
+
+        @pl.when(level < levels - 1)
+        def _():
+            pl.semaphore_signal(room.at[2], inc=1, device_id=(group, level + 1, core), device_id_type=MESH)
+
+    def in_part(k):
+        four.free(k, two)
+        where = span(k, chunk)
+        slot = lax.rem(k, 2)
+        rows = [query[where, :], keys[where, :]]
+        for source in (values, gate_grad):
+            rows += [source[where, n : n + part_width] for n in range(0, v_dim, part_width)]
+        first_sum = jnp.zeros((chunk, part_width), jnp.float32)
+        second_sum = jnp.zeros((chunk, part_width), jnp.float32)
+        for rank in range(ranks):
+            columns = slice(rank * part_width, (rank + 1) * part_width)
+            value = inner_rows(rows[0], dy[0, rank // 2, rank % 2])
+            for n in range(1, len(rows)):
+                value += inner_rows(rows[n], dy[n, rank // 2, rank % 2])
+            for run in range(ranks):
+                four.part[
+                    slot, rank // 2, rank % 2, :, run * part_width : (run + 1) * part_width
+                ] = lowered(value[run * piece : (run + 1) * piece, :])
+            first_sum += value * gain_first[:, columns]
+            second_sum += value * wide(normed_mid[k, :, :, :, columns].reshape(chunk, part_width))
+        pl.semaphore_wait(room.at[0], 1)
+        four.start(k)
+        ones = jnp.ones((8, part_width), jnp.float32)
+        flat = [
+            lax.dot_general(
+                ones,
+                item,
+                (((1,), (1,)), ((), ())),
+                precision=lax.Precision.HIGHEST,
+                preferred_element_type=jnp.float32,
+            )
+            for item in (first_sum, second_sum)
+        ]
+        line = lax.broadcasted_iota(jnp.int32, (8, chunk), 0)
+        sums[place, k] = jnp.where(line == 0, flat[0], flat[1])
+        for j in range(1, ranks):
+            sums_copy(k, j, place).start()
+
+    def in_room(wave):
+        @pl.when(within(wave - level, count) & (level < levels - 1))
+        def _():
+            pl.semaphore_wait(room.at[1], 1)
+
+        @pl.when(within(wave - (levels - 1 - level), count) & (level > 0))
+        def _():
+            pl.semaphore_wait(room.at[2], 1)
+
+    def in_finish(k):
+        four.finish(k)
+        for j in range(1, ranks):
+            sums_copy(k, j, sender(j)).wait_recv()
+        line = lax.broadcasted_iota(jnp.int32, (8, 128), 0)
+        lane = lax.broadcasted_iota(jnp.int32, (8, 128), 1)
+        means = lax.dot_general(
+            jnp.sum(sums[:, k], 0),
+            jnp.where(line == lane, 1.0 / width, 0.0),
+            (((0,), (0,)), ((), ())),
+            precision=lax.Precision.HIGHEST,
+            preferred_element_type=jnp.float32,
+        )
+        slot = lax.rem(k, 2)
+        for copy in units(k):
+            copy.wait()
+        mine = pl.ds(pl.multiple_of(place * part_width, part_width), part_width)
+        value = jnp.concatenate(
+            [total[:, run * part_width : (run + 1) * part_width] for run in range(ranks)], axis=0
+        )
+        normed = swish_slots[slot, :, :part_width]
+        outer = value * normed
+        line_one[...] += jnp.sum(outer.reshape(chunk // 8, 8, part_width), 0)
+        back = value * gain_first[:, mine] - means[:, :1] - normed * means[:, 1:2]
+        upstream = wide(branch[k, :, :, :, mine].reshape(chunk, part_width))
+        hidden[span(k, chunk), :part_width] = lowered(upstream + retained_slots[slot, :, :1] * back)
+
+        @pl.when(k + 2 < count)
+        def _():
+            for copy in units(k + 2):
+                copy.start()
 
     lead = 3
     mid_lag = lead + levels
     turn_lag = mid_lag + levels - 1
     branch_lag = turn_lag + levels
     last_lag = branch_lag + levels - 1
+    turned = turn_lag + count
+    close_lag = last_lag + count
 
     def at_wave(number, lag, step):
         @pl.when(within(number - lag, count))
@@ -1205,21 +1373,33 @@
                 retained_two.load(k).start()
                 swish_two.load(k).start()
 
-        @pl.when(number == turn_lag + count)
+        @pl.when(number == turned)
         def _():
             spread.drain(*range(4))
 
         for step, which in ((0, 1), (1, 2), (2, 0)):
 
-            @pl.when(number == turn_lag + count + step)
+            @pl.when(number == turned + step)
             def _():
                 weigh(which)
 
         for step, which in ((2, 1), (4, 2), (6, 0)):
 
-            @pl.when(number == turn_lag + count + step)
+            @pl.when(number == turned + step)
             def _():
                 swap.relay(which)
+
+        @pl.when(number == turned + 2)
+        def _():
+            mid_gather.drain()
+            mixed_in_ring.store(count - 2).wait()
+            mixed_in_ring.store(count - 1).wait()
+            late_loads.start(0, 1)
+
+        @pl.when(number == branch_lag + count)
+        def _():
+            dy_gather.drain()
+            late_loads.start(*range(2, 8))
 
         at_wave(number, last_lag, last)
         at_wave(number, last_lag, out_part)
@@ -1236,6 +1416,46 @@
             def _():
                 deal.relay(k)
 
+        at_wave(number, last_lag + levels + 1, make_room)
+
+        @pl.when(number == close_lag)
+        def _():
+            keys[...] = lowered(key_acc[...])
+            values[...] = lowered(value_acc[...])
+            for k in range(2):
+                for copy in units(k):
+                    copy.start()
+            late_loads.wait(*range(8))
+
+        at_wave(number, close_lag, in_part)
+        for step, before, which in ((0, 1, 0), (1, 0, 1), (2, 2, 2), (3, None, 3)):
+
+            @pl.when(number == close_lag + step)
+            def _():
+                if before is not None:
+                    swap.wait(before)
+                weigh_late(which)
+
+        at_wave(number, close_lag + 1, four.join)
+        in_room(number - close_lag - 1)
+        four.steps(number - close_lag - 1)
+        at_wave(number, close_lag + levels, in_finish)
+        for step, which in ((3, (0,)), (4, (1,)), (5, (2,)), (7, (3, 4))):
+
+            @pl.when(number == close_lag + step)
+            def _():
+                late.relay(*which)
+
+        for k in range(count):
+
+            @pl.when(number == close_lag + levels + k)
+            def _():
+                give.start(k)
+
+            @pl.when(number == close_lag + levels + k + 2)
+            def _():
+                give.relay(k)
+
     def hop_on(gather, hop, k):
         gather.hop(k, hop)
 
@@ -1244,234 +1464,33 @@
         def _():
             dy_gather.start(k)
 
-    in_order(count + last_lag + levels, wave)
-    deal.relay(count - 2, count - 1)
-    keys[...] = lowered(key_acc[...])
-    values[...] = lowered(value_acc[...])
-    ends = Moves([(keys, key_out), (values, value_out)], end_sems)
-    ends.start(0, 1)
-    swap.wait(0, 1, 2)
-    deal.wait(*range(count))
-    deal.drain(*range(count))
-    two.across(count - 2).wait_send()
-    two.across(count - 1).wait_send()
-    three.drain()
-    mid_gather.drain()
-    dy_gather.drain()
-    branch_gather.drain()
-    ends.wait(0, 1)
-    query_ends.wait(count)
-    for k in (count - 2, count - 1):
-        mixed_in_ring.store(k).wait()
-        grad_ring.store(k).wait()
-
-    def stored(k):
-        for copy in branch_stores(k):
-            copy.wait()
-
-    in_order(count, stored)
-
-
-def close_kernel(sizes, gain, gain_two, *refs):
-    ins, refs = refs[:13], refs[13:]
-    grad_out, gains_out, *refs = refs
-    targets, refs = refs[:5], refs[5:]
-    held, refs = refs[:13], refs[13:]
-    deltas, weights = held[:4], held[4:8]
-    normed_in, branch, mixed_in, unit, scale = held[8:]
-    grads, refs = refs[:5], refs[5:]
-    scatter_refs, refs = refs[:10], refs[10:]
-    swap_sems, refs = refs[:3], refs[3:]
-    sums, line_one, share, packed, gains, gains_in, refs = *refs[:6], refs[6:]
-    load_sems, sums_sent, sums_got, gain_sent, gain_got, refs = *refs[:5], refs[5:]
-    spread_sems, refs = refs[:3], refs[3:]
-    small_sems, halves = refs[:3], refs[3:]
-    at = around(AXES)
-    group, level, core = at
-    place = 2 * level + core
-    groups = sizes[0]
-    scatter = Scatter(at, sizes, sums.shape[1], scatter_refs)
-    _, levels, _, chunk, width = scatter.part.shape
-    count, ranks = sums.shape[1], 2 * levels
-    rows_all = count * chunk
-    loads = Moves(list(zip(ins, held)), load_sems)
-    loads.start(8, 3, 4, 5, 6, 7, 0, 1, 2, 9, 10, 11, 12)
-    greet(plane_peers(at, sizes) + column_all(at, sizes))
-    swap = Swap(at, sizes, list(zip(grads, targets, SWAP_AXES)), swap_sems, halves)
-    small = Swap(at, sizes, [(gains, gains_in, 1)], small_sems)
-    spread = Spread(
-        at,
-        sizes,
-        [(share.at[pl.ds(k * chunk, chunk)], grad_out, 0, rows_all, k * chunk) for k in range(count)],
-        spread_sems,
-    )
-    line_one[...] = jnp.zeros(line_one.shape, jnp.float32)
-    mine = pl.ds(pl.multiple_of(place * width, width), width)
-
-    def first(k):
-        scatter.free(k)
-        where = span(k, chunk)
-        rows = [d[where, :] for d in deltas]
-        one = jnp.zeros((chunk, width), jnp.float32)
-        two = jnp.zeros((chunk, width), jnp.float32)
-        for rank in range(ranks):
-            columns = slice(rank * width, (rank + 1) * width)
-            value = inner_rows(rows[0], weights[0][columns, :])
-            for row, weight in zip(rows[1:], weights[1:]):
-                value += inner_rows(row, weight[columns, :])
-            scatter.part[lax.rem(k, 2), rank // 2, rank % 2] = lowered(value)
-            one += value * gain[:, columns]
-            two += value * wide(normed_in[where, columns])
-        scatter.start(k)
-        ones = jnp.ones((8, width), jnp.float32)
-        flat = [
-            lax.dot_general(
-                ones,
-                item,
-                (((1,), (1,)), ((), ())),
-                precision=lax.Precision.HIGHEST,
-                preferred_element_type=jnp.float32,
-            )
-            for item in (one, two)
-        ]
-        line = lax.broadcasted_iota(jnp.int32, (8, chunk), 0)
-        sums[place, k] = jnp.where(line == 0, flat[0], flat[1])
-        for j in range(1, ranks):
-            sums_copy(k, j, place).start()
-
-    def sums_copy(k, j, owner):
-        peer = lax.rem(place + j, ranks)
-        return pltpu.make_async_remote_copy(
-            src_ref=sums.at[owner, k],
-            dst_ref=sums.at[owner, k],
-            send_sem=sums_sent.at[j - 1, k],
-            recv_sem=sums_got.at[j - 1, k],
-            device_id=(group, peer // 2, lax.rem(peer, 2)),
-            device_id_type=MESH,
-        )
-
-    def pack_copy(j, owner):
-        peer = lax.rem(place + j, ranks)
-        return pltpu.make_async_remote_copy(
-            src_ref=packed.at[owner],
-            dst_ref=packed.at[owner],
-            send_sem=gain_sent.at[j - 1],
-            recv_sem=gain_got.at[j - 1],
-            device_id=(group, peer // 2, lax.rem(peer, 2)),
-            device_id_type=MESH,
-        )
-
-    def sender(j):
-        return lax.rem(place + ranks - j, ranks)
-
-    def finish(k):
-        scatter.finish(k)
-        for j in range(1, ranks):
-            sums_copy(k, j, sender(j)).wait_recv()
-        line = lax.broadcasted_iota(jnp.int32, (8, 128), 0)
-        lane = lax.broadcasted_iota(jnp.int32, (8, 128), 1)
-        means = lax.dot_general(
-            jnp.sum(sums[:, k], 0),
-            jnp.where(line == lane, 1.0 / (ranks * width), 0.0),
-            (((0,), (0,)), ((), ())),
-            precision=lax.Precision.HIGHEST,
-            preferred_element_type=jnp.float32,
-        )
-        where = span(k, chunk)
-        value, normed = scatter.total[...], unit[where, :]
-        outer = value * normed
-        line_one[...] += jnp.sum(outer.reshape(chunk // 8, 8, width), 0)
-        back = value * gain[:, mine] - means[:, :1] - normed * means[:, 1:2]
-        share[where, :] = lowered(wide(branch[where, mine]) + scale[where, :1] * back)
-
-    def weigh(number):
-        if number == 4:
-
-            def part(k):
-                columns = span(k, chunk)
-                grads[4][:, columns] = lowered(inner_cols(mixed_in[...], branch[:, columns]))
-        else:
-
-            def part(k):
-                columns = span(k, chunk)
-                grads[number][columns, :] = lowered(inner_cols(normed_in[:, columns], deltas[number][...]))
-
-        in_order(ranks * width // chunk, part)
-        swap.start(number)
-
-    lag = levels - 1
-
-    def wave(number):
-        @pl.when(number < count)
-        def _():
-            first(number)
-
-        for step, which in ((1, 2), (2, 0), (3, 1)):
-
-            @pl.when(number == step)
-            def _():
-                weigh(which)
-
-        @pl.when(number < count)
-        def _():
-            scatter.join(number)
-
-        scatter.steps(number)
-
-        @pl.when(number == lag)
-        def _():
-            loads.wait(9, 10, 11, 12)
-
-        @pl.when(within(number - lag, count))
-        def _():
-            finish(number - lag)
-
-        for k in range(count):
-
-            @pl.when(number == lag + k)
-            def _():
-                spread.start(k)
-
-            @pl.when(number == lag + k + 2)
-            def _():
-                spread.relay(k)
-
-        @pl.when(number == lag + 1)
-        def _():
-            weigh(4)
-
-        for step, relayed in ((2, 3), (4, 2), (5, 0), (6, 1), (8, 4)):
-
-            @pl.when(number == step)
-            def _():
-                swap.relay(relayed)
-
-    loads.wait(3, 8)
-    weigh(3)
-    loads.wait(0, 1, 2, 4, 5, 6, 7)
-    in_order(count + lag, wave)
-    for k in (count - 2, count - 1):
-        spread.relay(k)
-    total = jnp.sum(gain_two[...], 0, keepdims=True)
-    packed[place] = jnp.concatenate([total, jnp.sum(line_one[...], 0, keepdims=True)], axis=1)
+    in_order(close_lag + levels + count, wave)
+    give.relay(count - 2, count - 1)
+    packed[place] = jnp.concatenate(
+        [jnp.sum(gain_acc[...], 0, keepdims=True), jnp.sum(line_one[...], 0, keepdims=True)], axis=1
+    )
     for j in range(1, ranks):
         pack_copy(j, place).start()
     for j in range(1, ranks):
         pack_copy(j, sender(j)).wait_recv()
-    everything = ranks * width
-    line = lax.broadcasted_iota(jnp.int32, (8, everything), 0)
-    two = sum(packed[rank, :, :everything] for rank in range(ranks))
-    one = jnp.concatenate([packed[rank, :, everything:] for rank in range(ranks)], axis=1)
-    gains[...] = jnp.where(line == 0, one, two)
+    line = lax.broadcasted_iota(jnp.int32, (8, width), 0)
+    two_sum = sum(packed[rank, :, :width] for rank in range(ranks))
+    one_sum = jnp.concatenate([packed[rank, :, width:] for rank in range(ranks)], axis=1)
+    gains[...] = jnp.where(line == 0, one_sum, two_sum)
     small.start(0)
     small.wait(0)
-    swap.wait(*range(5))
-    spread.wait(*range(count))
-    spread.drain(*range(count))
     gains_out[...] = jnp.sum(gains_in[...], 0)
+    late.wait(*range(5))
+    give.wait(*range(count))
+    give.drain(*range(count))
+    deal.wait(*range(count))
+    deal.drain(*range(count))
+    four.drain()
+    three.across(count - 2).wait_send()
+    three.across(count - 1).wait_send()
+    branch_gather.drain()
     for j in range(1, ranks):
         pack_copy(j, place).wait_send()
-    scatter.drain()
 
     def drain(k):
         for j in range(1, ranks):
@@ -1650,54 +1669,45 @@
     )
     rate = jnp.log1p(-jnp.exp2(-5.0 - place.astype(f32))).reshape(1)
     by_rows = (PIECE, width)
-    (
-        mixed_in,
-        _,
-        delta_branch,
-        delta_swish,
-        delta_query,
-        delta_keys,
-        delta_values,
-        gain_two_part,
-        mixed_all,
-        *ff_grads,
-    ) = kernel_call(
+    pieces = (count, sizes[1], 2) + by_rows
+    blocks = (sizes[1], 2, slice_width)
+    late_w = [struct(shape) for shape in ((width, v_dim), (v_dim, width), (width, v_dim), (qk_dim, width))]
+    late_w.append(late_w[3])
+    late_axes = (0, 1, 0, 1, 1)
+    core_outs = kernel_call(
         functools.partial(core_kernel, sizes),
         1,
-        [("smem", dealt_start), ("smem", rate), ("vmem", wide_two)]
+        [("smem", dealt_start), ("smem", rate), ("vmem", wide_two), ("vmem", wide_one)]
         + anywhere((query, keys, values, x_rows, dy_part, swish_in))
+        + anywhere((normed_in.reshape(pieces), unit_share, scale_one))
+        + anywhere([w.reshape(blocks + w.shape[1:]) for w in (query_w, key_w, value_w, swish_w)])
         + anywhere(low),
-        anywhere(
-            [
-                struct((rows_dev, v_dim)),
-                struct((rows_dev, v_dim), f32),
-                struct((rows_dev, width)),
-                struct((rows_dev, v_dim)),
-                struct((rows_dev, qk_dim)),
-                struct((rows_dev, qk_dim)),
-                struct((rows_dev, v_dim)),
-            ]
-        )
-        + [("vmem", struct((8, width), f32))]
+        anywhere([struct((rows_dev, v_dim)), struct((rows_dev, v_dim), f32)])
+        + [("vmem", struct((8, gain_attn.shape[0]), f32))]
         + anywhere(
             [
+                struct((sizes[0] * rows_dev, slice_width)),
                 struct((sizes[0] * rows_dev, slice_width)),
                 swap_shape(full_w[7], 1, sizes),
                 swap_shape(full_w[5], 0, sizes),
                 swap_shape(full_w[6], 0, sizes),
             ]
+            + [swap_shape(w, a, sizes) for w, a in zip(late_w, late_axes)]
         ),
         held_like((query, keys, values, x_rows))
         + held_like(full_w[4:])
         + Scatter.rooms(count, sizes, by_rows)
         + Scatter.rooms(count, sizes, by_rows)[:1]
-        + Scatter.sems(count, sizes) * 3
+        + Scatter.sems(count, sizes) * 4
         + Gather.scratch(count, sizes, by_rows)
         + Gather.scratch(count, sizes, (chunk, slice_width))
         + Gather.scratch(count, sizes, by_rows)
         + Spread.scratch(4, sizes)
         + Spread.scratch(count, sizes)
         + Swap.scratch(3, sizes)
+        + Swap.scratch(5, sizes)
+        + Swap.scratch(1, sizes)
+        + Spread.scratch(count, sizes)
         + [
             VMEM((rows_dev, ff_dim), bf16),
             VMEM((rows_dev, ff_dim), bf16),
@@ -1706,66 +1716,34 @@
             VMEM((2, chunk, v_dim), f32),
             VMEM((2, chunk, v_dim), f32),
             VMEM((2, chunk, v_dim), bf16),
-            VMEM((2, chunk, v_dim), bf16),
             VMEM((rows_dev, qk_dim), f32),
             VMEM((rows_dev, v_dim), f32),
             VMEM((chunk, qk_dim), f32),
             VMEM((chunk, v_dim), bf16),
             VMEM((ff_dim, width), bf16),
             VMEM((rows_dev, slice_width), bf16),
-            DMA((5,)),
-            DMA((6, count)),
-            DMA((ranks, count)),
-            DMA((1, count)),
-            DMA((2,)),
-        ]
-        + half_blocks([(full_w[7], 1), (full_w[5], 0), (full_w[6], 0)], sizes),
-    )
-    close_ins = (
-        delta_query,
-        delta_keys,
-        delta_values,
-        delta_swish,
-        query_w,
-        key_w,
-        value_w,
-        swish_w,
-        normed_in,
-        delta_branch,
-        mixed_in,
-        unit_share,
-        scale_one,
-    )
-    swaps = len(SWAP_AXES)
-    grad_all, gains, *attn_grads = kernel_call(
-        functools.partial(close_kernel, sizes),
-        2,
-        [("vmem", wide_one), ("vmem", gain_two_part)] + anywhere(close_ins),
-        anywhere([struct((sizes[0] * rows_dev, slice_width))])
-        + [("vmem", struct((8, gain_attn.shape[0]), f32))]
-        + anywhere([swap_shape(w, a, sizes) for w, a in zip(full_w[:5], SWAP_AXES)]),
-        held_like(close_ins)
-        + held_like(full_w[:5])
-        + Scatter.scratch(count, sizes, (chunk, slice_width))
-        + Swap.scratch(swaps, sizes)
-        + [
+            VMEM((8, width), f32),
             VMEM((ranks, count, 8, chunk), f32),
             VMEM((8, slice_width), f32),
-            VMEM((rows_dev, slice_width), jnp.bfloat16),
             VMEM((ranks, 1, width + slice_width), f32),
             VMEM((8, width), f32),
             VMEM((sizes[0], 8, gain_attn.shape[0]), f32),
-            DMA((len(close_ins),)),
+            DMA((5,)),
+            DMA((5, count)),
+            DMA((8,)),
+            DMA((2, count)),
+            pltpu.SemaphoreType.REGULAR((3,)),
             DMA((ranks - 1, count)),
             DMA((ranks - 1, count)),
             DMA((ranks - 1,)),
             DMA((ranks - 1,)),
         ]
-        + Spread.scratch(count, sizes)
-        + Swap.scratch(1, sizes)
-        + half_blocks(list(zip(full_w[:5], SWAP_AXES)), sizes),
-    )
-    grads = [jnp.sum(wide(g), 0) for g in attn_grads + ff_grads[1:] + ff_grads[:1]]
+        + half_blocks([(full_w[7], 1), (full_w[5], 0), (full_w[6], 0)], sizes)
+        + half_blocks(list(zip(late_w, late_axes))[3:], sizes),
+    )
+    _, _, gains, mixed_all, grad_all, *parts = core_outs
+    down, gate, up, swish, out, value, query, key = (jnp.sum(wide(g), 0) for g in parts)
+    grads = (query.T, key.T, value, swish, out, gate, up, down)
     slot_match = dealing[:, None] == ident[None, :]
     slot_len = jnp.sum(jnp.where(slot_match, lengths[None, :], 0), 1)
     slot_home = jnp.sum(jnp.where(slot_match, starts[None, :], 0), 1)

time: 522 us -> 513 us (0.983)
  Pallas kernels: 489 us -> 481 us
    pallas_call x3 -> x2, Pallas kernels: 489 us -> 481 us  [kernel_call(): pl.pallas_call(body, out_shape=[shape for _, shape in outs], in_specs=[pl...]
where the time goes in v6:
time: 513 us
  Pallas kernels  481 us (94%)
  local copies, waits for them, and re-layouts  17.5 us (3%)
  other arithmetic  13.6 us (3%)
    pallas_call x2, Pallas kernels, kernel_call(): pl.pallas_call(body, out_shape=[shape for _, shape in outs], in_specs=[pl...  481 us
    gather x2, local copies, waits for them, and re-layouts, pick(): return whole.at[rows].get(mode='promise_in_bounds')  12.3 us

profile of v6, /device:TPU:0, one launch (start us, length us, event | category | flops | bytes accessed | tf_op | source)
XLA Modules:
  0.0 512.6 jit_solution(314595144064906917)
XLA Ops:
  0.6 0.7 dynamic_slice.3
  1.4 0.8 reduce-window.17
  2.2 0.7 bitcast_subtract_fusion
  2.9 0.9 select_reduce_fusion.4
  3.7 0.2 reduce-window.16
  3.9 0.5 fusion.4
  4.4 0.0 copy-start.7
  4.4 0.1 add_clamp_fusion
  4.5 0.1 min.12
  4.6 0.5 and_select_fusion.1.begins
  5.1 1.3 select_maximum_fusion.gain_rows
  6.4 0.0 copy-done.7
  6.5 125.8 %shard_map.229 = (bf16[1536,2048]{1,0:T(8,128)(2,1)}, bf16[1536,256]{1,0:T(8,128)(2,1)}, bf16[1536,256]{1,0:T(8,128)(2,1)}, bf16[1536,512]{1,0:T(8,128)(2,1)}, f...) custom-call(s32[3]{0:T(128)} %get-tuple-element.101.bounds, ...), custom_call_target="tpu_custom_call" | custom-call | tf_op jit(solution)/shard_map/pallas_call | solution.py:1523
  132.3 354.8 %shard_map.230 = (bf16[1536,512]{1,0:T(8,128)(2,1)}, f32[1536,512]{1,0:T(8,128)}, f32[8,512]{1,0:T(8,128)}, bf16[6144,256]{1,0:T(8,128)(2,1)}, bf16[6144,256]{1,...) custom-call(s32[3]{0:T(128)} %get-tuple-element.101.bounds, ...), custom_call_target="tpu_custom_call" | custom-call | tf_op jit(solution)/shard_map/pallas_call | solution.py:1523
  487.1 0.0 copy-start.3
  487.1 0.0 copy-start.4
  487.2 4.1 convert_reduce_fusion
  491.2 0.0 copy-done.3
  491.2 0.0 copy-done.4
  491.2 0.0 copy-start.1
  491.2 0.0 copy-start.2
  491.2 1.8 convert_reduce_fusion.2
  493.0 0.0 copy-done.1
  493.0 0.8 copy-done.2
  493.9 0.0 copy-start.5
  493.9 0.0 copy-start.6
  493.9 1.8 convert_reduce_fusion.4
  495.7 0.0 copy-done.5
  495.7 0.0 copy-done.6
  495.7 0.3 convert_reduce_fusion.6
  495.9 0.0 copy-start.8
  495.9 0.0 copy-start.9
  496.0 1.0 copy.28
  497.0 1.0 copy.29
  498.0 0.0 copy-done.8
  498.0 0.0 copy-done.9
  498.0 0.2 select_reduce_fusion.3
  498.1 0.1 reshape.187
  498.2 0.2 reduce_window_sum.27
  498.4 0.1 reduce_window_sum.28
  498.5 0.1 select_reduce_fusion.1
  498.6 0.1 convert_reduce_fusion.8
  498.7 0.1 select_reduce_fusion
  498.9 0.0 copy-start
  498.9 7.0 %gather_fusion.1 = bf16[1536,256]{1,0:T(8,128)(2,1)} fusion(bf16[6144,256]{1,0:T(8,128)(2,1)} %get-tuple-element.62, s32[2048]{0:T(1024)S(1)} %pad_clamp_fusion), kind=kCustom, calls=%fused_computation.1 | custom fusion | bytes 1579008 | tf_op jit(solution)/shard_map/gather | solution.py:1556
  505.9 0.0 copy-done
  505.9 5.4 %gather_fusion = bf16[1536,256]{1,0:T(8,128)(2,1)} fusion(bf16[6144,256]{1,0:T(8,128)(2,1)S(1)} %copy-done, s32[2048]{0:T(1024)S(1)} %pad_clamp_fusion), kind=kCustom, calls=%fused_computation | custom fusion | bytes 1579008 | tf_op jit(solution)/shard_map/gather | solution.py:1556
  511.2 1.4 fusion.5
  (6 shorter events, 0.1 us)
Async XLA Ops:
  4.4 2.0 copy-start.7
  487.1 4.1 copy-start.3
  487.1 4.1 copy-start.4
  491.2 1.8 copy-start.1
  491.2 2.6 copy-start.2
  493.9 1.8 copy-start.5
  493.9 1.8 copy-start.6
  495.9 2.0 copy-start.8
  495.9 2.0 copy-start.9
  498.9 7.0 %copy-start = (bf16[6144,256]{1,0:T(8,128)(2,1)S(1)}, bf16[6144,256]{1,0:T(8,128)(2,1)}, u32[]{:S(2)}) copy-start(bf16[6144,256]{1,0:T(8,128)(2,1)} %get-tuple-element.61) | copy-start | bytes 9437188

commit v7 on v6

--- a/solution.py
+++ b/solution.py
@@ -1150,6 +1150,7 @@
                 three.part[
                     lax.rem(k, 2), rank // 2, rank % 2, :, run * part_width : (run + 1) * part_width
                 ] = lowered(value[run * piece : (run + 1) * piece, :] + held)
+        pl.semaphore_wait(room.at[0, 0], 1)
         three.start(k)
 
     def out_finish(k):
@@ -1234,17 +1235,18 @@
             device_id_type=MESH,
         )
 
-    def make_room(k):
-        three.sent(k)
-        pl.semaphore_signal(room.at[0], inc=1, device_id=(group, level, 1 - core), device_id_type=MESH)
+    def make_room(scatter, turn_of, k):
+        scatter.sent(k)
+        where = room.at[turn_of]
+        pl.semaphore_signal(where.at[0], inc=1, device_id=(group, level, 1 - core), device_id_type=MESH)
 
         @pl.when(level > 0)
         def _():
-            pl.semaphore_signal(room.at[1], inc=1, device_id=(group, level - 1, core), device_id_type=MESH)
+            pl.semaphore_signal(where.at[1], inc=1, device_id=(group, level - 1, core), device_id_type=MESH)
 
         @pl.when(level < levels - 1)
         def _():
-            pl.semaphore_signal(room.at[2], inc=1, device_id=(group, level + 1, core), device_id_type=MESH)
+            pl.semaphore_signal(where.at[2], inc=1, device_id=(group, level + 1, core), device_id_type=MESH)
 
     def in_part(k):
         four.free(k, two)
@@ -1266,7 +1268,7 @@
                 ] = lowered(value[run * piece : (run + 1) * piece, :])
             first_sum += value * gain_first[:, columns]
             second_sum += value * wide(normed_mid[k, :, :, :, columns].reshape(chunk, part_width))
-        pl.semaphore_wait(room.at[0], 1)
+        pl.semaphore_wait(room.at[1, 0], 1)
         four.start(k)
         ones = jnp.ones((8, part_width), jnp.float32)
         flat = [
@@ -1284,14 +1286,14 @@
         for j in range(1, ranks):
             sums_copy(k, j, place).start()
 
-    def in_room(wave):
+    def in_room(turn_of, wave):
         @pl.when(within(wave - level, count) & (level < levels - 1))
         def _():
-            pl.semaphore_wait(room.at[1], 1)
+            pl.semaphore_wait(room.at[turn_of, 1], 1)
 
         @pl.when(within(wave - (levels - 1 - level), count) & (level > 0))
         def _():
-            pl.semaphore_wait(room.at[2], 1)
+            pl.semaphore_wait(room.at[turn_of, 2], 1)
 
     def in_finish(k):
         four.finish(k)
@@ -1332,6 +1334,7 @@
     last_lag = branch_lag + levels - 1
     turned = turn_lag + count
     close_lag = last_lag + count
+    out_lag = last_lag - 2
 
     def at_wave(number, lag, step):
         @pl.when(within(number - lag, count))
@@ -1340,8 +1343,11 @@
 
     def wave(number):
         at_wave(number, lead, first)
-        for gather, lag, scatter in ((branch_gather, branch_lag, two), (mid_gather, mid_lag, one)):
-            at_wave(number, lag + 1, scatter.sent)
+        for gather, lag, sent in (
+            (branch_gather, branch_lag, functools.partial(make_room, two, 0)),
+            (mid_gather, mid_lag, one.sent),
+        ):
+            at_wave(number, lag + 1, sent)
             for hop in range(levels - 1, 0, -1):
                 at_wave(number, lag + hop, functools.partial(hop_on, gather, hop))
         at_wave(number, branch_lag, branch_norm)
@@ -1402,21 +1408,22 @@
             late_loads.start(*range(2, 8))
 
         at_wave(number, last_lag, last)
-        at_wave(number, last_lag, out_part)
-        at_wave(number, last_lag + 1, three.join)
-        three.steps(number - last_lag - 1)
-        at_wave(number, last_lag + levels, out_finish)
+        at_wave(number, out_lag, out_part)
+        at_wave(number, out_lag + 1, three.join)
+        in_room(0, number - out_lag - 1)
+        three.steps(number - out_lag - 1)
+        at_wave(number, out_lag + levels, out_finish)
         for k in range(count):
 
-            @pl.when(number == last_lag + levels + k)
+            @pl.when(number == out_lag + levels + k)
             def _():
                 deal.start(k)
 
-            @pl.when(number == last_lag + levels + k + 2)
+            @pl.when(number == out_lag + levels + k + 2)
             def _():
                 deal.relay(k)
 
-        at_wave(number, last_lag + levels + 1, make_room)
+        at_wave(number, out_lag + levels + 1, functools.partial(make_room, three, 1))
 
         @pl.when(number == close_lag)
         def _():
@@ -1427,7 +1434,6 @@
                     copy.start()
             late_loads.wait(*range(8))
 
-        at_wave(number, close_lag, in_part)
         for step, before, which in ((0, 1, 0), (1, 0, 1), (2, 2, 2), (3, None, 3)):
 
             @pl.when(number == close_lag + step)
@@ -1436,8 +1442,9 @@
                     swap.wait(before)
                 weigh_late(which)
 
+        at_wave(number, close_lag, in_part)
         at_wave(number, close_lag + 1, four.join)
-        in_room(number - close_lag - 1)
+        in_room(1, number - close_lag - 1)
         four.steps(number - close_lag - 1)
         at_wave(number, close_lag + levels, in_finish)
         for step, which in ((3, (0,)), (4, (1,)), (5, (2,)), (7, (3, 4))):
@@ -1732,7 +1739,7 @@
             DMA((5, count)),
             DMA((8,)),
             DMA((2, count)),
-            pltpu.SemaphoreType.REGULAR((3,)),
+            pltpu.SemaphoreType.REGULAR((2, 3)),
             DMA((ranks - 1, count)),
             DMA((ranks - 1, count)),
             DMA((ranks - 1,)),

time: 513 us -> 506 us (0.986)
  Pallas kernels: 481 us -> 474 us
    pallas_call x2, Pallas kernels: 481 us -> 474 us  [kernel_call(): pl.pallas_call(body, out_shape=[shape for _, shape in outs], in_specs=[pl...]
where the time goes in v7:
time: 506 us
  Pallas kernels  474 us (94%)
  local copies, waits for them, and re-layouts  17.5 us (3%)
  other arithmetic  13.6 us (3%)
    pallas_call x2, Pallas kernels, kernel_call(): pl.pallas_call(body, out_shape=[shape for _, shape in outs], in_specs=[pl...  474 us
    gather x2, local copies, waits for them, and re-layouts, pick(): return whole.at[rows].get(mode='promise_in_bounds')  12.3 us

profile of v7, /device:TPU:0, one launch (start us, length us, event | category | flops | bytes accessed | tf_op | source)
XLA Modules:
  0.0 506.0 jit_solution(9147270131262274947)
XLA Ops:
  0.6 0.7 dynamic_slice.3
  1.4 0.8 reduce-window.17
  2.2 0.7 bitcast_subtract_fusion
  2.9 0.9 select_reduce_fusion.4
  3.7 0.2 reduce-window.16
  3.9 0.5 fusion.4
  4.4 0.0 copy-start.7
  4.4 0.1 add_clamp_fusion
  4.5 0.1 min.12
  4.6 0.5 and_select_fusion.1.begins
  5.1 1.3 select_maximum_fusion.gain_rows
  6.4 0.0 copy-done.7
  6.5 125.8 %shard_map.229 = (bf16[1536,2048]{1,0:T(8,128)(2,1)}, bf16[1536,256]{1,0:T(8,128)(2,1)}, bf16[1536,256]{1,0:T(8,128)(2,1)}, bf16[1536,512]{1,0:T(8,128)(2,1)}, f...) custom-call(s32[3]{0:T(128)} %get-tuple-element.101.bounds, ...), custom_call_target="tpu_custom_call" | custom-call | tf_op jit(solution)/shard_map/pallas_call | solution.py:1530
  132.3 348.2 %shard_map.230 = (bf16[1536,512]{1,0:T(8,128)(2,1)}, f32[1536,512]{1,0:T(8,128)}, f32[8,512]{1,0:T(8,128)}, bf16[6144,256]{1,0:T(8,128)(2,1)}, bf16[6144,256]{1,...) custom-call(s32[3]{0:T(128)} %get-tuple-element.101.bounds, ...), custom_call_target="tpu_custom_call" | custom-call | tf_op jit(solution)/shard_map/pallas_call | solution.py:1530
  480.5 0.0 copy-start.3
  480.5 0.0 copy-start.4
  480.5 4.1 convert_reduce_fusion
  484.6 0.0 copy-done.3
  484.6 0.0 copy-done.4
  484.6 0.0 copy-start.1
  484.6 0.0 copy-start.2
  484.6 1.8 convert_reduce_fusion.2
  486.4 0.0 copy-done.1
  486.4 0.8 copy-done.2
  487.2 0.0 copy-start.5
  487.2 0.0 copy-start.6
  487.2 1.8 convert_reduce_fusion.4
  489.1 0.0 copy-done.5
  489.1 0.0 copy-done.6
  489.1 0.3 convert_reduce_fusion.6
  489.3 0.0 copy-start.8
  489.3 0.0 copy-start.9
  489.3 1.0 copy.28
  490.3 1.0 copy.29
  491.3 0.0 copy-done.8
  491.3 0.0 copy-done.9
  491.3 0.2 select_reduce_fusion.3
  491.5 0.1 reshape.187
  491.6 0.2 reduce_window_sum.27
  491.8 0.1 reduce_window_sum.28
  491.9 0.1 select_reduce_fusion.1
  492.0 0.1 convert_reduce_fusion.8
  492.1 0.1 select_reduce_fusion
  492.3 0.0 copy-start
  492.3 7.0 %gather_fusion.1 = bf16[1536,256]{1,0:T(8,128)(2,1)} fusion(bf16[6144,256]{1,0:T(8,128)(2,1)} %get-tuple-element.62, s32[2048]{0:T(1024)S(1)} %pad_clamp_fusion), kind=kCustom, calls=%fused_computation.1 | custom fusion | bytes 1579008 | tf_op jit(solution)/shard_map/gather | solution.py:1563
  499.3 0.0 copy-done
  499.3 5.4 %gather_fusion = bf16[1536,256]{1,0:T(8,128)(2,1)} fusion(bf16[6144,256]{1,0:T(8,128)(2,1)S(1)} %copy-done, s32[2048]{0:T(1024)S(1)} %pad_clamp_fusion), kind=kCustom, calls=%fused_computation | custom fusion | bytes 1579008 | tf_op jit(solution)/shard_map/gather | solution.py:1563
  504.6 1.4 fusion.5
  (6 shorter events, 0.1 us)
Async XLA Ops:
  4.4 2.0 copy-start.7
  480.5 4.1 copy-start.3
  480.5 4.1 copy-start.4
  484.6 1.8 copy-start.1
  484.6 2.6 copy-start.2
  487.2 1.8 copy-start.5
  487.2 1.8 copy-start.6
  489.3 2.0 copy-start.8
  489.3 2.0 copy-start.9
  492.3 7.0 %copy-start = (bf16[6144,256]{1,0:T(8,128)(2,1)S(1)}, bf16[6144,256]{1,0:T(8,128)(2,1)}, u32[]{:S(2)}) copy-start(bf16[6144,256]{1,0:T(8,128)(2,1)} %get-tuple-element.61) | copy-start | bytes 9437188

commit v8 on v7

--- a/solution.py
+++ b/solution.py
@@ -891,7 +891,7 @@
     project_src, refs = refs[:4], refs[4:]
     shards, refs = refs[:4], refs[4:]
     mixed_in_out, retained_out, gains_out, *refs = refs
-    mixed_dst, grad_dst, down_dst, gate_dst, up_dst, *refs = refs
+    homes, down_dst, gate_dst, up_dst, *refs = refs
     late_dst, refs = refs[:5], refs[5:]
     query, keys, values, x_rows, out_w, gate_w, up_w, down_w, *refs = refs
     rooms, refs = refs[:4], refs[4:]
@@ -918,6 +918,8 @@
     ranks = 2 * levels
     chunk = ranks * piece
     part_width = width // ranks
+    mixed_dst = homes.at[:, pl.ds(0, part_width)]
+    grad_dst = homes.at[:, pl.ds(part_width, part_width)]
     loads = Moves(
         [
             (dy_src, dy.at[:, level, core]),
@@ -1504,6 +1506,72 @@
             sums_copy(k, j, place).wait_send()
 
     in_order(count, drain)
+
+
+def finish_kernel(first_seq, last_seq, starts, bases, begins, home, homes, *refs):
+    parts, refs = refs[:8], refs[8:]
+    mixed_out, grad_out, *refs = refs
+    outs, refs = refs[:8], refs[8:]
+    homes_held, *refs = refs
+    held, sums, refs = refs[:8], refs[8:16], refs[16:]
+    picked, load_sems, store_sems = refs
+    loads = Moves(list(zip(parts, held)) + [(homes, homes_held)], load_sems)
+    stores = Moves(
+        list(zip(sums, outs)) + [(picked.at[0], mixed_out), (picked.at[1], grad_out)], store_sems
+    )
+    loads.start(*range(9))
+    for number in range(8):
+        loads.wait(number)
+        ways, rows, columns = held[number].shape
+        run = min(64, rows)
+        turned = number < 2
+
+        def block(k):
+            where = span(k, run)
+            total = wide(held[number][0, where, :])
+            for way in range(1, ways):
+                total += wide(held[number][way, where, :])
+            sums[number][where, :] = total
+
+        def turn(k):
+            where = span(k, 128)
+            total = wide(held[number][0, :, where])
+            for way in range(1, ways):
+                total += wide(held[number][way, :, where])
+            sums[number][where, :] = total.T
+
+        if turned:
+            in_order(columns // 128, turn)
+        else:
+            in_order(rows // run, block)
+        stores.start(number)
+    loads.wait(8)
+    width = picked.shape[2]
+    rows = 128
+    window = rows + 16
+    lane = lax.broadcasted_iota(jnp.int32, (rows, window), 1)
+
+    def pick_block(k):
+        own = home[0] + k * rows + lax.broadcasted_iota(jnp.int32, (rows, 1), 0)
+
+        def one(seq, total):
+            start = begins[k, seq]
+            inside = (own >= starts[seq]) & (own < starts[seq + 1])
+            wanted = jnp.where(inside, own + bases[seq] - 16 * start, -1)
+            chosen = jnp.where(lane == wanted, 1.0, 0.0).astype(jnp.bfloat16)
+            there = jnp.concatenate([homes_held[start + n] for n in range(window // 16)], axis=0)
+            return total + matmul(chosen, there)
+
+        total = lax.fori_loop(
+            first_seq[k], last_seq[k] + 1, one, jnp.zeros((rows, 2 * width), jnp.float32)
+        )
+        where = span(k, rows)
+        picked[0, where, :] = lowered(total[:, :width])
+        picked[1, where, :] = lowered(total[:, width:])
+
+    in_order(picked.shape[1] // rows, pick_block)
+    stores.start(8, 9)
+    stores.wait(*range(10))
 
 
 def column_all(at, sizes):
@@ -1693,8 +1761,7 @@
         + [("vmem", struct((8, gain_attn.shape[0]), f32))]
         + anywhere(
             [
-                struct((sizes[0] * rows_dev, slice_width)),
-                struct((sizes[0] * rows_dev, slice_width)),
+                struct((sizes[0] * rows_dev, 2 * slice_width)),
                 swap_shape(full_w[7], 1, sizes),
                 swap_shape(full_w[5], 0, sizes),
                 swap_shape(full_w[6], 0, sizes),
@@ -1748,9 +1815,7 @@
         + half_blocks([(full_w[7], 1), (full_w[5], 0), (full_w[6], 0)], sizes)
         + half_blocks(list(zip(late_w, late_axes))[3:], sizes),
     )
-    _, _, gains, mixed_all, grad_all, *parts = core_outs
-    down, gate, up, swish, out, value, query, key = (jnp.sum(wide(g), 0) for g in parts)
-    grads = (query.T, key.T, value, swish, out, gate, up, down)
+    _, _, gains, homes, *parts = core_outs
     slot_match = dealing[:, None] == ident[None, :]
     slot_len = jnp.sum(jnp.where(slot_match, lengths[None, :], 0), 1)
     slot_home = jnp.sum(jnp.where(slot_match, starts[None, :], 0), 1)
@@ -1758,13 +1823,26 @@
     slot_start = (jnp.cumsum(per_group, 1) - per_group).reshape(-1)
     slot_base = ident // SEQ_DEV * rows_dev + slot_start - slot_home
     owner_base = jnp.sum(jnp.where(dealing[None, :] == ident[:, None], slot_base[None, :], 0), 1)
-    global_rows = group * rows_dev + rows
-    seq_of = jnp.sum((global_rows[:, None] >= starts[None, :]).astype(jnp.int32), 1) - 1
-    targets = (
-        jnp.sum(jnp.where(seq_of[:, None] == ident[None, :], owner_base[None, :], 0), 1)
-        + global_rows
-    )
-    mixed_rows, grad_rows = pick(targets, mixed_all), pick(targets, grad_all)
+    blocks_at = group * rows_dev + jnp.arange(rows_dev // 128, dtype=jnp.int32) * 128
+    first_seq = jnp.sum((blocks_at[:, None] >= starts[None, :]).astype(jnp.int32), 1) - 1
+    last_seq = jnp.sum((blocks_at[:, None] + 127 >= starts[None, :]).astype(jnp.int32), 1) - 1
+    total_rows = sizes[0] * rows_dev
+    home_begins = jnp.clip(blocks_at[:, None] + owner_base[None, :], 0, total_rows - 144) // 16
+    all_starts = jnp.concatenate([starts, jnp.full((1,), total_rows, jnp.int32)])
+    homes = homes.reshape(total_rows // 16, 16, 2 * slice_width)
+    order = [parts[n] for n in (6, 7, 5, 3, 4, 1, 2, 0)]
+    owners = (w_query, w_key, w_value, w_swish, w_out, w_gate, w_up, w_down)
+    finals = [struct(w.shape, f32) for w in owners]
+    picks = struct((2, rows_dev, slice_width))
+    one_place = {"smem": pl.BlockSpec(memory_space=pltpu.SMEM), "any": pl.BlockSpec(memory_space=pl.ANY)}
+    mixed_rows, grad_rows, *grads = pl.pallas_call(
+        finish_kernel,
+        out_shape=[struct((rows_dev, slice_width))] * 2 + finals,
+        in_specs=[one_place["smem"]] * 6 + [one_place["any"]] * 9,
+        out_specs=[one_place["any"]] * 10,
+        scratch_shapes=held_like([homes] + order + finals + [picks]) + [DMA((9,)), DMA((10,))],
+        compiler_params=pltpu.CompilerParams(vmem_limit_bytes=60 * 2**20),
+    )(first_seq, last_seq, all_starts, owner_base, home_begins, blocks_at[:1], homes, *order)
     return (
         mixed_rows,
         grad_rows,

time: 506 us -> 501 us (level)
  local copies, waits for them, and re-layouts: 17.5 us -> 2.39 us
  Pallas kernels: 474 us -> 489 us
  other arithmetic: 13.6 us -> 7.79 us
    pallas_call x0 -> x1, Pallas kernels: none -> 15.1 us  [shards(): pl.pallas_call(finish_kernel, out_shape=[struct((rows_dev, slice_width))]...]
    gather x2 -> x0, local copies, waits for them, and re-layouts: 12.3 us -> none  [pick(): return whole.at[rows].get(mode='promise_in_bounds')]
    reduce_sum x6 -> x0, other arithmetic: 8.12 us -> none  [the longest x4 7.93 us: shards(): jnp.sum(wide(g), 0)]
where the time goes in v8:
time: 501 us; the launch traced here: 500 us
  Pallas kernels  489 us (98%)
  other arithmetic  7.79 us (2%)
    pallas_call x2, Pallas kernels, kernel_call(): pl.pallas_call(body, out_shape=[shape for _, shape in outs], in_specs=[pl...  474 us
    pallas_call x1, Pallas kernels, shards(): pl.pallas_call(finish_kernel, out_shape=[struct((rows_dev, slice_width))]...  15.1 us

profile of v8, /device:TPU:0, one launch (start us, length us, event | category | flops | bytes accessed | tf_op | source)
XLA Modules:
  0.0 500.1 jit_solution(10933412120832680006)
XLA Ops:
  0.6 0.7 dynamic_slice.3
  1.4 0.8 reduce-window.16
  2.2 0.7 bitcast_subtract_fusion.1
  2.9 0.9 select_reduce_fusion.3
  3.7 0.2 reduce-window.17
  3.9 0.5 fusion.6
  4.4 0.0 copy-start.1
  4.4 0.1 add_clamp_fusion
  4.5 0.1 min.22
  4.6 0.5 and_select_fusion.begins
  5.1 1.3 select_maximum_fusion.gain_rows
  6.4 0.0 copy-done.1
  6.5 125.8 %shard_map.229 = (bf16[1536,2048]{1,0:T(8,128)(2,1)}, bf16[1536,256]{1,0:T(8,128)(2,1)}, bf16[1536,256]{1,0:T(8,128)(2,1)}, bf16[1536,512]{1,0:T(8,128)(2,1)}, f...) custom-call(s32[3]{0:T(128)} %get-tuple-element.97.bounds, ...), custom_call_target="tpu_custom_call" | custom-call | tf_op jit(solution)/shard_map/pallas_call | solution.py:1598
  132.3 0.0 copy-start.3
  132.3 0.0 copy-start.4
  132.3 348.2 %shard_map.230 = (bf16[1536,512]{1,0:T(8,128)(2,1)}, f32[1536,512]{1,0:T(8,128)}, f32[8,512]{1,0:T(8,128)}, bf16[6144,512]{1,0:T(8,128)(2,1)}, bf16[3,512,512]{2...) custom-call(s32[3]{0:T(128)} %get-tuple-element.97.bounds, ...), custom_call_target="tpu_custom_call" | custom-call | tf_op jit(solution)/shard_map/pallas_call | solution.py:1598
  480.6 0.0 copy-start
  480.6 0.0 copy-done.3
  480.6 0.0 copy-done.4
  480.6 0.2 select_reduce_fusion.2
  480.8 0.1 reshape.159
  480.9 0.2 reduce_window_sum.27
  481.1 0.1 reduce_window_sum.28
  481.2 0.1 select_reduce_fusion.bases
  481.3 0.0 copy-start.2
  481.3 0.7 add_select_fusion.begins
  482.0 0.5 broadcast_add_fusion.1.last_seq
  482.5 0.5 broadcast_add_fusion.2.first_seq
  483.0 0.6 pad_add_fusion.starts
  483.6 0.0 copy-done
  483.6 0.0 copy-done.2
  483.6 15.1 %shard_map.231 = (bf16[1536,256]{1,0:T(8,128)(2,1)}, bf16[1536,256]{1,0:T(8,128)(2,1)}, f32[512,256]{1,0:T(8,128)}, f32[512,256]{1,0:T(8,128)}, f32[512,512]{1,0...) custom-call(s32[12]{0:T(128)} %broadcast_add_fusion.2.first_seq, ...), custom_call_target="tpu_custom_call" | custom-call | tf_op jit(solution)/shard_map/pallas_call | solution.py:1838
  498.7 1.4 fusion.7
  (3 shorter events, 0.0 us)
Async XLA Ops:
  4.4 2.0 copy-start.1
  132.3 348.3 %copy-start.3 = (s32[12]{0:T(128)S(1)}, s32[12]{0:T(128)}, u32[]{:S(2)}) copy-start(s32[12]{0:T(128)} %param.16) | copy-start | bytes 148
  132.3 348.3 %copy-start.4 = (s32[12]{0:T(128)S(1)}, s32[12]{0:T(128)}, u32[]{:S(2)}) copy-start(s32[12]{0:T(128)} %param.17) | copy-start | bytes 148
  480.6 3.0 copy-start
  481.3 2.3 copy-start.2

commit v9 on v8

--- a/solution.py
+++ b/solution.py
@@ -679,7 +679,7 @@
     return lowered(matmul(jnp.concatenate(chosen, axis=1), jnp.concatenate(windows, axis=0)))
 
 
-def front_kernel(sizes, bounds, shifts, begins, tokens, cotangent, gain_rows, *refs):
+def front_kernel(sizes, bounds, shifts, begins, tokens, cotangent, gain_attn, gain_mlp, *refs):
     masters, refs = refs[:8], refs[8:]
     normed_out, query_out, key_out, value_out, swish_out, dy_out, *refs = refs
     weight_outs, rounded_outs, refs = refs[:4], refs[4:8], refs[8:]
@@ -697,18 +697,20 @@
     ranks = 2 * levels
     piece = chunk // ranks
     loads = Moves(
-        list(zip(masters, held)) + [(tokens, tokens_held), (gain_rows, gains_held), (cotangent, dy_held)], load_sems
-    )
-    loads.start(8, 9, 2, 3, 1, 0, 10, 4, 5, 6, 7)
+        list(zip(masters, held)) + [(tokens, tokens_held), (cotangent, dy_held)], load_sems
+    )
+    loads.start(8, 2, 3, 1, 0, 9, 4, 5, 6, 7)
+    gains_held[...] = jnp.zeros(gains_held.shape, jnp.float32)
+    gains_held[0:1, :] = gain_attn[...]
+    gains_held[1:2, :] = gain_mlp[...]
     greet(plane_peers(at, sizes) + column_peers(at, sizes))
-    loads.wait(8, 9)
+    loads.wait(8)
     spread = Spread(
         at,
         sizes,
         quarters(tokens_held, tokens_all)
-        + [(rounded[2], weights[2], 0), (rounded[3], weights[3], 0)]
-        + quarters(dy_held, dy_all)
-        + [(rounded[1], weights[1], 0), (rounded[0], weights[0], 0)],
+        + [(rounded[number], weights[number], 0) for number in (2, 3, 1, 0)]
+        + quarters(dy_held, dy_all),
         spread_sems,
     )
     small = Spread(at, sizes, [(gains_held, gains_all, 0)], small_sems, relay=False)
@@ -731,7 +733,7 @@
     spread.start(4)
     for number in (3, 1, 0, 4, 5, 6, 7):
         cast(number)
-    loads.wait(10)
+    loads.wait(9)
     stores.start(*range(4))
     for number in range(4):
         spread.relay(number)
@@ -802,9 +804,10 @@
         for step, relayed, started in (
             (1, (4,), (8, 9)),
             (3, (5,), (10, 11)),
-            (5, (6, 7), ()),
-            (6, (8, 9), ()),
-            (8, (10,), ()),
+            (4, (6,), ()),
+            (5, (7,), ()),
+            (7, (8, 9), ()),
+            (9, (10,), ()),
         ):
 
             @pl.when(number == step)
@@ -840,7 +843,9 @@
     spread.relay(11)
     project(2, None)
     project(3, 5)
-    spread.wait(*range(6, 10))
+    project(1, 6)
+    project(0, 7)
+    spread.wait(*range(8, 12))
 
     def dy_chunk(k):
         for half in range(2):
@@ -848,8 +853,6 @@
 
     in_order(count, dy_chunk)
     ends.start(8)
-    project(1, 10)
-    project(0, 11)
     small.drain(0)
     spread.drain(*range(12))
     gather.drain()
@@ -1653,12 +1656,13 @@
     slice_width = tokens.shape[1]
     seq_count = lengths.shape[0]
     ident = jnp.arange(seq_count, dtype=jnp.int32)
-    starts = jnp.cumsum(lengths) - lengths
+    starts = jnp.sum(jnp.where(ident[:, None] > ident[None, :], lengths[None, :], 0), 1)
     picked = lax.dynamic_slice_in_dim(dealing, group * SEQ_DEV, SEQ_DEV)
     match = picked[:, None] == ident[None, :]
     dealt_len = jnp.sum(jnp.where(match, lengths[None, :], 0), 1)
     home_start = jnp.sum(jnp.where(match, starts[None, :], 0), 1)
-    dealt_start = jnp.cumsum(dealt_len) - dealt_len
+    slots = jnp.arange(SEQ_DEV, dtype=jnp.int32)
+    dealt_start = jnp.sum(jnp.where(slots[:, None] > slots[None, :], dealt_len[None, :], 0), 1)
     rows = jnp.arange(rows_dev, dtype=jnp.int32)
     seq_ids = jnp.sum((rows[:, None] >= dealt_start[None, :]).astype(jnp.int32), 1) - 1
     sizes = (lax.axis_size("dp"), lax.axis_size("heads"))
@@ -1671,7 +1675,7 @@
     f32 = jnp.float32
     masters = (w_query, w_key, w_value, w_swish, w_out, w_gate, w_up, w_down)
     axes = (0, 0, 0, 0, 1, 0, 0, 1)
-    gain_rows = jnp.pad(jnp.stack([gain_attn, gain_mlp]), ((0, 6), (0, 0)))
+    gain_rows = struct((8, gain_attn.shape[0]), f32)
     shifts = home_start - dealt_start
     firsts = jnp.arange(2 * count, dtype=jnp.int32) * (chunk // 2)
     begins = jnp.clip(firsts[:, None] + shifts[None, :], 0, sizes[0] * rows_dev - chunk) // 16
@@ -1702,7 +1706,9 @@
         functools.partial(front_kernel, sizes),
         0,
         [("smem", dealt_start), ("smem", shifts), ("smem", begins.reshape(-1))]
-        + anywhere((tokens.reshape(by_runs.shape), cotangent.reshape(by_runs.shape), gain_rows) + masters),
+        + anywhere((tokens.reshape(by_runs.shape), cotangent.reshape(by_runs.shape)))
+        + [("vmem", gain_attn.reshape(1, -1)), ("vmem", gain_mlp.reshape(1, -1))]
+        + anywhere(masters),
         anywhere(
             [
                 struct((rows_dev, width)),
@@ -1736,7 +1742,7 @@
             VMEM((rows_dev, qk_dim), bf16),
             VMEM((rows_dev, v_dim), bf16),
             VMEM((rows_dev, v_dim), f32),
-            DMA((11,)),
+            DMA((10,)),
             DMA((4,)),
             DMA((9,)),
             DMA((count,)),

time: 501 us -> 498 us (level)
  no operation moved by 1% of the time
where the time goes in v9:
time: 498 us; the launch traced here: 497 us
  Pallas kernels  489 us (98%)
  other arithmetic  5.26 us (1%)
    pallas_call x2, Pallas kernels, kernel_call(): pl.pallas_call(body, out_shape=[shape for _, shape in outs], in_specs=[pl...  474 us
    pallas_call x1, Pallas kernels, shards(): pl.pallas_call(finish_kernel, out_shape=[struct((rows_dev, slice_width))]...  14.9 us

profile of v9, /device:TPU:0, one launch (start us, length us, event | category | flops | bytes accessed | tf_op | source)
XLA Modules:
  0.0 497.4 jit_solution(8502852464677187896)
XLA Ops:
  0.6 0.7 dynamic_slice.3
  1.4 0.9 select_reduce_fusion.2
  2.2 0.9 select_reduce_fusion.4
  3.1 0.1 select_reduce_fusion.5.bounds
  3.2 0.0 copy-start.2
  3.2 0.0 copy-start.3
  3.3 0.1 add_clamp_fusion
  3.3 0.1 min.22
  3.4 0.5 and_select_fusion.begins
  4.0 0.0 copy-done.2
  4.0 0.0 copy-done.3
  4.0 125.7 %shard_map.229 = (bf16[1536,2048]{1,0:T(8,128)(2,1)}, bf16[1536,256]{1,0:T(8,128)(2,1)}, bf16[1536,256]{1,0:T(8,128)(2,1)}, bf16[1536,512]{1,0:T(8,128)(2,1)}, f...) custom-call(s32[3]{0:T(128)} %copy-done.2, ...), custom_call_target="tpu_custom_call" | custom-call | tf_op jit(solution)/shard_map/pallas_call | solution.py:1601
  129.8 0.0 copy-start.4
  129.8 348.2 %shard_map.230 = (bf16[1536,512]{1,0:T(8,128)(2,1)}, f32[1536,512]{1,0:T(8,128)}, f32[8,512]{1,0:T(8,128)}, bf16[6144,512]{1,0:T(8,128)(2,1)}, bf16[3,512,512]{2...) custom-call(s32[3]{0:T(128)} %copy-done.2, ...), custom_call_target="tpu_custom_call" | custom-call | tf_op jit(solution)/shard_map/pallas_call | solution.py:1601
  478.1 0.0 copy-start
  478.1 0.0 copy-done.4
  478.1 0.2 select_reduce_fusion.1
  478.3 0.1 reshape.117
  478.4 0.2 reduce_window_sum.13
  478.5 0.1 reduce_window_sum.14
  478.7 0.1 select_reduce_fusion.bases
  478.8 0.0 copy-start.1
  478.8 0.7 add_select_fusion.begins
  479.4 0.5 broadcast_add_fusion.1.last_seq
  480.0 0.5 broadcast_add_fusion.2.first_seq
  480.5 0.6 pad_add_fusion.starts
  481.1 0.0 copy-done
  481.1 0.0 copy-done.1
  481.1 14.9 %shard_map.231 = (bf16[1536,256]{1,0:T(8,128)(2,1)}, bf16[1536,256]{1,0:T(8,128)(2,1)}, f32[512,256]{1,0:T(8,128)}, f32[512,256]{1,0:T(8,128)}, f32[512,512]{1,0...) custom-call(s32[12]{0:T(128)} %broadcast_add_fusion.2.first_seq, ...), custom_call_target="tpu_custom_call" | custom-call | tf_op jit(solution)/shard_map/pallas_call | solution.py:1844
  496.0 1.4 fusion.6
  (4 shorter events, 0.0 us)
Async XLA Ops:
  3.2 0.7 copy-start.2
  3.2 0.7 copy-start.3
  129.8 348.3 %copy-start.4 = (s32[12]{0:T(128)S(1)}, s32[12]{0:T(128)}, u32[]{:S(2)}) copy-start(s32[12]{0:T(128)} %param.17) | copy-start | bytes 148
  478.1 3.0 copy-start
  478.8 2.3 copy-start.1

commit v10 on v9

--- a/solution.py
+++ b/solution.py
@@ -1511,10 +1511,11 @@
     in_order(count, drain)
 
 
-def finish_kernel(first_seq, last_seq, starts, bases, begins, home, homes, *refs):
+def finish_kernel(first_seq, last_seq, starts, bases, begins, home, gains, homes, *refs):
     parts, refs = refs[:8], refs[8:]
     mixed_out, grad_out, *refs = refs
     outs, refs = refs[:8], refs[8:]
+    gain_one, gain_two, *refs = refs
     homes_held, *refs = refs
     held, sums, refs = refs[:8], refs[8:16], refs[16:]
     picked, load_sems, store_sems = refs
@@ -1523,6 +1524,8 @@
         list(zip(sums, outs)) + [(picked.at[0], mixed_out), (picked.at[1], grad_out)], store_sems
     )
     loads.start(*range(9))
+    gain_one[...] = gains[0:1, :]
+    gain_two[...] = gains[1:2, :]
     for number in range(8):
         loads.wait(number)
         ways, rows, columns = held[number].shape
@@ -1841,14 +1844,15 @@
     finals = [struct(w.shape, f32) for w in owners]
     picks = struct((2, rows_dev, slice_width))
     one_place = {"smem": pl.BlockSpec(memory_space=pltpu.SMEM), "any": pl.BlockSpec(memory_space=pl.ANY)}
-    mixed_rows, grad_rows, *grads = pl.pallas_call(
+    one_place["vmem"] = pl.BlockSpec(memory_space=pltpu.VMEM)
+    mixed_rows, grad_rows, *grads, gain_one, gain_two = pl.pallas_call(
         finish_kernel,
-        out_shape=[struct((rows_dev, slice_width))] * 2 + finals,
-        in_specs=[one_place["smem"]] * 6 + [one_place["any"]] * 9,
-        out_specs=[one_place["any"]] * 10,
+        out_shape=[struct((rows_dev, slice_width))] * 2 + finals + [struct((1, gain_attn.shape[0]), f32)] * 2,
+        in_specs=[one_place["smem"]] * 6 + [one_place["vmem"]] + [one_place["any"]] * 9,
+        out_specs=[one_place["any"]] * 10 + [one_place["vmem"]] * 2,
         scratch_shapes=held_like([homes] + order + finals + [picks]) + [DMA((9,)), DMA((10,))],
         compiler_params=pltpu.CompilerParams(vmem_limit_bytes=60 * 2**20),
-    )(first_seq, last_seq, all_starts, owner_base, home_begins, blocks_at[:1], homes, *order)
+    )(first_seq, last_seq, all_starts, owner_base, home_begins, blocks_at[:1], gains, homes, *order)
     return (
         mixed_rows,
         grad_rows,
@@ -1860,8 +1864,8 @@
         grads[5],
         grads[6],
         grads[7],
-        gains[0],
-        gains[1],
+        gain_one.reshape(-1),
+        gain_two.reshape(-1),
     )
 
 

time: 498 us -> 497 us (level)
  no operation moved by 1% of the time
where the time goes in v10:
time: 497 us; the launch traced here: 496 us
  Pallas kernels  489 us (98%)
  other arithmetic  5.41 us (1%)
    pallas_call x2, Pallas kernels, kernel_call(): pl.pallas_call(body, out_shape=[shape for _, shape in outs], in_specs=[pl...  474 us
    pallas_call x1, Pallas kernels, shards(): pl.pallas_call(finish_kernel, out_shape=[struct((rows_dev, slice_width))]...  15.1 us

profile of v10, /device:TPU:0, one launch (start us, length us, event | category | flops | bytes accessed | tf_op | source)
XLA Modules:
  0.0 496.5 jit_solution(7879628264289062082)
XLA Ops:
  0.7 0.7 dynamic_slice.3
  1.4 0.9 select_reduce_fusion.2
  2.2 0.9 select_reduce_fusion.4
  3.1 0.1 select_reduce_fusion.5.bounds
  3.2 0.0 copy-start.1
  3.2 0.0 copy-start.3
  3.3 0.1 add_clamp_fusion
  3.3 0.1 min.22
  3.4 0.5 and_select_fusion.begins
  4.0 0.0 copy-done.1
  4.0 0.0 copy-done.3
  4.0 125.8 %shard_map.229 = (bf16[1536,2048]{1,0:T(8,128)(2,1)}, bf16[1536,256]{1,0:T(8,128)(2,1)}, bf16[1536,256]{1,0:T(8,128)(2,1)}, bf16[1536,512]{1,0:T(8,128)(2,1)}, f...) custom-call(s32[3]{0:T(128)} %copy-done.1, ...), custom_call_target="tpu_custom_call" | custom-call | tf_op jit(solution)/shard_map/pallas_call | solution.py:1604
  129.8 0.0 copy-start.4
  129.8 348.2 %shard_map.230 = (bf16[1536,512]{1,0:T(8,128)(2,1)}, f32[1536,512]{1,0:T(8,128)}, f32[8,512]{1,0:T(8,128)}, bf16[6144,512]{1,0:T(8,128)(2,1)}, bf16[3,512,512]{2...) custom-call(s32[3]{0:T(128)} %copy-done.1, ...), custom_call_target="tpu_custom_call" | custom-call | tf_op jit(solution)/shard_map/pallas_call | solution.py:1604
  478.0 0.0 copy-start
  478.0 0.0 copy-done.4
  478.0 0.2 select_reduce_fusion.1
  478.3 0.1 reshape.123
  478.3 0.2 reduce_window_sum.13
  478.5 0.1 reduce_window_sum.14
  478.6 0.1 select_reduce_fusion.bases
  478.7 0.0 copy-start.2
  478.8 0.7 add_select_fusion.begins
  479.4 0.6 broadcast_add_fusion.1.last_seq
  480.0 0.5 broadcast_add_fusion.2.first_seq
  480.5 0.7 pad_add_fusion.starts
  481.2 0.0 copy-done
  481.2 0.0 copy-done.2
  481.2 15.1 %shard_map.231 = (bf16[1536,256]{1,0:T(8,128)(2,1)}, bf16[1536,256]{1,0:T(8,128)(2,1)}, f32[512,256]{1,0:T(8,128)}, f32[512,256]{1,0:T(8,128)}, f32[512,512]{1,0...) custom-call(s32[12]{0:T(128)} %broadcast_add_fusion.2.first_seq, ...), custom_call_target="tpu_custom_call" | custom-call | tf_op jit(solution)/shard_map/pallas_call | solution.py:1848
  (4 shorter events, 0.0 us)
Async XLA Ops:
  3.2 0.7 copy-start.1
  3.2 0.7 copy-start.3
  129.8 348.2 %copy-start.4 = (s32[12]{0:T(128)S(1)}, s32[12]{0:T(128)}, u32[]{:S(2)}) copy-start(s32[12]{0:T(128)} %param.17) | copy-start | bytes 148
  478.0 3.2 copy-start
  478.7 2.4 copy-start.2
